TPU v7x, 128 devices: a whole 4x4x4 slice. The times are simulated.
128 devices in a mesh: rows: 32 (over y_lo, x, z), cols: 4 (over y_hi, core).
Axes of the slice: x: 4, y: 4 (y_hi: 2, y_lo: 2; y = y_hi * 2 + y_lo), z: 4, core: 2. Of those that a mesh axis runs over, the one named last changes fastest.
Arguments:
- features: bfloat16 [256, 64, 2048], P('rows', 'cols'), may hold values from -6 to 12
- image_rows: int32 [256], P('rows'), may hold values from 0 to 3, never falling along the last dimension, each value on 1 to 96 neighbouring positions
- seg_labels: int32 [256, 64], P('rows', 'cols'), may hold values from 0 to 12
- edge_labels: int32 [256, 64], P('rows', 'cols'), may hold values from 0 to 1
- part_labels: int32 [256, 64], P('rows', 'cols'), may hold values from 0 to 2
- task_weights: int32 [3], replicated, may hold values from 1 to 8
- block_params: float32 [4472832], P(('rows', 'cols'))
- block_moment: float32 [4472832], P(('rows', 'cols')), may hold values from -0.03 to 0.03
- head_params: float32 [1392640], P(('rows', 'cols'))
- head_moment: float32 [1392640], P(('rows', 'cols')), may hold values from -0.03 to 0.03
- rate_params: float32 [2048, 6912], P('cols', 'rows'), may hold values from -0.046875 to 0.046875
- rate_moment: float32 [2048, 6912], P('cols', 'rows'), may hold values from -0.03 to 0.03
Outputs:
- loss_value: float32 [], replicated
- pooled: float32 [4, 2048], replicated
- feature_grad: float32 [256, 64, 2048], P('rows', 'cols')
- block_moment_next: float32 [4472832], P(('rows', 'cols'))
- head_moment_next: float32 [1392640], P(('rows', 'cols'))
- rate_moment_next: float32 [2048, 6912], P('cols', 'rows')
Inputs may be any that keep to these rules, and one draw needn't show every extreme that they name: `image_rows`: image numbers never fall along the rows; each of the 4 images covers 1 to 96 consecutive rows, and one covers exactly 96.
All inputs are finite; a program needn't handle non-finite values.
Results may differ from a plain program's by a relative error of at most 0.018.
Values may be sent and summed in bfloat16 or wider, within the bound.
A program may use at most 320 MiB of HBM per device.

v0:
```python
import math

import jax
import jax.numpy as jnp
from jax import lax
from jax.sharding import PartitionSpec as P

CIN = 2048
MID = 512
ASPP = 256
SEG = 13
PART = 3
HEADS = 17


EPSILON = 1e-05
MOMENTUM_KEEP = 0.5
rate_list = (6, 12, 18)
block_dilation = 4
widest_margin = 18


def from_behind(value, axis, steps):
    count = lax.axis_size(axis)
    first, last = (max(0, -steps), min(count, count - steps))
    return lax.ppermute(value, axis, [(source, source + steps) for source in range(first, last)])


def silu_slope(values):
    sigmoid_part = jax.nn.sigmoid(values)
    return sigmoid_part * (1.0 + values * (1.0 - sigmoid_part))


def block_layout():
    return [(CIN, MID), (9, MID, MID), (MID, CIN), (2, 2, MID), (2, CIN)]


def head_layout():
    return [
        (CIN, ASPP),
        (CIN, ASPP),
        (ASPP,),
        (5 * ASPP, ASPP),
        (5, 2, ASPP),
        (ASPP, HEADS),
        (HEADS,),
    ]


def unpack(vector, layout):
    pieces = []
    cursor = 0
    for extent in layout:
        number = math.prod(extent)
        pieces.append(vector[cursor : cursor + number].reshape(extent))
        cursor = cursor + number
    return pieces


def pack_flat(pieces, length):
    joined = jnp.concatenate([item.reshape(-1) for item in pieces])
    return jnp.pad(joined, (0, length - joined.shape[0]))


def global_sums(values):
    return lax.psum(values, ("rows", "cols"))


def neighbour_rows(stripe, offset):
    return from_behind(stripe, "rows", offset)


def all_columns(stripe):
    return lax.all_gather(stripe, "cols", axis=1, tiled=True)


def rows_around(stripe, margin):
    height = stripe.shape[0]
    hop_count = -(-margin // height)
    upper_parts = []
    lower_parts = []
    for distance in range(hop_count, 0, -1):
        needed = min(height, margin - (distance - 1) * height)
        upper_parts.append(neighbour_rows(stripe[height - needed :], distance))
    for distance in range(1, hop_count + 1):
        needed = min(height, margin - (distance - 1) * height)
        lower_parts.append(neighbour_rows(stripe[:needed], -distance))
    return jnp.concatenate(upper_parts + [stripe] + lower_parts, axis=0)


def full_window(stripe, margin):
    widened = rows_around(all_columns(stripe), margin)
    return jnp.pad(widened, ((0, 0), (margin, margin), (0, 0)))


def extend(stripe, margin):
    across = stripe.shape[1]
    padded = full_window(stripe, margin)
    return lax.dynamic_slice_in_dim(padded, lax.axis_index("cols") * across, across + 2 * margin, 1)


def row_masks(all_ids, first_row, height, margin, dilation):
    padded = jnp.pad(all_ids, (margin, margin), constant_values=-1)
    window = lax.dynamic_slice_in_dim(padded, first_row, height + 2 * margin)
    own_ids = window[margin : margin + height]
    mask_list = []
    for row_tap in range(3):
        offset = margin + (row_tap - 1) * dilation
        mask_list.append((window[offset : offset + height] == own_ids).astype(jnp.bfloat16))
    return mask_list


def conv_forward(window, kernel, mask_list, margin, dilation, height, across):
    running = None
    for row_tap in range(3):
        for col_tap in range(3):
            top_row = margin + (row_tap - 1) * dilation
            left_col = margin + (col_tap - 1) * dilation
            masked = (
                window[top_row : top_row + height, left_col : left_col + across]
                * mask_list[row_tap][:, None, None]
            )
            partial_out = jnp.dot(
                masked.reshape(height * across, -1),
                kernel[3 * row_tap + col_tap],
                preferred_element_type=jnp.float32,
            )
            running = partial_out if running is None else running + partial_out
    return running


def conv_weight_grad(window, grad_out, mask_list, margin, dilation, height, across):
    tap_grads = []
    for row_tap in range(3):
        for col_tap in range(3):
            top_row = margin + (row_tap - 1) * dilation
            left_col = margin + (col_tap - 1) * dilation
            masked = (
                window[top_row : top_row + height, left_col : left_col + across]
                * mask_list[row_tap][:, None, None]
            )
            tap_grads.append(
                jnp.einsum(
                    "pc,po->co",
                    masked.reshape(height * across, -1),
                    grad_out,
                    preferred_element_type=jnp.float32,
                )
            )
    return jnp.stack(tap_grads)


def conv_input_grad(grad_window, kernel, mask_list, margin, dilation, height, across):
    running = None
    for row_tap in range(3):
        for col_tap in range(3):
            top_row = margin - (row_tap - 1) * dilation
            left_col = margin - (col_tap - 1) * dilation
            region = (
                grad_window[top_row : top_row + height, left_col : left_col + across]
                * mask_list[2 - row_tap][:, None, None]
            )
            partial_out = jnp.einsum(
                "po,co->pc",
                region.reshape(height * across, -1),
                kernel[3 * row_tap + col_tap],
                preferred_element_type=jnp.float32,
            )
            running = partial_out if running is None else running + partial_out
    return running


def moments(values):
    return (jnp.sum(values, axis=0), jnp.sum(values * values, axis=0))


def normalize(values, totals, number, gain_row, shift_row):
    average = totals[0] / number
    variance = totals[1] / number - average * average
    scale_row = lax.rsqrt(variance + EPSILON)
    centered = (values - average) * scale_row
    return (centered, centered * gain_row + shift_row, scale_row)


def norm_back(grad_norm, centered, scale_row, gain_row, totals, number):
    return gain_row * scale_row * (grad_norm - totals[0] / number - centered * totals[1] / number)


def per_device(
    features,
    image_rows,
    seg_labels,
    edge_labels,
    part_labels,
    task_weights,
    block_params,
    block_moment,
    head_params,
    head_moment,
    rate_params,
    rate_moment,
):
    height, across, channels = features.shape
    pixels = height * across
    columns = across * lax.axis_size("cols")
    rows_all = height * lax.axis_size("rows")
    total_pixels = rows_all * columns
    images = max(rows_all // 64, 2)
    highest = lax.Precision.HIGHEST
    block_all, head_all = (
        lax.all_gather(block_params.astype(jnp.bfloat16), ("rows", "cols"), axis=0, tiled=True),
        lax.all_gather(head_params.astype(jnp.bfloat16), ("rows", "cols"), axis=0, tiled=True),
    )
    rate_slab = lax.all_gather(rate_params.astype(jnp.bfloat16), "rows", axis=1, tiled=True)
    rate_block = lax.all_gather(rate_slab, "cols", axis=0, tiled=True)
    slab = rate_block.shape[0]
    w_rates = rate_block.reshape(slab, 3, 9, ASPP).transpose(1, 2, 0, 3)
    all_ids = lax.all_gather(image_rows, "rows", axis=0, tiled=True)
    first_row = lax.axis_index("rows") * height
    w_reduce, w_spatial, w_expand, mid_norm, out_norm = unpack(block_all, block_layout())
    w_point, w_pool, pool_bias, w_project, head_norm, w_heads, heads_bias = unpack(
        head_all, head_layout()
    )
    mid_norm = mid_norm.astype(jnp.float32)
    out_norm = out_norm.astype(jnp.float32)
    head_norm = head_norm.astype(jnp.float32)
    pool_bias = pool_bias.astype(jnp.float32)
    heads_bias = heads_bias.astype(jnp.float32)
    inputs = features.reshape(pixels, channels)
    block_masks = row_masks(all_ids, first_row, height, block_dilation, block_dilation)
    rate_masks = [
        row_masks(all_ids, first_row, height, widest_margin, dilation) for dilation in rate_list
    ]
    image_range = jnp.arange(images, dtype=jnp.int32)
    member = (image_rows[None, :] == image_range[:, None]).astype(jnp.float32)
    image_area = (
        jnp.sum((all_ids[None, :] == image_range[:, None]).astype(jnp.float32), axis=1) * columns
    )
    first_pre = jnp.dot(inputs, w_reduce, preferred_element_type=jnp.float32)
    first_cent, first_norm, first_scale = normalize(
        first_pre, global_sums(moments(first_pre)), total_pixels, mid_norm[0, 0], mid_norm[0, 1]
    )
    first_act = jax.nn.silu(first_norm).astype(jnp.bfloat16)
    block_window = extend(first_act.reshape(height, across, MID), block_dilation)
    second_pre = conv_forward(
        block_window, w_spatial, block_masks, block_dilation, block_dilation, height, across
    )
    second_cent, second_norm, second_scale = normalize(
        second_pre, global_sums(moments(second_pre)), total_pixels, mid_norm[1, 0], mid_norm[1, 1]
    )
    second_act = jax.nn.silu(second_norm).astype(jnp.bfloat16)
    third_pre = jnp.dot(second_act, w_expand, preferred_element_type=jnp.float32)
    third_cent, third_norm, third_scale = normalize(
        third_pre, global_sums(moments(third_pre)), total_pixels, out_norm[0], out_norm[1]
    )
    residual = third_norm + inputs.astype(jnp.float32)
    block_out = jax.nn.silu(residual).astype(jnp.bfloat16)
    grid = block_out.reshape(height, across, channels)
    conv_window = extend(grid, widest_margin)
    rate_parts = [
        conv_forward(
            conv_window,
            w_rates[branch],
            rate_masks[branch],
            widest_margin,
            rate_list[branch],
            height,
            across,
        )
        for branch in range(3)
    ]
    branch_list = [jnp.dot(block_out, w_point, preferred_element_type=jnp.float32)] + rate_parts
    branch_pre = jnp.stack(branch_list)
    pool_local = jnp.dot(member, jnp.sum(grid, axis=1, dtype=jnp.float32), precision=highest)
    branch_sums, branch_squares, pool_total = global_sums(
        (jnp.sum(branch_pre, axis=1), jnp.sum(branch_pre * branch_pre, axis=1), pool_local)
    )
    branch_gain = head_norm[:4, 0][:, None, :]
    branch_cent, branch_norm, branch_scale = normalize(
        branch_pre,
        (branch_sums[:, None, :], branch_squares[:, None, :]),
        total_pixels,
        branch_gain,
        head_norm[:4, 1][:, None, :],
    )
    branch_act = jax.nn.silu(branch_norm)
    pooled = pool_total / image_area[:, None]
    pooled_low = pooled.astype(jnp.bfloat16)
    pool_pre = jnp.dot(pooled_low, w_pool, preferred_element_type=jnp.float32) + pool_bias
    pool_act = jax.nn.silu(pool_pre)
    pool_rows = jnp.dot(member.T, pool_act, precision=highest)
    pool_map = jnp.broadcast_to(pool_rows[:, None, :], (height, across, ASPP)).reshape(pixels, ASPP)
    joined = jnp.concatenate(
        [branch_act[0], branch_act[1], branch_act[2], branch_act[3], pool_map], axis=1
    ).astype(jnp.bfloat16)
    projected = jnp.dot(joined, w_project, preferred_element_type=jnp.float32)
    proj_cent, proj_norm, proj_scale = normalize(
        projected, global_sums(moments(projected)), total_pixels, head_norm[4, 0], head_norm[4, 1]
    )
    feature_map = jax.nn.silu(proj_norm).astype(jnp.bfloat16)
    logits = jnp.dot(feature_map, w_heads, preferred_element_type=jnp.float32) + heads_bias
    weight_vals = task_weights.astype(jnp.float32)
    shares = weight_vals / jnp.sum(weight_vals)
    seg_scores = logits[:, :SEG]
    seg_hot = (
        seg_labels.reshape(pixels)[:, None] == jnp.arange(SEG, dtype=jnp.int32)[None, :]
    ).astype(jnp.float32)
    seg_lse = jax.nn.logsumexp(seg_scores, axis=1)
    seg_terms = seg_lse - jnp.sum(seg_scores * seg_hot, axis=1)
    seg_grad = jnp.exp(seg_scores - seg_lse[:, None]) - seg_hot
    edge_logit = logits[:, SEG]
    edge_target = edge_labels.reshape(pixels).astype(jnp.float32)
    edge_terms = jax.nn.softplus(edge_logit) - edge_target * edge_logit
    edge_grad = jax.nn.sigmoid(edge_logit) - edge_target
    part_scores = logits[:, SEG + 1 :]
    part_hot = (
        part_labels.reshape(pixels)[:, None] == jnp.arange(PART, dtype=jnp.int32)[None, :]
    ).astype(jnp.float32)
    part_lse = jax.nn.logsumexp(part_scores, axis=1)
    part_terms = part_lse - jnp.sum(part_scores * part_hot, axis=1)
    part_grad = jnp.exp(part_scores - part_lse[:, None]) - part_hot
    loss_local = (
        shares[0] * jnp.sum(seg_terms)
        + shares[1] * jnp.sum(edge_terms)
        + shares[2] * jnp.sum(part_terms)
    ) / total_pixels
    logit_grad = (
        jnp.concatenate(
            [seg_grad * shares[0], edge_grad[:, None] * shares[1], part_grad * shares[2]], axis=1
        )
        / total_pixels
    ).astype(jnp.bfloat16)
    grad_heads = jnp.einsum(
        "pc,pk->ck", feature_map, logit_grad, preferred_element_type=jnp.float32
    )
    grad_heads_bias = jnp.sum(logit_grad, axis=0, dtype=jnp.float32)
    feature_grad_map = jnp.einsum(
        "pk,ck->pc", logit_grad, w_heads, preferred_element_type=jnp.float32
    )
    proj_grad_norm = feature_grad_map * silu_slope(proj_norm)
    proj_shift_grad = jnp.sum(proj_grad_norm, axis=0)
    proj_gain_grad = jnp.sum(proj_grad_norm * proj_cent, axis=0)
    loss_total, proj_shift_all, proj_gain_all = global_sums(
        (loss_local, proj_shift_grad, proj_gain_grad)
    )
    projected_grad = norm_back(
        proj_grad_norm,
        proj_cent,
        proj_scale,
        head_norm[4, 0],
        (proj_shift_all, proj_gain_all),
        total_pixels,
    ).astype(jnp.bfloat16)
    grad_project = jnp.einsum(
        "pc,po->co", joined, projected_grad, preferred_element_type=jnp.float32
    )
    joined_grad = jnp.einsum(
        "po,co->pc", projected_grad, w_project, preferred_element_type=jnp.float32
    )
    branch_in_grad = joined_grad[:, : 4 * ASPP].reshape(pixels, 4, ASPP).transpose(1, 0, 2)
    pool_map_grad = joined_grad[:, 4 * ASPP :]
    pool_act_local = jnp.dot(
        member, jnp.sum(pool_map_grad.reshape(height, across, ASPP), axis=1), precision=highest
    )
    branch_grad_norm = branch_in_grad * silu_slope(branch_norm)
    branch_shift_grad = jnp.sum(branch_grad_norm, axis=1)
    branch_gain_grad = jnp.sum(branch_grad_norm * branch_cent, axis=1)
    branch_shift_all, branch_gain_all, pool_act_grad = global_sums(
        (branch_shift_grad, branch_gain_grad, pool_act_local)
    )
    branch_grad = norm_back(
        branch_grad_norm,
        branch_cent,
        branch_scale,
        branch_gain,
        (branch_shift_all[:, None, :], branch_gain_all[:, None, :]),
        total_pixels,
    ).astype(jnp.bfloat16)
    pool_slope = silu_slope(pool_pre)
    pool_pre_local = pool_act_local * pool_slope
    grad_pool = jnp.dot(pooled_low.astype(jnp.float32).T, pool_pre_local, precision=highest)
    grad_pool_bias = jnp.sum(pool_pre_local, axis=0)
    pooled_grad = (
        jnp.dot(pool_act_grad * pool_slope, w_pool.astype(jnp.float32).T, precision=highest)
        / image_area[:, None]
    )
    pool_back_rows = jnp.dot(member.T, pooled_grad, precision=highest)
    grad_point = jnp.einsum(
        "pc,po->co", block_out, branch_grad[0], preferred_element_type=jnp.float32
    )
    out_grad = jnp.einsum("po,co->pc", branch_grad[0], w_point, preferred_element_type=jnp.float32)
    rate_stack = jnp.concatenate([branch_grad[1], branch_grad[2], branch_grad[3]], axis=1).reshape(
        height, across, 3 * ASPP
    )
    rate_grads = []
    grad_window = extend(rate_stack, widest_margin)
    for branch in range(3):
        rate_grads.append(
            conv_weight_grad(
                conv_window,
                branch_grad[branch + 1],
                rate_masks[branch],
                widest_margin,
                rate_list[branch],
                height,
                across,
            )
        )
        out_grad = out_grad + conv_input_grad(
            grad_window[:, :, branch * ASPP : (branch + 1) * ASPP],
            w_rates[branch],
            rate_masks[branch],
            widest_margin,
            rate_list[branch],
            height,
            across,
        )
    out_grad = out_grad + jnp.broadcast_to(
        pool_back_rows[:, None, :], (height, across, channels)
    ).reshape(pixels, channels)
    rate_flat = jnp.stack(rate_grads).transpose(2, 0, 1, 3).reshape(slab, 27 * ASPP)
    rate_flat = lax.psum_scatter(
        rate_flat.astype(jnp.bfloat16), "cols", scatter_dimension=0, tiled=True
    ).astype(jnp.float32)
    rate_share = lax.psum_scatter(
        rate_flat.astype(jnp.bfloat16), "rows", scatter_dimension=1, tiled=True
    ).astype(jnp.float32)
    norm_grads = jnp.concatenate(
        [
            jnp.stack([branch_gain_grad, branch_shift_grad], axis=1),
            jnp.stack([proj_gain_grad, proj_shift_grad])[None],
        ],
        axis=0,
    )
    head_grad = pack_flat(
        [
            grad_point,
            grad_pool,
            grad_pool_bias,
            grad_project,
            norm_grads,
            grad_heads,
            grad_heads_bias,
        ],
        head_all.shape[0],
    )
    residual_grad = out_grad * silu_slope(residual)
    third_shift_grad = jnp.sum(residual_grad, axis=0)
    third_gain_grad = jnp.sum(residual_grad * third_cent, axis=0)
    third_grad = norm_back(
        residual_grad,
        third_cent,
        third_scale,
        out_norm[0],
        global_sums((third_shift_grad, third_gain_grad)),
        total_pixels,
    ).astype(jnp.bfloat16)
    grad_expand = jnp.einsum(
        "pc,po->co", second_act, third_grad, preferred_element_type=jnp.float32
    )
    second_act_grad = jnp.einsum(
        "po,co->pc", third_grad, w_expand, preferred_element_type=jnp.float32
    )
    second_grad_norm = second_act_grad * silu_slope(second_norm)
    second_shift_grad = jnp.sum(second_grad_norm, axis=0)
    second_gain_grad = jnp.sum(second_grad_norm * second_cent, axis=0)
    second_grad = norm_back(
        second_grad_norm,
        second_cent,
        second_scale,
        mid_norm[1, 0],
        global_sums((second_shift_grad, second_gain_grad)),
        total_pixels,
    ).astype(jnp.bfloat16)
    grad_spatial = conv_weight_grad(
        block_window, second_grad, block_masks, block_dilation, block_dilation, height, across
    )
    block_grad_window = extend(second_grad.reshape(height, across, MID), block_dilation)
    first_act_grad = conv_input_grad(
        block_grad_window, w_spatial, block_masks, block_dilation, block_dilation, height, across
    )
    first_grad_norm = first_act_grad * silu_slope(first_norm)
    first_shift_grad = jnp.sum(first_grad_norm, axis=0)
    first_gain_grad = jnp.sum(first_grad_norm * first_cent, axis=0)
    first_grad = norm_back(
        first_grad_norm,
        first_cent,
        first_scale,
        mid_norm[0, 0],
        global_sums((first_shift_grad, first_gain_grad)),
        total_pixels,
    ).astype(jnp.bfloat16)
    grad_reduce = jnp.einsum("pc,po->co", inputs, first_grad, preferred_element_type=jnp.float32)
    input_grad = residual_grad + jnp.einsum(
        "po,co->pc", first_grad, w_reduce, preferred_element_type=jnp.float32
    )
    mid_grads = jnp.stack(
        [
            jnp.stack([first_gain_grad, first_shift_grad]),
            jnp.stack([second_gain_grad, second_shift_grad]),
        ]
    )
    out_grads = jnp.stack([third_gain_grad, third_shift_grad])
    block_grad = pack_flat(
        [grad_reduce, grad_spatial, grad_expand, mid_grads, out_grads], block_all.shape[0]
    )
    block_share, head_share = (
        lax.psum_scatter(block_grad, ("rows", "cols"), scatter_dimension=0, tiled=True),
        lax.psum_scatter(head_grad, ("rows", "cols"), scatter_dimension=0, tiled=True),
    )
    block_moment_next = MOMENTUM_KEEP * block_moment + block_share
    head_moment_next = MOMENTUM_KEEP * head_moment + head_share
    rate_moment_next = MOMENTUM_KEEP * rate_moment + rate_share
    return (
        loss_total,
        pooled,
        input_grad.reshape(height, across, channels),
        block_moment_next,
        head_moment_next,
        rate_moment_next,
    )


def solution(mesh):
    return jax.shard_map(
        per_device,
        mesh=mesh,
        in_specs=(
            P("rows", "cols", None),
            P("rows"),
            P("rows", "cols"),
            P("rows", "cols"),
            P("rows", "cols"),
            P(),
            P(("rows", "cols")),
            P(("rows", "cols")),
            P(("rows", "cols")),
            P(("rows", "cols")),
            P("cols", "rows"),
            P("cols", "rows"),
        ),
        out_specs=(
            P(),
            P(),
            P("rows", "cols", None),
            P(("rows", "cols")),
            P(("rows", "cols")),
            P("cols", "rows"),
        ),
        check_vma=False,
    )
```

profile of v0, /device:TPU:0, one launch (start us, length us, event | category | flops | bytes accessed | tf_op | source)
XLA Modules:
  0.0 2300.8 jit_solution(11917114025994361728)
XLA Ops:
  15.0 20.4 all-reduce.8
  35.6 194.1 %all-gather.14.cloned.1.call-done = bf16[128,1,34944]{2,1,0:T(2,128)(2,1)} async-done(((bf16[1,1,34944]{2,1,0:T(2,128)(2,1)}), bf16[128,1,34944]{2,1,0:T(2,128)(2,1)}) %all-gather.14.cloned.1.call-update) | async-done | bytes 8945680 | tf_op jit(solution)/shard_map/all_gather | solution.py:211
  229.7 193.0 %reduce = bf16[128,34944]{1,0:T(8,128)(2,1)} reduce(bf16[128,1,34944]{2,1,0:T(2,128)(2,1)} %all-gather.14.cloned.1.call-done, bf16[]{:T(256)} %constant.139), dimensions={1}, to_apply=%all-gather.reduce_sub_computation | reduce | bytes 17891330 | tf_op jit(solution)/shard_map/all_gather | solution.py:211
  422.8 18.8 reshape.740
  441.5 4.6 fusion.258
  446.8 3.1 slice.847
  450.5 62.5 %all-reduce.20 = (f32[512]{0:T(512)S(1)}, f32[512]{0:T(512)S(1)}) all-reduce(f32[512]{0:T(512)S(1)} %get-tuple-element.21, f32[512]{0:T(512)S(1)} %get-tuple-element.20), channel_id=1, replica_groups=mesh['rows'=32,'cols'=4] {'rows','cols'}, use_global_device_ids=true, to_apply=%region_4.5 | all-reduce | flops 1024 | bytes 8192 | tf_op jit(solution)/shard_map/psum | solution.py:66
  513.7 8.8 all_gather.28
  523.4 3.1 collective-permute-start
  528.1 4.5 fusion.257
  532.7 4.3 slice.886
  561.3 68.9 %all-reduce.19 = (f32[512]{0:T(512)S(1)}, f32[512]{0:T(512)S(1)}) all-reduce(f32[512]{0:T(512)S(1)} %get-tuple-element.19, f32[512]{0:T(512)S(1)} %get-tuple-element.18), channel_id=1, replica_groups=mesh['rows'=32,'cols'=4] {'rows','cols'}, use_global_device_ids=true, to_apply=%region_8.9 | all-reduce | flops 1024 | bytes 8192 | tf_op jit(solution)/shard_map/psum | solution.py:66
  633.9 62.3 %all-reduce.18 = (f32[2048]{0:T(1024)S(1)}, f32[2048]{0:T(1024)S(1)}) all-reduce(f32[2048]{0:T(1024)S(1)} %get-tuple-element.9, f32[2048]{0:T(1024)S(1)} %get-tuple-element.8), channel_id=1, replica_groups=mesh['rows'=32,'cols'=4] {'rows','cols'}, use_global_device_ids=true, to_apply=%region_12.13 | all-reduce | flops 4096 | bytes 32768 | tf_op jit(solution)/shard_map/psum | solution.py:66
  705.9 16.7 reduce.1
  722.6 5.8 reshape.742
  728.4 4.7 collective-permute-start.3
  733.1 3.1 fusion.259
  736.3 5.4 collective-permute-start.4
  749.2 8.6 collective-permute-start.2
  764.7 114.7 %collective-permute-done.2 = bf16[2,64,2048]{2,1,0:T(8,128)(2,1)} collective-permute-done((bf16[2,64,2048]{2,1,0:T(8,128)(2,1)}, bf16[2,64,2048]{2,1,0:T(8,128)(2,1)}, u32[]{:S(2)}, u32[]{:S(2)}) %collective-permute-start.2) | collective-permute-done | bytes 524320 | tf_op jit(solution)/shard_map/ppermute | solution.py:26
  885.9 28.3 %collective-permute-done.5 = bf16[8,64,2048]{2,1,0:T(8,128)(2,1)} collective-permute-done((bf16[8,64,2048]{2,1,0:T(8,128)(2,1)}, bf16[8,64,2048]{2,1,0:T(8,128)(2,1)}, u32[]{:S(2)}, u32[]{:S(2)}) %collective-permute-start.5) | collective-permute-done | bytes 2097184 | tf_op jit(solution)/shard_map/ppermute | solution.py:26
  917.9 3.4 fusion.120
  921.3 3.4 fusion.123
  924.7 3.7 fusion.126
  977.9 136.4 %all-reduce.17 = (f32[4,256]{1,0:T(4,128)S(1)}, f32[4,256]{1,0:T(4,128)S(1)}, f32[4,2048]{1,0:T(4,128)}) all-reduce(f32[4,256]{1,0:T(4,128)S(1)} %get-tuple-element.13, f32[4,256]{1,0:T(4,128)S(1)} %get-tuple-element.12, f32[4,2048]{1,0:T(4,128)S(1)} %fusion.199), channel_id=1, replica_groups=mesh['rows'=32,'cols'=4] {'rows','cols'}, use_global_device_ids=true, to_apply=%region_16.17 | all-reduce | flops 10240 | bytes 81920 | tf_op jit(solution)/shard_map/psum | solution.py:66
  1121.0 64.4 %all-reduce.16 = (f32[256]{0:T(256)S(1)}, f32[256]{0:T(256)S(1)}) all-reduce(f32[256]{0:T(256)S(1)} %get-tuple-element.25, f32[256]{0:T(256)S(1)} %get-tuple-element.24), channel_id=1, replica_groups=mesh['rows'=32,'cols'=4] {'rows','cols'}, use_global_device_ids=true, to_apply=%region_23.24 | all-reduce | flops 512 | bytes 4096 | tf_op jit(solution)/shard_map/psum | solution.py:66
  1195.0 62.7 %all-reduce.15 = (f32[256]{0:T(256)S(1)}, f32[256]{0:T(256)S(1)}) all-reduce(f32[256]{0:T(256)S(1)} %get-tuple-element.23, f32[256]{0:T(256)S(1)} %get-tuple-element.22), channel_id=1, replica_groups=mesh['rows'=32,'cols'=4] {'rows','cols'}, use_global_device_ids=true, to_apply=%region_37.38 | all-reduce | flops 512 | bytes 4096 | tf_op jit(solution)/shard_map/psum | solution.py:66
  1263.6 64.6 %all-reduce.14 = (f32[4,256]{1,0:T(4,128)}, f32[4,256]{1,0:T(4,128)S(1)}, f32[4,256]{1,0:T(4,128)S(1)}) all-reduce(f32[4,256]{1,0:T(4,128)} %get-tuple-element.224, f32[4,256]{1,0:T(4,128)} %get-tuple-element.11, f32[4,256]{1,0:T(4,128)} %get-tuple-element.10), channel_id=1, replica_groups=mesh['rows'=32,'cols'=4] {'rows','cols'}, use_global_device_ids=true, to_apply=%region_43.44 | all-reduce | flops 3072 | bytes 24576 | tf_op jit(solution)/shard_map/psum | solution.py:66
  1331.7 10.0 all_gather.34
  1343.5 4.3 collective-permute-start.9
  1347.8 3.3 collective-permute-start.10
  1362.0 8.0 collective-permute-start.8
  1406.1 3.7 copy-done.4
  1409.8 19.4 pad_maximum_fusion
  1433.7 12.8 dynamic-update-slice.31
  1456.1 6.3 pad.40
  1491.7 195.5 %all-reduce.13 = (f32[2048]{0:T(1024)S(1)}, f32[2048]{0:T(1024)S(1)}) all-reduce(f32[2048]{0:T(1024)} %get-tuple-element.7, f32[2048]{0:T(1024)} %get-tuple-element.6), channel_id=1, replica_groups=mesh['rows'=32,'cols'=4] {'rows','cols'}, use_global_device_ids=true, to_apply=%region_47.48 | all-reduce | flops 4096 | bytes 32768 | tf_op jit(solution)/shard_map/psum | solution.py:66
  1691.5 62.4 %all-reduce.12 = (f32[512]{0:T(512)S(1)}, f32[512]{0:T(512)S(1)}) all-reduce(f32[512]{0:T(512)S(1)} %get-tuple-element.17, f32[512]{0:T(512)S(1)} %get-tuple-element.16), channel_id=1, replica_groups=mesh['rows'=32,'cols'=4] {'rows','cols'}, use_global_device_ids=true, to_apply=%region_51.52 | all-reduce | flops 1024 | bytes 8192 | tf_op jit(solution)/shard_map/psum | solution.py:66
  1755.9 8.3 all_gather.35
  1771.2 3.5 copy-done.3
  1777.5 9.8 copy.38
  1787.4 5.2 copy.39
  1796.4 70.2 %all-reduce.11 = (f32[]{:T(128)}, f32[512]{0:T(512)S(1)}, f32[512]{0:T(512)S(1)}) all-reduce(f32[]{:T(128)S(6)} %div.151, f32[512]{0:T(512)S(1)} %get-tuple-element.15, f32[512]{0:T(512)S(1)} %get-tuple-element.14), channel_id=1, replica_groups=mesh['rows'=32,'cols'=4] {'rows','cols'}, use_global_device_ids=true, to_apply=%region_33.34 | all-reduce | flops 1025 | bytes 8200 | tf_op jit(solution)/shard_map/psum | solution.py:66
  1869.4 5.4 copy.30
  1874.8 3.4 copy.37
  1882.9 6.4 pad.39
  1893.0 220.9 %all-reduce.24.cloned.1.call-done = (f32[4472832]{0:T(1024)}, f32[1392640]{0:T(1024)}) async-done(((f32[4472832]{0:T(1024)}, f32[1392640]{0:T(1024)}), (f32[4472832]{0:T(1024)}, f32[1392640]{0:T(1024)})) %all-reduce.24.cloned.1.call-update) | async-done | bytes 23461904
  2117.1 174.7 %reduce-scatter.5.cloned.1.call-done = bf16[512,216]{0,1:T(8,128)(2,1)} async-done(((bf16[512,6912]{0,1:T(8,128)(2,1)}), bf16[512,216]{0,1:T(8,128)(2,1)}) %reduce-scatter.5.cloned.1.call-update) | async-done | bytes 221200 | tf_op jit(solution)/shard_map/reduce_scatter | solution.py:425
  (677 shorter events, 270.1 us)
Async XLA Ops:
  7.2 222.6 %all-gather.14.cloned.1.call-start = ((), (), s32[]{:S(2)}) async-start(), calls=%async_computation.7 | async-start | bytes 18031104 | tf_op jit(solution)/shard_map/all_gather | solution.py:211
  8.9 690.6 %all-gather.10.cloned.1.call-start = ((), (), s32[]{:S(2)}) async-start(), calls=%async_computation.3 | async-start | bytes 7299072 | tf_op jit(solution)/shard_map/all_gather | solution.py:214
  10.7 695.2 %all-gather.16.cloned.1.call-start = ((), (), s32[]{:S(2)}) async-start(), calls=%async_computation.8 | async-start | bytes 5614080 | tf_op jit(solution)/shard_map/all_gather | solution.py:212
  12.2 716.2 %all-gather.8.cloned.1.call-start = ((), (), s32[]{:S(2)}) async-start(), calls=%async_computation.2 | async-start | bytes 2621440 | tf_op jit(solution)/shard_map/all_gather | solution.py:74
  35.6 519.9 %copy-start.143 = (bf16[8]{0:T(256)(128)(2,1)}, bf16[8]{0:T(256)(128)(2,1)S(1)}, u32[]{:S(2)}) copy-start(bf16[8]{0:T(256)(128)(2,1)S(1)} %get-tuple-element.213) | copy-start | bytes 52
  35.6 519.9 %copy-start.145 = (bf16[8]{0:T(256)(128)(2,1)}, bf16[8]{0:T(256)(128)(2,1)S(1)}, u32[]{:S(2)}) copy-start(bf16[8]{0:T(256)(128)(2,1)S(1)} %get-tuple-element.214) | copy-start | bytes 52
  450.0 180.9 %copy-start.114 = (f32[1,1,512]{2,1,0:T(1,128)}, f32[1,1,512]{2,1,0:T(1,128)S(1)}, u32[]{:S(2)}) copy-start(f32[1,1,512]{2,1,0:T(1,128)S(1)} %get-tuple-element.189) | copy-start | bytes 6148
  450.0 180.9 %copy-start.124 = (f32[1,1,512]{2,1,0:T(1,128)}, f32[1,1,512]{2,1,0:T(1,128)S(1)}, u32[]{:S(2)}) copy-start(f32[1,1,512]{2,1,0:T(1,128)S(1)} %get-tuple-element.190) | copy-start | bytes 6148
  523.4 30.8 %collective-permute-start = (bf16[4,64,512]{2,1,0:T(8,128)(2,1)}, bf16[4,64,512]{2,1,0:T(8,128)(2,1)S(1)}, u32[]{:S(2)}, u32[]{:S(2)}) collective-permute-start(bf16[4,64,512]{2,1,0:T(8,128)(2,1)} %get-tuple-element.151), channel_id=1, source_target_pairs={{0,4},{4,8},{8,12},{12,16},{16,20},{20,24},{24,28},{28,32},{32,36}... | collective-permute-start | bytes 786440 | tf_op jit(solution)/shard_map/ppermute | solution.py:26
  526.5 27.7 %collective-permute-start.1 = (bf16[4,64,512]{2,1,0:T(8,128)(2,1)}, bf16[4,64,512]{2,1,0:T(8,128)(2,1)}, u32[]{:S(2)}, u32[]{:S(2)}) collective-permute-start(bf16[4,64,512]{2,1,0:T(8,128)(2,1)} %get-tuple-element.150), channel_id=1, source_target_pairs={{4,0},{8,4},{12,8},{16,12},{20,16},{24,20},{28,24},{32,28},{36,32}... | collective-permute-start | bytes 786440 | tf_op jit(solution)/shard_map/ppermute | solution.py:26
  560.2 142.9 %copy-start.161 = (s32[3]{0:T(128)S(1)}, s32[3]{0:T(128)}, u32[]{:S(2)}) copy-start(s32[3]{0:T(128)} %param.17) | copy-start | bytes 40
  561.2 144.5 %copy-start.37 = (f32[128,512]{1,0:T(8,128)}, f32[128,512]{1,0:T(8,128)S(1)}, u32[]{:S(2)}) copy-start(f32[128,512]{1,0:T(8,128)S(1)} %get-tuple-element.216) | copy-start | bytes 786436
  699.4 229.0 %all-gather.12.cloned.1.call-start = ((), (), s32[]{:S(2)}) async-start(), calls=%async_computation.4 | async-start | bytes 35389440 | tf_op jit(solution)/shard_map/all_gather | solution.py:215
  700.0 1189.5 %reduce-scatter.3.cloned.1.call-start = ((), (), s32[]{:S(2)}) async-start(), calls=%async_computation.5 | async-start | bytes 35389440 | tf_op jit(solution)/shard_map/reduce_scatter | solution.py:422
  705.8 212.1 %copy-start.135 = (bf16[8]{0:T(256)(128)(2,1)}, bf16[8]{0:T(256)(128)(2,1)S(1)}, u32[]{:S(2)}) copy-start(bf16[8]{0:T(256)(128)(2,1)S(1)} %get-tuple-element.208) | copy-start | bytes 52
  705.8 212.1 %copy-start.139 = (bf16[8]{0:T(256)(128)(2,1)}, bf16[8]{0:T(256)(128)(2,1)S(1)}, u32[]{:S(2)}) copy-start(bf16[8]{0:T(256)(128)(2,1)S(1)} %get-tuple-element.212) | copy-start | bytes 52
  705.8 215.5 %copy-start.133 = (bf16[8]{0:T(256)(128)(2,1)}, bf16[8]{0:T(256)(128)(2,1)S(1)}, u32[]{:S(2)}) copy-start(bf16[8]{0:T(256)(128)(2,1)S(1)} %get-tuple-element.209) | copy-start | bytes 52
  705.8 215.5 %copy-start.137 = (bf16[8]{0:T(256)(128)(2,1)}, bf16[8]{0:T(256)(128)(2,1)S(1)}, u32[]{:S(2)}) copy-start(bf16[8]{0:T(256)(128)(2,1)S(1)} %get-tuple-element.207) | copy-start | bytes 52
  705.8 218.9 %copy-start.129 = (bf16[8]{0:T(256)(128)(2,1)}, bf16[8]{0:T(256)(128)(2,1)S(1)}, u32[]{:S(2)}) copy-start(bf16[8]{0:T(256)(128)(2,1)S(1)} %get-tuple-element.210) | copy-start | bytes 52
  705.8 218.9 %copy-start.131 = (bf16[8]{0:T(256)(128)(2,1)}, bf16[8]{0:T(256)(128)(2,1)S(1)}, u32[]{:S(2)}) copy-start(bf16[8]{0:T(256)(128)(2,1)S(1)} %get-tuple-element.211) | copy-start | bytes 52
  728.4 153.5 %collective-permute-start.3 = (bf16[8,64,2048]{2,1,0:T(8,128)(2,1)}, bf16[8,64,2048]{2,1,0:T(8,128)(2,1)}, u32[]{:S(2)}, u32[]{:S(2)}) collective-permute-start(bf16[8,64,2048]{2,1,0:T(8,128)(2,1)} %all-gather.8.cloned.1.call-done), channel_id=1, source_target_pairs={{0,8},{4,12},{8,16},{12,20},{16,24},{20,28},{24,32},{28,36},{32,40... | collective-permute-start | bytes 6291464 | tf_op jit(solution)/shard_map/ppermute | solution.py:26
  736.3 147.5 %collective-permute-start.4 = (bf16[8,64,2048]{2,1,0:T(8,128)(2,1)}, bf16[8,64,2048]{2,1,0:T(8,128)(2,1)}, u32[]{:S(2)}, u32[]{:S(2)}) collective-permute-start(bf16[8,64,2048]{2,1,0:T(8,128)(2,1)} %all-gather.8.cloned.1.call-done), channel_id=1, source_target_pairs={{0,4},{4,8},{8,12},{12,16},{16,20},{20,24},{24,28},{28,32},{32,36}... | collective-permute-start | bytes 6291464 | tf_op jit(solution)/shard_map/ppermute | solution.py:26
  744.2 170.0 %collective-permute-start.5 = (bf16[8,64,2048]{2,1,0:T(8,128)(2,1)}, bf16[8,64,2048]{2,1,0:T(8,128)(2,1)}, u32[]{:S(2)}, u32[]{:S(2)}) collective-permute-start(bf16[8,64,2048]{2,1,0:T(8,128)(2,1)} %all-gather.8.cloned.1.call-done), channel_id=1, source_target_pairs={{4,0},{8,4},{12,8},{16,12},{20,16},{24,20},{28,24},{32,28},{36,32}... | collective-permute-start | bytes 6291464 | tf_op jit(solution)/shard_map/ppermute | solution.py:26
  745.5 170.5 %collective-permute-start.6 = (bf16[8,64,2048]{2,1,0:T(8,128)(2,1)}, bf16[8,64,2048]{2,1,0:T(8,128)(2,1)}, u32[]{:S(2)}, u32[]{:S(2)}) collective-permute-start(bf16[8,64,2048]{2,1,0:T(8,128)(2,1)} %all-gather.8.cloned.1.call-done), channel_id=1, source_target_pairs={{8,0},{12,4},{16,8},{20,12},{24,16},{28,20},{32,24},{36,28},{40,32... | collective-permute-start | bytes 6291464 | tf_op jit(solution)/shard_map/ppermute | solution.py:26
  749.2 130.2 %collective-permute-start.2 = (bf16[2,64,2048]{2,1,0:T(8,128)(2,1)}, bf16[2,64,2048]{2,1,0:T(8,128)(2,1)}, u32[]{:S(2)}, u32[]{:S(2)}) collective-permute-start(bf16[2,64,2048]{2,1,0:T(8,128)(2,1)} %get-tuple-element.145), channel_id=1, source_target_pairs={{0,12},{4,16},{8,20},{12,24},{16,28},{20,32},{24,36},{28,40},{32,4... | collective-permute-start | bytes 1572872 | tf_op jit(solution)/shard_map/ppermute | solution.py:26
  762.7 354.3 %copy-start.7 = (bf16[2048,256]{1,0:T(8,128)(2,1)}, bf16[2048,256]{1,0:T(8,128)(2,1)S(1)}, u32[]{:S(2)}) copy-start(bf16[2048,256]{1,0:T(8,128)(2,1)S(1)} %slice.961) | copy-start | bytes 3145732
  879.4 38.5 %collective-permute-start.7 = (bf16[2,64,2048]{2,1,0:T(8,128)(2,1)}, bf16[2,64,2048]{2,1,0:T(8,128)(2,1)S(1)}, u32[]{:S(2)}, u32[]{:S(2)}) collective-permute-start(bf16[2,64,2048]{2,1,0:T(8,128)(2,1)} %get-tuple-element.144), channel_id=1, source_target_pairs={{12,0},{16,4},{20,8},{24,12},{28,16},{32,20},{36,24},{40,28},{44,3... | collective-permute-start | bytes 1572872 | tf_op jit(solution)/shard_map/ppermute | solution.py:26
  1117.1 237.0 %copy-start.95 = (f32[4,2048]{1,0:T(4,128)}, f32[4,2048]{1,0:T(4,128)S(1)}, u32[]{:S(2)}) copy-start(f32[4,2048]{1,0:T(4,128)S(1)} %broadcast_divide_fusion) | copy-start | bytes 98308
  1343.5 120.8 %collective-permute-start.9 = (bf16[8,64,768]{2,1,0:T(8,128)(2,1)}, bf16[8,64,768]{2,1,0:T(8,128)(2,1)}, u32[]{:S(2)}, u32[]{:S(2)}) collective-permute-start(bf16[8,64,768]{2,1,0:T(8,128)(2,1)} %all_gather.34), channel_id=1, source_target_pairs={{0,8},{4,12},{8,16},{12,20},{16,24},{20,28},{24,32},{28,36},{32,40... | collective-permute-start | bytes 2359304 | tf_op jit(solution)/shard_map/ppermute | solution.py:26
  1347.8 119.1 %collective-permute-start.10 = (bf16[8,64,768]{2,1,0:T(8,128)(2,1)}, bf16[8,64,768]{2,1,0:T(8,128)(2,1)}, u32[]{:S(2)}, u32[]{:S(2)}) collective-permute-start(bf16[8,64,768]{2,1,0:T(8,128)(2,1)} %all_gather.34), channel_id=1, source_target_pairs={{0,4},{4,8},{8,12},{12,16},{16,20},{20,24},{24,28},{28,32},{32,36}... | collective-permute-start | bytes 2359304 | tf_op jit(solution)/shard_map/ppermute | solution.py:26
  1351.0 118.3 %collective-permute-start.11 = (bf16[8,64,768]{2,1,0:T(8,128)(2,1)}, bf16[8,64,768]{2,1,0:T(8,128)(2,1)}, u32[]{:S(2)}, u32[]{:S(2)}) collective-permute-start(bf16[8,64,768]{2,1,0:T(8,128)(2,1)} %all_gather.34), channel_id=1, source_target_pairs={{4,0},{8,4},{12,8},{16,12},{20,16},{24,20},{28,24},{32,28},{36,32}... | collective-permute-start | bytes 2359304 | tf_op jit(solution)/shard_map/ppermute | solution.py:26
  1352.3 118.3 %collective-permute-start.12 = (bf16[8,64,768]{2,1,0:T(8,128)(2,1)}, bf16[8,64,768]{2,1,0:T(8,128)(2,1)}, u32[]{:S(2)}, u32[]{:S(2)}) collective-permute-start(bf16[8,64,768]{2,1,0:T(8,128)(2,1)} %all_gather.34), channel_id=1, source_target_pairs={{8,0},{12,4},{16,8},{20,12},{24,16},{28,20},{32,24},{36,28},{40,32... | collective-permute-start | bytes 2359304 | tf_op jit(solution)/shard_map/ppermute | solution.py:26
  1362.0 100.6 %collective-permute-start.8 = (bf16[2,64,768]{2,1,0:T(8,128)(2,1)}, bf16[2,64,768]{2,1,0:T(8,128)(2,1)S(1)}, u32[]{:S(2)}, u32[]{:S(2)}) collective-permute-start(bf16[2,64,768]{2,1,0:T(8,128)(2,1)} %get-tuple-element.147), channel_id=1, source_target_pairs={{0,12},{4,16},{8,20},{12,24},{16,28},{20,32},{24,36},{28,40},{32,4... | collective-permute-start | bytes 589832 | tf_op jit(solution)/shard_map/ppermute | solution.py:26
  1429.3 684.6 %all-reduce.24.cloned.1.call-start = ((), (), s32[]{:S(2)}) async-start(), calls=%async_computation.9 | async-start | bytes 46923776
  1462.6 9.4 collective-permute-start.13
  1488.5 200.5 %copy-start.38 = (f32[128,512]{1,0:T(8,128)S(1)}, f32[128,512]{1,0:T(8,128)}, u32[]{:S(2)}) copy-start(f32[128,512]{1,0:T(8,128)} %copy-done.37) | copy-start | bytes 786436
  1489.0 280.2 %copy-start.83 = (bf16[8,16,512]{2,1,0:T(8,128)(2,1)S(1)}, bf16[8,16,512]{2,1,0:T(8,128)(2,1)}, u32[]{:S(2)}) copy-start(bf16[8,16,512]{2,1,0:T(8,128)(2,1)} %copy-done.82) | copy-start | bytes 393220
  1491.6 276.9 %copy-start.87 = (bf16[8,16,512]{2,1,0:T(8,128)(2,1)S(1)}, bf16[8,16,512]{2,1,0:T(8,128)(2,1)}, u32[]{:S(2)}) copy-start(bf16[8,16,512]{2,1,0:T(8,128)(2,1)} %copy-done.86) | copy-start | bytes 393220
  1491.6 277.3 %copy-start.85 = (bf16[8,16,512]{2,1,0:T(8,128)(2,1)S(1)}, bf16[8,16,512]{2,1,0:T(8,128)(2,1)}, u32[]{:S(2)}) copy-start(bf16[8,16,512]{2,1,0:T(8,128)(2,1)} %copy-done.84) | copy-start | bytes 393220
  1491.6 277.9 %copy-start.81 = (bf16[8,16,512]{2,1,0:T(8,128)(2,1)S(1)}, bf16[8,16,512]{2,1,0:T(8,128)(2,1)}, u32[]{:S(2)}) copy-start(bf16[8,16,512]{2,1,0:T(8,128)(2,1)} %copy-done.80) | copy-start | bytes 393220
  1491.6 278.2 %copy-start.79 = (bf16[8,16,512]{2,1,0:T(8,128)(2,1)S(1)}, bf16[8,16,512]{2,1,0:T(8,128)(2,1)}, u32[]{:S(2)}) copy-start(bf16[8,16,512]{2,1,0:T(8,128)(2,1)} %copy-done.78) | copy-start | bytes 393220
  1491.7 278.6 %copy-start.77 = (bf16[8,16,512]{2,1,0:T(8,128)(2,1)S(1)}, bf16[8,16,512]{2,1,0:T(8,128)(2,1)}, u32[]{:S(2)}) copy-start(bf16[8,16,512]{2,1,0:T(8,128)(2,1)} %copy-done.76) | copy-start | bytes 393220
  1491.7 278.9 %copy-start.75 = (bf16[8,16,512]{2,1,0:T(8,128)(2,1)S(1)}, bf16[8,16,512]{2,1,0:T(8,128)(2,1)}, u32[]{:S(2)}) copy-start(bf16[8,16,512]{2,1,0:T(8,128)(2,1)} %copy-done.74) | copy-start | bytes 393220
  1764.3 28.4 %collective-permute-start.14 = (bf16[4,64,512]{2,1,0:T(8,128)(2,1)S(1)}, bf16[4,64,512]{2,1,0:T(8,128)(2,1)S(1)}, u32[]{:S(2)}, u32[]{:S(2)}) collective-permute-start(bf16[4,64,512]{2,1,0:T(8,128)(2,1)S(1)} %get-tuple-element.149), channel_id=1, source_target_pairs={{0,4},{4,8},{8,12},{12,16},{16,20},{20,24},{24,28},{28,32},{32,36}... | collective-permute-start | bytes 786440 | tf_op jit(solution)/shard_map/ppermute | solution.py:26
  1767.3 25.5 %collective-permute-start.15 = (bf16[4,64,512]{2,1,0:T(8,128)(2,1)S(1)}, bf16[4,64,512]{2,1,0:T(8,128)(2,1)S(1)}, u32[]{:S(2)}, u32[]{:S(2)}) collective-permute-start(bf16[4,64,512]{2,1,0:T(8,128)(2,1)S(1)} %get-tuple-element.148), channel_id=1, source_target_pairs={{4,0},{8,4},{12,8},{16,12},{20,16},{24,20},{28,24},{32,28},{36,32}... | collective-permute-start | bytes 786440 | tf_op jit(solution)/shard_map/ppermute | solution.py:26
  1889.4 224.5 %copy-start.99 = (f32[10880]{0:T(1024)S(1)}, f32[10880]{0:T(1024)}, u32[]{:S(2)}) copy-start(f32[10880]{0:T(1024)} %param.21) | copy-start | bytes 130564
  1889.4 226.0 %copy-start.98 = (f32[34944]{0:T(1024)S(1)}, f32[34944]{0:T(1024)}, u32[]{:S(2)}) copy-start(f32[34944]{0:T(1024)} %param.19) | copy-start | bytes 419332
  1889.4 402.4 %reduce-scatter.5.cloned.1.call-start = ((), (), s32[]{:S(2)}) async-start(), calls=%async_computation.6 | async-start | bytes 7299072 | tf_op jit(solution)/shard_map/reduce_scatter | solution.py:425
  (151 other events, 4111.4 us)
Sparse Core Ops, SparseCore 0:
  10.3 219.3 all-gather.13
  231.4 163.3 all-gather.9
  397.1 207.8 all-gather.15
  699.5 23.8 all-gather.7
  724.9 175.6 all-gather.11
  1429.4 208.6 reduce-scatter.2
  1889.5 224.3 all-reduce.23
  2116.4 175.3 reduce-scatter.4
where the time goes:
time: 2310 us; the launch traced here: 2300 us
  blocking collectives  897 us (39%)
  waiting for transfers between devices  734 us (32%)
  other arithmetic  280 us (12%)
  local copies, waits for them, and re-layouts  175 us (8%)
  matrix products  140 us (6%)
  starting transfers between devices  52.3 us (2%)
    psum x10, blocking collectives, global_sums(): return lax.psum(values, ('rows', 'cols'))  850 us
    unnamed x9, waiting for transfers between devices  222 us
    all_gather x1, waiting for transfers between devices, per_device(): lax.all_gather(block_params.astype(jnp.bfloat16), ('rows', 'cols'), axis=...  194 us
    all_gather x1, other arithmetic, per_device(): lax.all_gather(block_params.astype(jnp.bfloat16), ('rows', 'cols'), axis=...  193 us
    reduce_scatter x1, waiting for transfers between devices, per_device(): lax.psum_scatter(rate_flat.astype(jnp.bfloat16), 'rows', scatter_dimensio...  175 us
    ppermute x16, waiting for transfers between devices, from_behind(): lax.ppermute(value, axis, [(source, source + steps) for source in range(f...  143 us
    unnamed x393, local copies, waits for them, and re-layouts  105 us
    dot_general x36, matrix products, conv_forward(): jnp.dot(masked.reshape(height * across, -1), kernel[3 * row_tap + col_tap...  53.5 us
  transfers between devices with their start and end apart: 24, of which 5 were waited for; matrix products, arithmetic and copies ran while one was open for 22% of the time, Pallas kernels for 0%

commit v1 on v0

--- a/solution.py
+++ b/solution.py
@@ -1,9 +1,19 @@
+import functools
 import math
 
 import jax
 import jax.numpy as jnp
 from jax import lax
+from jax.experimental import pallas as pl
+from jax.experimental.pallas import tpu as pltpu
 from jax.sharding import PartitionSpec as P
+
+MESH = pl.DeviceIdType.MESH
+ANY = pl.BlockSpec(memory_space=pl.ANY)
+VMEM = pl.BlockSpec(memory_space=pltpu.VMEM)
+BLOCK_ROWS = 273
+HEAD_ROWS = 85
+PAYLOAD = 384
 
 CIN = 2048
 MID = 512
@@ -20,10 +30,524 @@
 widest_margin = 18
 
 
-def from_behind(value, axis, steps):
-    count = lax.axis_size(axis)
-    first, last = (max(0, -steps), min(count, count - steps))
-    return lax.ppermute(value, axis, [(source, source + steps) for source in range(first, last)])
+def device_of(row, col):
+    return {"rows": row, "cols": col}
+
+
+def split_place():
+    row, col = lax.axis_index("rows"), lax.axis_index("cols")
+    return {
+        "y": (row // 16) + 2 * (col // 2),
+        "x": lax.rem(row // 4, 4),
+        "z": lax.rem(row, 4),
+        "core": lax.rem(col, 2),
+    }
+
+
+def device_at(place):
+    row = lax.rem(place["y"], 2) * 16 + place["x"] * 4 + place["z"]
+    return device_of(row, (place["y"] // 2) * 2 + place["core"])
+
+
+def moved(place, axis, step, extent=4):
+    other = dict(place)
+    other[axis] = lax.rem(place[axis] + step + extent, extent)
+    return other
+
+
+def meet(sources, targets):
+    barrier = pltpu.get_barrier_semaphore()
+    for device in sources:
+        pl.semaphore_signal(barrier, inc=1, device_id=device, device_id_type=MESH)
+    pl.semaphore_wait(barrier, targets)
+
+
+def remote(source, target, send_sem, recv_sem, device):
+    return pltpu.make_async_remote_copy(
+        src_ref=source,
+        dst_ref=target,
+        send_sem=send_sem,
+        recv_sem=recv_sem,
+        device_id=device,
+        device_id_type=MESH,
+    )
+
+
+def total_kernel(x_ref, o_ref, near, far, near_send, near_recv, far_send, far_recv):
+    row, col = lax.axis_index("rows"), lax.axis_index("cols")
+    near_me = (row // 16) * 4 + col
+    far_me = lax.rem(row, 16)
+
+    def near_device(index):
+        return device_of((index // 4) * 16 + far_me, lax.rem(index, 4))
+
+    def far_device(index):
+        return device_of((row // 16) * 16 + index, col)
+
+    near_others = [lax.rem(near_me + step, 8) for step in range(1, 8)]
+    far_others = [lax.rem(far_me + step, 16) for step in range(1, 16)]
+    meet(
+        [near_device(i) for i in near_others] + [far_device(i) for i in far_others],
+        len(near_others) + len(far_others),
+    )
+
+    def stage(source, buffer, me, others, device, send_sem, recv_sem):
+        for step, index in enumerate(others):
+            remote(source, buffer.at[me], send_sem.at[step], recv_sem.at[me], device(index)).start()
+        buffer[me] = source[...]
+        for step, index in enumerate(others):
+            copy = remote(source, buffer.at[index], send_sem.at[step], recv_sem.at[index], device(index))
+            copy.wait_send()
+            copy.wait_recv()
+        total = buffer[0]
+        for index in range(1, buffer.shape[0]):
+            total = total + buffer[index]
+        o_ref[...] = total
+
+    stage(x_ref, near, near_me, near_others, near_device, near_send, near_recv)
+    stage(o_ref, far, far_me, far_others, far_device, far_send, far_recv)
+
+
+def all_sum(packed, collective):
+    shape = packed.shape
+    return pl.pallas_call(
+        total_kernel,
+        out_shape=jax.ShapeDtypeStruct(shape, jnp.float32),
+        in_specs=[VMEM],
+        out_specs=VMEM,
+        scratch_shapes=[
+            pltpu.VMEM((8,) + shape, jnp.float32),
+            pltpu.VMEM((16,) + shape, jnp.float32),
+            pltpu.SemaphoreType.DMA((7,)),
+            pltpu.SemaphoreType.DMA((8,)),
+            pltpu.SemaphoreType.DMA((15,)),
+            pltpu.SemaphoreType.DMA((16,)),
+        ],
+        compiler_params=pltpu.CompilerParams(
+            collective_id=collective, has_side_effects=True, vmem_limit_bytes=32 * 1024 * 1024
+        ),
+    )(packed)
+
+
+def sums_over_all(pieces, collective):
+    flat = jnp.concatenate([piece.reshape(-1) for piece in pieces])
+    rows = -(-flat.shape[0] // 1024) * 8
+    packed = jnp.pad(flat, (0, rows * 128 - flat.shape[0])).reshape(rows, 128)
+    flat = all_sum(packed, collective).reshape(-1)
+    results = []
+    cursor = 0
+    for piece in pieces:
+        results.append(flat[cursor : cursor + piece.size].reshape(piece.shape))
+        cursor += piece.size
+    return results
+
+
+GATHER_ORDERS = (("z", "x", "y"), ("x", "y", "z"), ("y", "z", "x"))
+
+
+def axis_view(place, fixed):
+    index = [slice(None)] * 4
+    if "y" in fixed:
+        index[0], index[3] = lax.rem(place["y"], 2), place["y"] // 2
+    if "x" in fixed:
+        index[1] = place["x"]
+    if "z" in fixed:
+        index[2] = place["z"]
+    return tuple(index)
+
+
+def params_kernel(x_ref, o_ref, local_sem, sends, recvs, core_send, core_recv):
+    me = split_place()
+    partners = [moved(me, axis, step) for axis in "xyz" for step in (1, 2, 3)]
+    twin = moved(me, "core", 1, 2)
+    meet([device_at(place) for place in partners + [twin]], 10)
+
+    def rows_of(third):
+        return pl.ds(third * 128, 128)
+
+    def block(place, third, free):
+        fixed = [axis for axis in "xyz" if axis not in free]
+        return o_ref.at[axis_view(place, fixed) + (place["core"], rows_of(third))]
+
+    own = pltpu.make_async_copy(x_ref, o_ref.at[axis_view(me, "xyz") + (me["core"],)], local_sem)
+    own.start()
+
+    def copy(third, phase, step, place, source):
+        order = GATHER_ORDERS[third]
+        free = order[:phase]
+        target = moved(me, order[phase], step)
+        if phase == 0:
+            outgoing = x_ref.at[rows_of(third)]
+        else:
+            outgoing = block(place, third, free)
+        return remote(
+            outgoing,
+            block(source, third, free),
+            sends.at[third, phase, step - 1],
+            recvs.at[third, phase, step - 1],
+            device_at(target),
+        )
+
+    for phase in range(3):
+        for third in range(3):
+            if phase > 0:
+                axis = GATHER_ORDERS[third][phase - 1]
+                for step in (1, 2, 3):
+                    copy(third, phase - 1, step, me, moved(me, axis, 4 - step)).wait_recv()
+                if phase == 1 and third == 0:
+                    own.wait()
+            for step in (1, 2, 3):
+                copy(third, phase, step, me, me).start()
+    core_copies = []
+    for third in range(3):
+        order = GATHER_ORDERS[third]
+        for step in (0, 1, 2, 3):
+            if step:
+                copy(third, 2, step, me, moved(me, order[2], 4 - step)).wait_recv()
+            view = block(moved(me, order[2], 4 - step), third, order[:2])
+            core_copy = remote(
+                view, view, core_send.at[third, step], core_recv.at[third, step], device_at(twin)
+            )
+            core_copy.start()
+            core_copies.append(core_copy)
+    for phase in range(3):
+        for third in range(3):
+            for step in (1, 2, 3):
+                copy(third, phase, step, me, me).wait_send()
+    for third in range(3):
+        order = GATHER_ORDERS[third]
+        for step in (0, 1, 2, 3):
+            core_copies[third * 4 + step].wait_send()
+            view = block(moved(moved(me, order[2], 4 - step), "core", 1, 2), third, order[:2])
+            remote(
+                view, view, core_send.at[third, step], core_recv.at[third, step], device_at(twin)
+            ).wait_recv()
+
+
+def gather_params(payload, collective):
+    gathered = pl.pallas_call(
+        params_kernel,
+        out_shape=jax.ShapeDtypeStruct((2, 4, 4, 2, 2, PAYLOAD, 128), jnp.bfloat16),
+        in_specs=[ANY],
+        out_specs=ANY,
+        scratch_shapes=[
+            pltpu.SemaphoreType.DMA,
+            pltpu.SemaphoreType.DMA((3, 3, 3)),
+            pltpu.SemaphoreType.DMA((3, 3, 3)),
+            pltpu.SemaphoreType.DMA((3, 4)),
+            pltpu.SemaphoreType.DMA((3, 4)),
+        ],
+        compiler_params=pltpu.CompilerParams(collective_id=collective, has_side_effects=True),
+    )(payload)
+    return gathered.reshape(128, PAYLOAD, 128)
+
+
+def scatter_kernel(
+    p_ref, o_ref, held, twin_part, parts, sums, local_sem, core_sems, sends, recvs
+):
+    me = split_place()
+    partners = [moved(me, axis, step) for axis in "xyz" for step in (1, 2, 3)]
+    twin = moved(me, "core", 1, 2)
+    meet([device_at(place) for place in partners + [twin]], 10)
+    core_copy = remote(
+        p_ref.at[:, :, :, :, 1 - me["core"]], twin_part, core_sems.at[0], core_sems.at[1], device_at(twin)
+    )
+    core_copy.start()
+    own = pltpu.make_async_copy(p_ref.at[:, :, :, :, me["core"]], held, local_sem)
+    own.start()
+    own.wait()
+    core_copy.wait()
+
+    def add_block(step, carry):
+        low_y, x, z, high_y = step // 32, lax.rem(step // 8, 4), lax.rem(step // 2, 4), lax.rem(step, 2)
+        total = held[low_y, x, z, high_y].astype(jnp.float32) + twin_part[
+            low_y, x, z, high_y
+        ].astype(jnp.float32)
+        held[low_y, x, z, high_y] = total.astype(jnp.bfloat16)
+        return carry
+
+    lax.fori_loop(0, 64, add_block, 0)
+
+    def view_of(third, phase, place):
+        order = GATHER_ORDERS[third]
+        axis = order[2 - phase]
+        if phase == 0:
+            return held.at[axis_view(place, [axis]) + (pl.ds(third * 128, 128),)]
+        left = order[: 3 - phase]
+        index = []
+        for name, key in (("y", 0), ("x", 1), ("z", 2), ("y", 3)):
+            if name not in left:
+                continue
+            if name != axis:
+                index.append(slice(None))
+            elif name == "y":
+                index.append(lax.rem(place["y"], 2) if key == 0 else place["y"] // 2)
+            else:
+                index.append(place[name])
+        return sums[third][phase - 1].at[tuple(index)]
+
+    def copy(third, phase, step):
+        axis = GATHER_ORDERS[third][2 - phase]
+        target = moved(me, axis, step)
+        return remote(
+            view_of(third, phase, target),
+            parts[third][phase].at[step - 1],
+            sends.at[third, phase, step - 1],
+            recvs.at[third, phase, step - 1],
+            device_at(target),
+        )
+
+    for phase in range(4):
+        for third in range(3):
+            if phase > 0:
+                total = view_of(third, phase - 1, me)[...].astype(jnp.float32)
+                for step in (1, 2, 3):
+                    copy(third, phase - 1, step).wait_recv()
+                    total = total + parts[third][phase - 1][step - 1].astype(jnp.float32)
+                if phase == 3:
+                    o_ref[pl.ds(third * 128, 128), :] = total
+                else:
+                    sums[third][phase - 1][...] = total.astype(jnp.bfloat16)
+            if phase < 3:
+                for step in (1, 2, 3):
+                    copy(third, phase, step).start()
+    for phase in range(3):
+        for third in range(3):
+            for step in (1, 2, 3):
+                copy(third, phase, step).wait_send()
+
+
+def scatter_entry(p_ref, o_ref, held, twin_part, *rest):
+    parts = [rest[3 * third : 3 * third + 3] for third in range(3)]
+    sums = [rest[9 + 2 * third : 11 + 2 * third] for third in range(3)]
+    scatter_kernel(p_ref, o_ref, held, twin_part, parts, sums, *rest[15:])
+
+
+def scatter_params(packed, collective):
+    lengths = {"y": (2, 2), "x": (4,), "z": (4,)}
+
+    def shape_left(left):
+        shape = ()
+        for name, number in (("y", 2), ("x", 4), ("z", 4), ("y", 2)):
+            if name in left:
+                shape += (number,)
+        return shape + (128, 128)
+
+    parts = []
+    sums = []
+    for order in GATHER_ORDERS:
+        for phase in range(3):
+            parts.append(pltpu.VMEM((3,) + shape_left(order[: 2 - phase]), jnp.bfloat16))
+        for phase in range(2):
+            sums.append(pltpu.VMEM(shape_left(order[: 2 - phase]), jnp.bfloat16))
+    half = (2, 4, 4, 2, PAYLOAD, 128)
+    return pl.pallas_call(
+        scatter_entry,
+        out_shape=jax.ShapeDtypeStruct((PAYLOAD, 128), jnp.float32),
+        in_specs=[ANY],
+        out_specs=VMEM,
+        scratch_shapes=[pltpu.VMEM(half, jnp.bfloat16), pltpu.VMEM(half, jnp.bfloat16)]
+        + parts
+        + sums
+        + [
+            pltpu.SemaphoreType.DMA,
+            pltpu.SemaphoreType.DMA((2,)),
+            pltpu.SemaphoreType.DMA((3, 3, 3)),
+            pltpu.SemaphoreType.DMA((3, 3, 3)),
+        ],
+        compiler_params=pltpu.CompilerParams(
+            collective_id=collective, has_side_effects=True, vmem_limit_bytes=56 * 1024 * 1024
+        ),
+    )(packed.reshape(2, 4, 4, 2, 2, PAYLOAD, 128))
+
+
+def neighbour(row, col, offset):
+    return lax.rem(row + offset[0] + 32, 32), lax.rem(col + offset[1] + 4, 4)
+
+
+def exchange_kernel(count, transfers, *refs):
+    ins, outs = refs[:count], refs[count:-3]
+    sends, recvs, locals_ = refs[-3:]
+    row, col = lax.axis_index("rows"), lax.axis_index("cols")
+    offsets = sorted({item[4] for item in transfers if item[4] != (0, 0)})
+    meet(
+        [device_of(*neighbour(row, col, (-o[0], -o[1]))) for o in offsets],
+        len(offsets),
+    )
+
+    def copy(number, receiving):
+        source_index, source, out_index, target, offset = transfers[number]
+        there = neighbour(row, col, offset)
+        origin = neighbour(row, col, (-offset[0], -offset[1])) if receiving else (row, col)
+        outgoing = ins[source_index].at[source(row, col)]
+        incoming = outs[out_index].at[target(*origin)]
+        if offset == (0, 0):
+            return pltpu.make_async_copy(outgoing, incoming, locals_.at[number])
+        return remote(outgoing, incoming, sends.at[number], recvs.at[number], device_of(*there))
+
+    for number, item in enumerate(transfers):
+        copy(number, False).start()
+    for number, item in enumerate(transfers):
+        if item[4] == (0, 0):
+            copy(number, False).wait()
+        else:
+            copy(number, True).wait_send()
+            copy(number, True).wait_recv()
+
+
+def exchange(arrays, shapes, transfers, collective):
+    number = len(transfers)
+    return pl.pallas_call(
+        functools.partial(exchange_kernel, len(arrays), transfers),
+        out_shape=[jax.ShapeDtypeStruct(shape, jnp.bfloat16) for shape in shapes],
+        in_specs=[VMEM] * len(arrays),
+        out_specs=[VMEM] * len(shapes),
+        scratch_shapes=[pltpu.SemaphoreType.DMA((number,)) for _ in range(3)],
+        compiler_params=pltpu.CompilerParams(
+            collective_id=collective, has_side_effects=True, vmem_limit_bytes=48 * 1024 * 1024
+        ),
+    )(*arrays)
+
+
+def every(row, col):
+    return (slice(None),)
+
+
+def halo_window(act, collective):
+    height, across, _ = act.shape
+    half = height // 2
+    transfers = []
+    for row_step in (-1, 0, 1):
+        for col_step in (-1, 0, 1):
+            rows = {-1: slice(0, half), 0: slice(0, height), 1: slice(half, height)}[row_step]
+            top = {-1: half + height, 0: half, 1: 0}[row_step]
+            left = {-1: 2 * across, 0: across, 1: 0}[col_step]
+            size = rows.stop - rows.start
+            transfers.append(
+                (
+                    0,
+                    lambda row, col, rows=rows: (pl.ds(rows.start, rows.stop - rows.start),),
+                    0,
+                    lambda row, col, top=top, size=size, left=left: (
+                        pl.ds(top, size),
+                        pl.ds(left, across),
+                    ),
+                    (row_step, col_step),
+                )
+            )
+    (window,) = exchange([act], [(2 * height, 3 * across, act.shape[2])], transfers, collective)
+    inside = jnp.arange(3 * across) + (lax.axis_index("cols") - 1) * across
+    keep = ((inside >= 0) & (inside < 4 * across)).astype(window.dtype)
+    return window * keep[None, :, None]
+
+
+def columns_to_channels(own, collective):
+    height, across, channels = own.shape
+    part = channels // 4
+    transfers = [
+        (
+            0,
+            lambda row, col, step=step: (
+                slice(None),
+                slice(None),
+                pl.ds(pl.multiple_of(lax.rem(col + step, 4) * part, part), part),
+            ),
+            0,
+            lambda row, col: (
+                slice(None),
+                pl.ds(pl.multiple_of(col * across, across), across),
+            ),
+            (0, step),
+        )
+        for step in range(4)
+    ]
+    return exchange([own], [(height, 4 * across, part)], transfers, collective)[0]
+
+
+def channels_to_columns(slab, collective):
+    height, width, channels = slab.shape
+    across = width // 4
+    transfers = [
+        (
+            0,
+            lambda row, col, step=step: (
+                slice(None),
+                pl.ds(pl.multiple_of(lax.rem(col + step, 4) * across, across), across),
+            ),
+            0,
+            lambda row, col: (col,),
+            (0, step),
+        )
+        for step in range(4)
+    ]
+    return exchange([slab], [(4, height, across, channels)], transfers, collective)[0]
+
+
+def channels_to_columns_back(slab, collective):
+    height, width, part = slab.shape
+    across = width // 4
+    transfers = [
+        (
+            0,
+            lambda row, col, step=step: (
+                slice(None),
+                pl.ds(pl.multiple_of(lax.rem(col + step, 4) * across, across), across),
+            ),
+            0,
+            lambda row, col: (
+                slice(None),
+                slice(None),
+                pl.ds(pl.multiple_of(col * part, part), part),
+            ),
+            (0, step),
+        )
+        for step in range(4)
+    ]
+    return exchange([slab], [(height, across, 4 * part)], transfers, collective)[0]
+
+
+def columns_together(own, collective):
+    height, across, channels = own.shape
+    transfers = [
+        (
+            0,
+            every,
+            0,
+            lambda row, col: (
+                slice(None),
+                pl.ds(pl.multiple_of(col * across, across), across),
+            ),
+            (0, step),
+        )
+        for step in range(4)
+    ]
+    return exchange([own], [(height, 4 * across, channels)], transfers, collective)[0]
+
+
+def shifted_rows(arrays, pick, collective):
+    height, across, channels = arrays[0].shape
+    transfers = []
+    for branch, rate in enumerate(rate_list):
+        for direction in range(2):
+            for hop in range(4):
+                if direction == 0:
+                    first, last = max(0, height * hop - rate), min(height, height * hop - rate + height)
+                    top = first + rate - height * hop
+                else:
+                    first, last = max(0, rate - height * hop), min(height, rate - height * hop + height)
+                    top = first - rate + height * hop
+                if first >= last:
+                    continue
+                transfers.append(
+                    (
+                        pick(branch, direction),
+                        lambda row, col, first=first, last=last: (pl.ds(first, last - first),),
+                        2 * branch + direction,
+                        lambda row, col, top=top, size=last - first: (pl.ds(top, size),),
+                        (hop if direction == 0 else -hop, 0),
+                    )
+                )
+    return exchange(arrays, [(height, across, channels)] * 6, transfers, collective)
 
 
 def silu_slope(values):
@@ -62,43 +586,6 @@
     return jnp.pad(joined, (0, length - joined.shape[0]))
 
 
-def global_sums(values):
-    return lax.psum(values, ("rows", "cols"))
-
-
-def neighbour_rows(stripe, offset):
-    return from_behind(stripe, "rows", offset)
-
-
-def all_columns(stripe):
-    return lax.all_gather(stripe, "cols", axis=1, tiled=True)
-
-
-def rows_around(stripe, margin):
-    height = stripe.shape[0]
-    hop_count = -(-margin // height)
-    upper_parts = []
-    lower_parts = []
-    for distance in range(hop_count, 0, -1):
-        needed = min(height, margin - (distance - 1) * height)
-        upper_parts.append(neighbour_rows(stripe[height - needed :], distance))
-    for distance in range(1, hop_count + 1):
-        needed = min(height, margin - (distance - 1) * height)
-        lower_parts.append(neighbour_rows(stripe[:needed], -distance))
-    return jnp.concatenate(upper_parts + [stripe] + lower_parts, axis=0)
-
-
-def full_window(stripe, margin):
-    widened = rows_around(all_columns(stripe), margin)
-    return jnp.pad(widened, ((0, 0), (margin, margin), (0, 0)))
-
-
-def extend(stripe, margin):
-    across = stripe.shape[1]
-    padded = full_window(stripe, margin)
-    return lax.dynamic_slice_in_dim(padded, lax.axis_index("cols") * across, across + 2 * margin, 1)
-
-
 def row_masks(all_ids, first_row, height, margin, dilation):
     padded = jnp.pad(all_ids, (margin, margin), constant_values=-1)
     window = lax.dynamic_slice_in_dim(padded, first_row, height + 2 * margin)
@@ -115,7 +602,7 @@
     for row_tap in range(3):
         for col_tap in range(3):
             top_row = margin + (row_tap - 1) * dilation
-            left_col = margin + (col_tap - 1) * dilation
+            left_col = across + (col_tap - 1) * dilation
             masked = (
                 window[top_row : top_row + height, left_col : left_col + across]
                 * mask_list[row_tap][:, None, None]
@@ -134,7 +621,7 @@
     for row_tap in range(3):
         for col_tap in range(3):
             top_row = margin + (row_tap - 1) * dilation
-            left_col = margin + (col_tap - 1) * dilation
+            left_col = across + (col_tap - 1) * dilation
             masked = (
                 window[top_row : top_row + height, left_col : left_col + across]
                 * mask_list[row_tap][:, None, None]
@@ -155,7 +642,7 @@
     for row_tap in range(3):
         for col_tap in range(3):
             top_row = margin - (row_tap - 1) * dilation
-            left_col = margin - (col_tap - 1) * dilation
+            left_col = across - (col_tap - 1) * dilation
             region = (
                 grad_window[top_row : top_row + height, left_col : left_col + across]
                 * mask_list[2 - row_tap][:, None, None]
@@ -207,15 +694,25 @@
     total_pixels = rows_all * columns
     images = max(rows_all // 64, 2)
     highest = lax.Precision.HIGHEST
-    block_all, head_all = (
-        lax.all_gather(block_params.astype(jnp.bfloat16), ("rows", "cols"), axis=0, tiled=True),
-        lax.all_gather(head_params.astype(jnp.bfloat16), ("rows", "cols"), axis=0, tiled=True),
+    payload = jnp.concatenate(
+        [
+            block_params.astype(jnp.bfloat16).reshape(BLOCK_ROWS, 128),
+            head_params.astype(jnp.bfloat16).reshape(HEAD_ROWS, 128),
+            jnp.pad(
+                image_rows.astype(jnp.bfloat16).reshape(1, height),
+                ((0, PAYLOAD - BLOCK_ROWS - HEAD_ROWS - 1), (0, 128 - height)),
+            ),
+        ],
+        axis=0,
     )
     rate_slab = lax.all_gather(rate_params.astype(jnp.bfloat16), "rows", axis=1, tiled=True)
-    rate_block = lax.all_gather(rate_slab, "cols", axis=0, tiled=True)
-    slab = rate_block.shape[0]
-    w_rates = rate_block.reshape(slab, 3, 9, ASPP).transpose(1, 2, 0, 3)
-    all_ids = lax.all_gather(image_rows, "rows", axis=0, tiled=True)
+    everything = gather_params(payload, 1)
+    block_all = everything[:, :BLOCK_ROWS].reshape(-1)
+    head_all = everything[:, BLOCK_ROWS : BLOCK_ROWS + HEAD_ROWS].reshape(-1)
+    all_ids = everything.reshape(32, 4, PAYLOAD, 128)[:, 0, BLOCK_ROWS + HEAD_ROWS, :height]
+    all_ids = all_ids.reshape(-1).astype(jnp.int32)
+    slab = rate_slab.shape[0]
+    w_rates = rate_slab.reshape(slab, 3, 9, ASPP)
     first_row = lax.axis_index("rows") * height
     w_reduce, w_spatial, w_expand, mid_norm, out_norm = unpack(block_all, block_layout())
     w_point, w_pool, pool_bias, w_project, head_norm, w_heads, heads_bias = unpack(
@@ -238,42 +735,62 @@
     )
     first_pre = jnp.dot(inputs, w_reduce, preferred_element_type=jnp.float32)
     first_cent, first_norm, first_scale = normalize(
-        first_pre, global_sums(moments(first_pre)), total_pixels, mid_norm[0, 0], mid_norm[0, 1]
+        first_pre, sums_over_all(moments(first_pre), 2), total_pixels, mid_norm[0, 0], mid_norm[0, 1]
     )
     first_act = jax.nn.silu(first_norm).astype(jnp.bfloat16)
-    block_window = extend(first_act.reshape(height, across, MID), block_dilation)
+    block_window = halo_window(first_act.reshape(height, across, MID), 3)
     second_pre = conv_forward(
         block_window, w_spatial, block_masks, block_dilation, block_dilation, height, across
     )
     second_cent, second_norm, second_scale = normalize(
-        second_pre, global_sums(moments(second_pre)), total_pixels, mid_norm[1, 0], mid_norm[1, 1]
+        second_pre, sums_over_all(moments(second_pre), 4), total_pixels, mid_norm[1, 0], mid_norm[1, 1]
     )
     second_act = jax.nn.silu(second_norm).astype(jnp.bfloat16)
     third_pre = jnp.dot(second_act, w_expand, preferred_element_type=jnp.float32)
     third_cent, third_norm, third_scale = normalize(
-        third_pre, global_sums(moments(third_pre)), total_pixels, out_norm[0], out_norm[1]
+        third_pre, sums_over_all(moments(third_pre), 5), total_pixels, out_norm[0], out_norm[1]
     )
     residual = third_norm + inputs.astype(jnp.float32)
     block_out = jax.nn.silu(residual).astype(jnp.bfloat16)
     grid = block_out.reshape(height, across, channels)
-    conv_window = extend(grid, widest_margin)
-    rate_parts = [
-        conv_forward(
-            conv_window,
-            w_rates[branch],
-            rate_masks[branch],
-            widest_margin,
-            rate_list[branch],
-            height,
-            across,
+    width = 4 * across
+    slab_map = columns_to_channels(grid, 6)
+    slab_padded = jnp.pad(slab_map, ((0, 0), (widest_margin, widest_margin), (0, 0)))
+    tap_sums = []
+    for branch, rate in enumerate(rate_list):
+        running = None
+        for col_tap in range(3):
+            start = widest_margin + (col_tap - 1) * rate
+            moved_map = slab_padded[:, start : start + width].reshape(height * width, slab)
+            part = jnp.dot(
+                moved_map,
+                w_rates[:, branch, col_tap::3].reshape(slab, 3 * ASPP),
+                preferred_element_type=jnp.float32,
+            )
+            running = part if running is None else running + part
+        tap_sums.append(running.astype(jnp.bfloat16))
+    tap_map = jnp.concatenate(tap_sums, axis=1).reshape(height, width, 9 * ASPP)
+    tap_parts = channels_to_columns(tap_map, 7)
+    tap_own = jnp.sum(tap_parts.astype(jnp.float32), axis=0).reshape(height, across, 3, 3, ASPP)
+    moved_taps = shifted_rows(
+        [tap_own[:, :, branch, tap].astype(jnp.bfloat16) for branch in range(3) for tap in (0, 2)],
+        lambda branch, direction: 2 * branch + direction,
+        8,
+    )
+    rate_parts = []
+    for branch in range(3):
+        masks = [mask.astype(jnp.float32)[:, None, None] for mask in rate_masks[branch]]
+        total = (
+            tap_own[:, :, branch, 1]
+            + moved_taps[2 * branch].astype(jnp.float32) * masks[0]
+            + moved_taps[2 * branch + 1].astype(jnp.float32) * masks[2]
         )
-        for branch in range(3)
-    ]
+        rate_parts.append(total.reshape(pixels, ASPP))
     branch_list = [jnp.dot(block_out, w_point, preferred_element_type=jnp.float32)] + rate_parts
     branch_pre = jnp.stack(branch_list)
     pool_local = jnp.dot(member, jnp.sum(grid, axis=1, dtype=jnp.float32), precision=highest)
-    branch_sums, branch_squares, pool_total = global_sums(
-        (jnp.sum(branch_pre, axis=1), jnp.sum(branch_pre * branch_pre, axis=1), pool_local)
+    branch_sums, branch_squares, pool_total = sums_over_all(
+        (jnp.sum(branch_pre, axis=1), jnp.sum(branch_pre * branch_pre, axis=1), pool_local), 9
     )
     branch_gain = head_norm[:4, 0][:, None, :]
     branch_cent, branch_norm, branch_scale = normalize(
@@ -295,7 +812,7 @@
     ).astype(jnp.bfloat16)
     projected = jnp.dot(joined, w_project, preferred_element_type=jnp.float32)
     proj_cent, proj_norm, proj_scale = normalize(
-        projected, global_sums(moments(projected)), total_pixels, head_norm[4, 0], head_norm[4, 1]
+        projected, sums_over_all(moments(projected), 10), total_pixels, head_norm[4, 0], head_norm[4, 1]
     )
     feature_map = jax.nn.silu(proj_norm).astype(jnp.bfloat16)
     logits = jnp.dot(feature_map, w_heads, preferred_element_type=jnp.float32) + heads_bias
@@ -340,8 +857,8 @@
     proj_grad_norm = feature_grad_map * silu_slope(proj_norm)
     proj_shift_grad = jnp.sum(proj_grad_norm, axis=0)
     proj_gain_grad = jnp.sum(proj_grad_norm * proj_cent, axis=0)
-    loss_total, proj_shift_all, proj_gain_all = global_sums(
-        (loss_local, proj_shift_grad, proj_gain_grad)
+    loss_total, proj_shift_all, proj_gain_all = sums_over_all(
+        (loss_local, proj_shift_grad, proj_gain_grad), 11
     )
     projected_grad = norm_back(
         proj_grad_norm,
@@ -365,8 +882,8 @@
     branch_grad_norm = branch_in_grad * silu_slope(branch_norm)
     branch_shift_grad = jnp.sum(branch_grad_norm, axis=1)
     branch_gain_grad = jnp.sum(branch_grad_norm * branch_cent, axis=1)
-    branch_shift_all, branch_gain_all, pool_act_grad = global_sums(
-        (branch_shift_grad, branch_gain_grad, pool_act_local)
+    branch_shift_all, branch_gain_all, pool_act_grad = sums_over_all(
+        (branch_shift_grad, branch_gain_grad, pool_act_local), 12
     )
     branch_grad = norm_back(
         branch_grad_norm,
@@ -389,42 +906,43 @@
         "pc,po->co", block_out, branch_grad[0], preferred_element_type=jnp.float32
     )
     out_grad = jnp.einsum("po,co->pc", branch_grad[0], w_point, preferred_element_type=jnp.float32)
-    rate_stack = jnp.concatenate([branch_grad[1], branch_grad[2], branch_grad[3]], axis=1).reshape(
-        height, across, 3 * ASPP
-    )
-    rate_grads = []
-    grad_window = extend(rate_stack, widest_margin)
+    rate_grad_maps = [branch_grad[branch + 1].reshape(height, across, ASPP) for branch in range(3)]
+    moved_grads = shifted_rows(rate_grad_maps, lambda branch, direction: branch, 13)
+    stacked = []
     for branch in range(3):
-        rate_grads.append(
-            conv_weight_grad(
-                conv_window,
-                branch_grad[branch + 1],
-                rate_masks[branch],
-                widest_margin,
-                rate_list[branch],
-                height,
-                across,
-            )
-        )
-        out_grad = out_grad + conv_input_grad(
-            grad_window[:, :, branch * ASPP : (branch + 1) * ASPP],
-            w_rates[branch],
-            rate_masks[branch],
-            widest_margin,
-            rate_list[branch],
-            height,
-            across,
-        )
+        masks = [mask[:, None, None] for mask in rate_masks[branch]]
+        stacked.append(moved_grads[2 * branch + 1] * masks[2])
+        stacked.append(rate_grad_maps[branch])
+        stacked.append(moved_grads[2 * branch] * masks[0])
+    wide_grads = columns_together(jnp.concatenate(stacked, axis=2), 14)
+    wide_padded = jnp.pad(wide_grads, ((0, 0), (widest_margin, widest_margin), (0, 0)))
+    tap_list = []
+    for branch, rate in enumerate(rate_list):
+        for row_tap in range(3):
+            first_channel = (3 * branch + row_tap) * ASPP
+            for col_tap in range(3):
+                start = widest_margin - (col_tap - 1) * rate
+                tap_list.append(
+                    wide_padded[:, start : start + width, first_channel : first_channel + ASPP]
+                )
+    tap_grads = jnp.concatenate(tap_list, axis=2).reshape(height * width, 27 * ASPP)
+    rate_flat = jnp.einsum(
+        "pc,pn->cn",
+        slab_map.reshape(height * width, slab),
+        tap_grads,
+        preferred_element_type=jnp.float32,
+    ).astype(jnp.bfloat16)
+    rate_share = lax.psum_scatter(rate_flat, "rows", scatter_dimension=1, tiled=True).astype(
+        jnp.float32
+    )
+    slab_grad = jnp.einsum(
+        "pn,cn->pc", tap_grads, rate_slab, preferred_element_type=jnp.float32
+    ).astype(jnp.bfloat16)
+    own_parts = channels_to_columns_back(slab_grad.reshape(height, width, slab), 15)
+    out_grad = out_grad + own_parts.reshape(pixels, channels).astype(jnp.float32)
     out_grad = out_grad + jnp.broadcast_to(
         pool_back_rows[:, None, :], (height, across, channels)
     ).reshape(pixels, channels)
-    rate_flat = jnp.stack(rate_grads).transpose(2, 0, 1, 3).reshape(slab, 27 * ASPP)
-    rate_flat = lax.psum_scatter(
-        rate_flat.astype(jnp.bfloat16), "cols", scatter_dimension=0, tiled=True
-    ).astype(jnp.float32)
-    rate_share = lax.psum_scatter(
-        rate_flat.astype(jnp.bfloat16), "rows", scatter_dimension=1, tiled=True
-    ).astype(jnp.float32)
     norm_grads = jnp.concatenate(
         [
             jnp.stack([branch_gain_grad, branch_shift_grad], axis=1),
@@ -452,7 +970,7 @@
         third_cent,
         third_scale,
         out_norm[0],
-        global_sums((third_shift_grad, third_gain_grad)),
+        sums_over_all((third_shift_grad, third_gain_grad), 16),
         total_pixels,
     ).astype(jnp.bfloat16)
     grad_expand = jnp.einsum(
@@ -469,13 +987,13 @@
         second_cent,
         second_scale,
         mid_norm[1, 0],
-        global_sums((second_shift_grad, second_gain_grad)),
+        sums_over_all((second_shift_grad, second_gain_grad), 17),
         total_pixels,
     ).astype(jnp.bfloat16)
     grad_spatial = conv_weight_grad(
         block_window, second_grad, block_masks, block_dilation, block_dilation, height, across
     )
-    block_grad_window = extend(second_grad.reshape(height, across, MID), block_dilation)
+    block_grad_window = halo_window(second_grad.reshape(height, across, MID), 18)
     first_act_grad = conv_input_grad(
         block_grad_window, w_spatial, block_masks, block_dilation, block_dilation, height, across
     )
@@ -487,7 +1005,7 @@
         first_cent,
         first_scale,
         mid_norm[0, 0],
-        global_sums((first_shift_grad, first_gain_grad)),
+        sums_over_all((first_shift_grad, first_gain_grad), 19),
         total_pixels,
     ).astype(jnp.bfloat16)
     grad_reduce = jnp.einsum("pc,po->co", inputs, first_grad, preferred_element_type=jnp.float32)
@@ -504,10 +1022,17 @@
     block_grad = pack_flat(
         [grad_reduce, grad_spatial, grad_expand, mid_grads, out_grads], block_all.shape[0]
     )
-    block_share, head_share = (
-        lax.psum_scatter(block_grad, ("rows", "cols"), scatter_dimension=0, tiled=True),
-        lax.psum_scatter(head_grad, ("rows", "cols"), scatter_dimension=0, tiled=True),
-    )
+    packed = jnp.concatenate(
+        [
+            block_grad.astype(jnp.bfloat16).reshape(128, BLOCK_ROWS, 128),
+            head_grad.astype(jnp.bfloat16).reshape(128, HEAD_ROWS, 128),
+            jnp.zeros((128, PAYLOAD - BLOCK_ROWS - HEAD_ROWS, 128), jnp.bfloat16),
+        ],
+        axis=1,
+    )
+    shares_all = scatter_params(packed, 20)
+    block_share = shares_all[:BLOCK_ROWS].reshape(-1)
+    head_share = shares_all[BLOCK_ROWS : BLOCK_ROWS + HEAD_ROWS].reshape(-1)
     block_moment_next = MOMENTUM_KEEP * block_moment + block_share
     head_moment_next = MOMENTUM_KEEP * head_moment + head_share
     rate_moment_next = MOMENTUM_KEEP * rate_moment + rate_share

time: 2310 us -> 791 us (0.34)
  blocking collectives: 897 us -> 0 us
  waiting for transfers between devices: 734 us -> 78.6 us
  Pallas kernels: 0 us -> 410 us
  other arithmetic: 280 us -> 52.5 us
  matrix products: 140 us -> 83 us
  starting transfers between devices: 52.3 us -> 0.08 us
  local copies, waits for them, and re-layouts: 175 us -> 138 us
    psum x10 -> x0, blocking collectives: 850 us -> none  [global_sums(): return lax.psum(values, ('rows', 'cols'))]
    pallas_call x0 -> x20, Pallas kernels: none -> 410 us  [the longest x10 146 us: all_sum(): pl.pallas_call(total_kernel, out_shape=jax.ShapeDtypeStruct(shape, jnp.fl...]
    unnamed x9 -> x2, waiting for transfers between devices: 222 us -> 0.03 us
    all_gather x2 -> x0, other arithmetic: 210 us -> none  [the longest x1 193 us: per_device(): lax.all_gather(block_params.astype(jnp.bfloat16), ('rows', 'cols'), axis=...]
    all_gather x4 -> x0, waiting for transfers between devices: 194 us -> none  [the longest x1 194 us: per_device(): lax.all_gather(block_params.astype(jnp.bfloat16), ('rows', 'cols'), axis=...]
    ppermute x16 -> x0, waiting for transfers between devices: 143 us -> none  [from_behind(): lax.ppermute(value, axis, [(source, source + steps) for source in range(f...]
    reduce_scatter x2 -> x1, waiting for transfers between devices: 175 us -> 78.6 us  [per_device(): lax.psum_scatter(rate_flat, 'rows', scatter_dimension=1, tiled=True)]
    unnamed x393 -> x250, local copies, waits for them, and re-layouts: 105 us -> 38.8 us
  transfers between devices with their start and end apart: 24 -> 2, of which waited for: 5 -> 1; matrix products, arithmetic and copies ran while one was open for 22% -> 18% of each run, Pallas kernels for 0% -> 27%
where the time goes in v1:
time: 791 us; the launch traced here: 784 us
  Pallas kernels  410 us (52%)
  local copies, waits for them, and re-layouts  138 us (17%)
  matrix products  83 us (10%)
  waiting for transfers between devices  78.6 us (10%)
  other arithmetic  52.5 us (7%)
  between operations  20.7 us (3%)
    pallas_call x10, Pallas kernels, all_sum(): pl.pallas_call(total_kernel, out_shape=jax.ShapeDtypeStruct(shape, jnp.fl...  146 us
    pallas_call x8, Pallas kernels, exchange(): pl.pallas_call(functools.partial(exchange_kernel, len(arrays), transfers)...  126 us
    reduce_scatter x1, waiting for transfers between devices, per_device(): lax.psum_scatter(rate_flat, 'rows', scatter_dimension=1, tiled=True)  78.6 us
    pallas_call x1, Pallas kernels, scatter_params(): pl.pallas_call(scatter_entry, out_shape=jax.ShapeDtypeStruct((PAYLOAD, 12...  71.7 us
    pallas_call x1, Pallas kernels, gather_params(): pl.pallas_call(params_kernel, out_shape=jax.ShapeDtypeStruct((2, 4, 4, 2,...  66.4 us
    slice x5, local copies, waits for them, and re-layouts, unpack(): pieces.append(vector[cursor:cursor + number].reshape(extent))  42.9 us
    unnamed x250, local copies, waits for them, and re-layouts  38.8 us
    concatenate x3, local copies, waits for them, and re-layouts, per_device(): jnp.concatenate([block_grad.astype(jnp.bfloat16).reshape(128, BLOCK_ROWS,...  17.5 us
  transfers between devices with their start and end apart: 2, of which 1 were waited for; matrix products, arithmetic and copies ran while one was open for 18% of the time, Pallas kernels for 27%

profile of v1, /device:TPU:0, one launch (start us, length us, event | category | flops | bytes accessed | tf_op | source)
XLA Modules:
  0.0 783.6 jit_solution(9557745984802387375)
XLA Ops:
  14.1 66.4 %shard_map.163 = bf16[2,4,4,2,2,384,128]{6,5,4,3,2,1,0:T(8,128)(2,1)} custom-call(bf16[384,128]{1,0:T(8,128)(2,1)} %fusion.95.x_ref), custom_call_target="tpu_custom_call" | custom-call | tf_op jit(solution)/shard_map/pallas_call | solution.py:228
  80.5 3.3 slice.760
  83.9 7.8 slice.730
  91.6 2.9 slice.617
  94.5 2.4 reshape.735
  96.9 10.1 %slice.575 = bf16[8736,512]{1,0:T(8,128)(2,1)} reshape(bf16[128,273,128]{2,1,0:T(8,128)(2,1)} %slice.730) | data formatting | bytes 17891328 | tf_op jit(solution)/shard_map/slice | solution.py:579
  107.0 14.7 %slice.609 = bf16[2184,2048]{1,0:T(8,128)(2,1)} reshape(bf16[128,273,128]{2,1,0:T(8,128)(2,1)} %slice.730) | data formatting | bytes 17891328 | tf_op jit(solution)/shard_map/slice | solution.py:579
  121.7 14.6 %slice.579 = bf16[4368,2,512]{2,1,0:T(2,128)(2,1)} reshape(bf16[128,273,128]{2,1,0:T(8,128)(2,1)} %slice.730) | data formatting | bytes 17891328 | tf_op jit(solution)/shard_map/slice | solution.py:579
  142.8 16.8 %shard_map.164 = f32[8,128]{1,0:T(8,128)S(1)} custom-call(f32[8,128]{1,0:T(8,128)S(1)} %pad_maximum_fusion.6.x_ref), custom_call_target="tpu_custom_call" | custom-call | tf_op jit(solution)/shard_map/pallas_call | solution.py:113
  161.1 15.7 %shard_map.165 = bf16[16,48,512]{2,1,0:T(8,128)(2,1)S(1)} custom-call(bf16[8,16,512]{2,1,0:T(8,128)(2,1)S(1)} %bitcast.449), custom_call_target="tpu_custom_call" | custom-call | tf_op jit(solution)/shard_map/pallas_call | solution.py:400
  189.5 15.7 %shard_map.166 = f32[8,128]{1,0:T(8,128)S(1)} custom-call(f32[8,128]{1,0:T(8,128)S(1)} %pad_maximum_fusion.7.x_ref), custom_call_target="tpu_custom_call" | custom-call | tf_op jit(solution)/shard_map/pallas_call | solution.py:113
  205.8 2.1 fusion.135
  208.0 13.9 %shard_map.167 = f32[32,128]{1,0:T(8,128)S(1)} custom-call(f32[32,128]{1,0:T(8,128)S(1)} %pad_maximum_fusion.2.x_ref), custom_call_target="tpu_custom_call" | custom-call | tf_op jit(solution)/shard_map/pallas_call | solution.py:113
  224.1 8.1 %shard_map.168 = bf16[8,64,512]{2,1,0:T(8,128)(2,1)S(1)} custom-call(bf16[8,16,2048]{2,1,0:T(8,128)(2,1)S(1)} %bitcast.442), custom_call_target="tpu_custom_call" | custom-call | tf_op jit(solution)/shard_map/pallas_call | solution.py:400
  242.5 3.8 fusion.150
  252.1 29.2 %shard_map.169 = bf16[4,8,16,2304]{3,2,1,0:T(8,128)(2,1)S(1)} custom-call(bf16[8,64,2304]{2,1,0:T(8,128)(2,1)S(1)} %bitcast.441), custom_call_target="tpu_custom_call" | custom-call | tf_op jit(solution)/shard_map/pallas_call | solution.py:400
  285.1 10.5 %shard_map.170 = (bf16[8,16,256]{2,1,0:T(8,128)(2,1)S(1)}, bf16[8,16,256]{2,1,0:T(8,128)(2,1)S(1)}, bf16[8,16,256]{2,1,0:T(8,128)(2,1)S(1)}, bf16[8,16,256]{2,1,...) custom-call(bf16[8,16,256]{2,1,0:T(8,128)(2,1)S(1)} %get-tuple-element.116.refs_0_, ...), custom_call_target="tpu_custom_call" | custom-call | tf_op jit(solution)/shard_map/pallas_call | solution.py:400
  295.9 21.8 %shard_map.171 = f32[80,128]{1,0:T(8,128)S(1)} custom-call(f32[80,128]{1,0:T(8,128)S(1)} %maximum_bitcast_fusion.x_ref), custom_call_target="tpu_custom_call" | custom-call | tf_op jit(solution)/shard_map/pallas_call | solution.py:113
  321.4 13.6 %shard_map.172 = f32[8,128]{1,0:T(8,128)S(1)} custom-call(f32[8,128]{1,0:T(8,128)S(1)} %fusion.103.x_ref), custom_call_target="tpu_custom_call" | custom-call | tf_op jit(solution)/shard_map/pallas_call | solution.py:113
  345.5 12.6 %shard_map.173 = f32[8,128]{1,0:T(8,128)S(1)} custom-call(f32[8,128]{1,0:T(8,128)S(1)} %fusion.102.x_ref), custom_call_target="tpu_custom_call" | custom-call | tf_op jit(solution)/shard_map/pallas_call | solution.py:113
  364.0 12.5 %shard_map.174 = f32[24,128]{1,0:T(8,128)S(1)} custom-call(f32[24,128]{1,0:T(8,128)S(1)} %pad_maximum_fusion.4.x_ref), custom_call_target="tpu_custom_call" | custom-call | tf_op jit(solution)/shard_map/pallas_call | solution.py:113
  379.6 2.1 convolution_divide_fusion
  382.7 12.1 %shard_map.175 = (bf16[8,16,256]{2,1,0:T(8,128)(2,1)S(1)}, bf16[8,16,256]{2,1,0:T(8,128)(2,1)S(1)}, bf16[8,16,256]{2,1,0:T(8,128)(2,1)S(1)}, bf16[8,16,256]{2,1,...) custom-call(bf16[8,16,256]{2,1,0:T(8,128)(2,1)S(1)} %bitcast.447, ...), custom_call_target="tpu_custom_call" | custom-call | tf_op jit(solution)/shard_map/pallas_call | solution.py:400
  399.1 28.2 %shard_map.176 = bf16[8,64,2304]{2,1,0:T(8,128)(2,1)S(1)} custom-call(bf16[8,16,2304]{2,1,0:T(8,128)(2,1)S(1)} %constant_dynamic-update-slice_fusion.5.refs_0_), custom_call_target="tpu_custom_call" | custom-call | tf_op jit(solution)/shard_map/pallas_call | solution.py:400
  431.6 3.8 convolution_convert_fusion.5
  435.4 9.8 %shard_map.177 = bf16[8,16,2048]{2,1,0:T(8,128)(2,1)S(1)} custom-call(bf16[8,64,512]{2,1,0:T(8,128)(2,1)S(1)} %bitcast.451), custom_call_target="tpu_custom_call" | custom-call | tf_op jit(solution)/shard_map/pallas_call | solution.py:400
  445.3 2.3 fusion.134
  448.8 14.6 %shard_map.178 = f32[32,128]{1,0:T(8,128)S(1)} custom-call(f32[32,128]{1,0:T(8,128)S(1)} %pad_maximum_fusion.3.x_ref), custom_call_target="tpu_custom_call" | custom-call | tf_op jit(solution)/shard_map/pallas_call | solution.py:113
  463.8 3.7 fusion.138
  467.6 2.1 fusion.10
  469.7 6.2 bitcast_convert_fusion
  480.5 10.7 %dynamic-update-slice.3 = bf16[1383441]{0:T(1024)(128)(2,1)S(1)} dynamic-update-slice(bf16[1383441]{0:T(1024)(128)(2,1)S(1)} %dynamic-update-slice.2, bf16[327680]{0:T(1024)(128)(2,1)} %bitcast.488, s32[]{} %constant.135) | dynamic-update-slice | bytes 1310724
  492.0 2.1 pad.48
  494.1 3.8 concatenate.141
  498.1 11.6 %shard_map.179 = f32[8,128]{1,0:T(8,128)S(1)} custom-call(f32[8,128]{1,0:T(8,128)S(1)} %pad_maximum_fusion.8.x_ref), custom_call_target="tpu_custom_call" | custom-call | tf_op jit(solution)/shard_map/pallas_call | solution.py:113
  511.9 12.9 %shard_map.180 = bf16[16,48,512]{2,1,0:T(8,128)(2,1)S(1)} custom-call(bf16[8,16,512]{2,1,0:T(8,128)(2,1)S(1)} %bitcast.440), custom_call_target="tpu_custom_call" | custom-call | tf_op jit(solution)/shard_map/pallas_call | solution.py:400
  539.2 12.7 %shard_map.181 = f32[8,128]{1,0:T(8,128)S(1)} custom-call(f32[8,128]{1,0:T(8,128)S(1)} %pad_maximum_fusion.9.x_ref), custom_call_target="tpu_custom_call" | custom-call | tf_op jit(solution)/shard_map/pallas_call | solution.py:113
  554.1 2.1 fusion
  556.2 4.2 copy.48
  560.4 4.1 copy.59
  574.5 6.9 copy.60
  583.2 3.5 constant_dynamic-update-slice_fusion.21
  586.8 4.3 pad.47
  591.1 13.2 %concatenate.138 = bf16[2,4,4,2,2,273,128]{6,5,4,3,2,1,0:T(8,128)(2,1)} reshape(bf16[4472832]{0:T(1024)(128)(2,1)} %pad.47) | data formatting | bytes 17891328 | tf_op jit(solution)/shard_map/concatenate | solution.py:1025
  604.2 13.8 %maximum_maximum_fusion.p_ref = bf16[2,4,4,2,2,384,128]{6,5,4,3,2,1,0:T(8,128)(2,1)} fusion(bf16[2,4,4,2,2,85,128]{6,5,4,3,2,1,0:T(8,128)(2,1)S(1)} %concatenate.141, bf16[2,4,4,2,2,273,128]{6,5,4,3,2,1,0:T(8,128)(2,1)} %concatenate.138, bf16[384]{0:T(512)(128)(2,1)S(1)} %copy-done.77), kind=kLoop, calls=%fused_computation.1 | loop fusion | flops 37748736 | bytes 24314624 | tf_op jit(solution)/shard_map/concatenate | solution.py:1025
  618.0 71.7 %shard_map.182 = f32[384,128]{1,0:T(8,128)} custom-call(bf16[2,4,4,2,2,384,128]{6,5,4,3,2,1,0:T(8,128)(2,1)} %maximum_maximum_fusion.p_ref), custom_call_target="tpu_custom_call" | custom-call | tf_op jit(solution)/shard_map/pallas_call | solution.py:344
  689.8 3.4 convolution_add_fusion
  696.2 78.6 %reduce-scatter.2.cloned.1.call-done = bf16[512,216]{0,1:T(8,128)(2,1)} async-done(((bf16[512,6912]{0,1:T(8,128)(2,1)}), bf16[512,216]{0,1:T(8,128)(2,1)}) %reduce-scatter.2.cloned.1.call-update) | async-done | bytes 221200 | tf_op jit(solution)/shard_map/reduce_scatter | solution.py:935
  (461 shorter events, 120.2 us)
Async XLA Ops:
  7.2 235.3 %all-gather.2.cloned.1.call-start = ((), (), s32[]{:S(2)}) async-start(), calls=%async_computation.1 | async-start | bytes 7299072 | tf_op jit(solution)/shard_map/all_gather | solution.py:708
  9.0 765.8 %reduce-scatter.2.cloned.1.call-start = ((), (), s32[]{:S(2)}) async-start(), calls=%async_computation.2 | async-start | bytes 7299072 | tf_op jit(solution)/shard_map/reduce_scatter | solution.py:935
  121.6 19.1 %copy-start.12 = (bf16[8,16,2048]{2,1,0:T(8,128)(2,1)S(1)}, bf16[8,16,2048]{2,1,0:T(8,128)(2,1)}, u32[]{:S(2)}) copy-start(bf16[8,16,2048]{2,1,0:T(8,128)(2,1)} %param.12) | copy-start | bytes 1572868
  142.8 34.4 %copy-start.31 = (f32[512,128]{0,1:T(8,128)}, f32[512,128]{0,1:T(8,128)S(1)}, u32[]{:S(2)}) copy-start(f32[512,128]{0,1:T(8,128)S(1)} %get-tuple-element.175) | copy-start | bytes 786436
  159.7 17.5 %copy-start.48 = (f32[512]{0:T(512)}, f32[512]{0:T(512)S(1)}, u32[]{:S(2)}) copy-start(f32[512]{0:T(512)S(1)} %multiply_bitcast_fusion.4) | copy-start | bytes 6148
  160.4 16.8 %copy-start.50 = (f32[1,1,512]{2,1,0:T(1,128)}, f32[1,1,512]{2,1,0:T(1,128)S(1)}, u32[]{:S(2)}) copy-start(f32[1,1,512]{2,1,0:T(1,128)S(1)} %get-tuple-element.147) | copy-start | bytes 6148
  160.4 22.5 %copy-start.65 = (f32[1,1,512]{2,1,0:T(1,128)}, f32[1,1,512]{2,1,0:T(1,128)S(1)}, u32[]{:S(2)}) copy-start(f32[1,1,512]{2,1,0:T(1,128)S(1)} %get-tuple-element.146) | copy-start | bytes 6148
  160.4 45.4 %copy-start.58 = (f32[1,1,512]{2,1,0:T(1,128)}, f32[1,1,512]{2,1,0:T(1,128)S(1)}, u32[]{:S(2)}) copy-start(f32[1,1,512]{2,1,0:T(1,128)S(1)} %get-tuple-element.144) | copy-start | bytes 6148
  160.4 45.4 %copy-start.71 = (f32[1,1,512]{2,1,0:T(1,128)}, f32[1,1,512]{2,1,0:T(1,128)S(1)}, u32[]{:S(2)}) copy-start(f32[1,1,512]{2,1,0:T(1,128)S(1)} %get-tuple-element.145) | copy-start | bytes 6148
  161.0 16.2 %copy-start.46 = (f32[512]{0:T(512)}, f32[512]{0:T(512)S(1)}, u32[]{:S(2)}) copy-start(f32[512]{0:T(512)S(1)} %get-tuple-element.149) | copy-start | bytes 6148
  186.8 37.1 %copy-start.81 = (s32[8]{0:T(128)S(1)}, s32[8]{0:T(128)}, u32[]{:S(2)}) copy-start(s32[8]{0:T(128)} %param.13) | copy-start | bytes 100
  188.2 44.7 %copy-start.91 = (s32[3]{0:T(128)S(1)}, s32[3]{0:T(128)}, u32[]{:S(2)}) copy-start(s32[3]{0:T(128)} %param.17) | copy-start | bytes 40
  189.5 18.4 %copy-start.7 = (f32[128,512]{1,0:T(8,128)}, f32[128,512]{1,0:T(8,128)S(1)}, u32[]{:S(2)}) copy-start(f32[128,512]{1,0:T(8,128)S(1)} %get-tuple-element.176) | copy-start | bytes 786436
  205.2 17.5 %copy-start.55 = (f32[512]{0:T(512)}, f32[512]{0:T(512)S(1)}, u32[]{:S(2)}) copy-start(f32[512]{0:T(512)S(1)} %multiply_bitcast_fusion.3) | copy-start | bytes 6148
  223.3 23.0 %copy-start.42 = (f32[1,2048]{1,0:T(1,128)}, f32[1,2048]{1,0:T(1,128)S(1)}, u32[]{:S(2)}) copy-start(f32[1,2048]{1,0:T(1,128)S(1)} %get-tuple-element.130) | copy-start | bytes 24580
  223.3 23.0 %copy-start.44 = (f32[1,2048]{1,0:T(1,128)}, f32[1,2048]{1,0:T(1,128)S(1)}, u32[]{:S(2)}) copy-start(f32[1,2048]{1,0:T(1,128)S(1)} %get-tuple-element.131) | copy-start | bytes 24580
  282.6 35.2 %copy-start.86 = (f32[4]{0:T(128)S(1)}, f32[4]{0:T(128)}, u32[]{:S(2)}) copy-start(f32[4]{0:T(128)} %broadcast_multiply_fusion.2) | copy-start | bytes 52
  282.6 35.3 %copy-start.85 = (f32[256]{0:T(256)S(1)}, f32[256]{0:T(256)}, u32[]{:S(2)}) copy-start(f32[256]{0:T(256)} %slice_convert_fusion.4) | copy-start | bytes 3076
  282.6 36.8 %copy-start.82 = (s32[8]{0:T(128)S(1)}, s32[8]{0:T(128)}, u32[]{:S(2)}) copy-start(s32[8]{0:T(128)} %param.13) | copy-start | bytes 100
  284.7 50.2 %copy-start.63 = (f32[1,1,256]{2,1,0:T(1,128)S(1)}, f32[1,1,256]{2,1,0:T(1,128)}, u32[]{:S(2)}) copy-start(f32[1,1,256]{2,1,0:T(1,128)} %get-tuple-element.142) | copy-start | bytes 3076
  284.7 50.3 %copy-start.78 = (f32[1,1,256]{2,1,0:T(1,128)S(1)}, f32[1,1,256]{2,1,0:T(1,128)}, u32[]{:S(2)}) copy-start(f32[1,1,256]{2,1,0:T(1,128)} %get-tuple-element.143) | copy-start | bytes 3076
  285.0 50.0 %copy-start.38 = (bf16[256,17]{1,0:T(8,128)(2,1)S(1)}, bf16[256,17]{1,0:T(8,128)(2,1)}, u32[]{:S(2)}) copy-start(bf16[256,17]{1,0:T(8,128)(2,1)} %reshape.739) | copy-start | bytes 26116
  285.0 50.0 %copy-start.94 = (f32[17]{0:T(128)S(1)}, f32[17]{0:T(128)}, u32[]{:S(2)}) copy-start(f32[17]{0:T(128)} %slice_convert_fusion.3) | copy-start | bytes 208
  285.0 50.3 %copy-start.84 = (f32[128,1]{0,1:T(1,128)S(1)}, f32[128,1]{0,1:T(1,128)}, u32[]{:S(2)}) copy-start(f32[128,1]{0,1:T(1,128)} %convert_element_type.301) | copy-start | bytes 1540
  285.0 50.9 %copy-start.74 = (s32[128]{0:T(128)S(1)}, s32[128]{0:T(128)}, u32[]{:S(2)}) copy-start(s32[128]{0:T(128)} %eq.99) | copy-start | bytes 1540
  285.1 52.1 %copy-start.73 = (s32[128]{0:T(128)S(1)}, s32[128]{0:T(128)}, u32[]{:S(2)}) copy-start(s32[128]{0:T(128)} %eq.95) | copy-start | bytes 1540
  285.1 54.9 %copy-start.88 = (f32[128]{0:T(128)S(1)}, f32[128]{0:T(128)}, u32[]{:S(2)}) copy-start(f32[128]{0:T(128)} %convert_element_type.299) | copy-start | bytes 1540
  317.9 60.0 %copy-start.36 = (f32[4,2048]{1,0:T(4,128)}, f32[4,2048]{1,0:T(4,128)S(1)}, u32[]{:S(2)}) copy-start(f32[4,2048]{1,0:T(4,128)S(1)} %broadcast_divide_fusion) | copy-start | bytes 98308
  319.4 44.0 %copy-start.60 = (f32[4,256]{1,0:T(4,128)}, f32[4,256]{1,0:T(4,128)S(1)}, u32[]{:S(2)}) copy-start(f32[4,256]{1,0:T(4,128)S(1)} %convolution_add_fusion.19) | copy-start | bytes 12292
  361.4 18.2 %copy-start.87 = (f32[4]{0:T(128)S(1)}, f32[4]{0:T(128)}, u32[]{:S(2)}) copy-start(f32[4]{0:T(128)} %broadcast_multiply_fusion.2) | copy-start | bytes 52
  445.3 18.2 %copy-start.41 = (f32[1,2048]{1,0:T(1,128)S(1)}, f32[1,2048]{1,0:T(1,128)}, u32[]{:S(2)}) copy-start(f32[1,2048]{1,0:T(1,128)} %get-tuple-element.129) | copy-start | bytes 24580
  445.3 18.5 %copy-start.8 = (f32[128,512]{1,0:T(8,128)S(1)}, f32[128,512]{1,0:T(8,128)}, u32[]{:S(2)}) copy-start(f32[128,512]{1,0:T(8,128)} %copy-done.7) | copy-start | bytes 786436
  445.3 18.5 %copy-start.53 = (f32[512]{0:T(512)S(1)}, f32[512]{0:T(512)}, u32[]{:S(2)}) copy-start(f32[512]{0:T(512)} %copy-done.52) | copy-start | bytes 6148
  445.3 18.5 %copy-start.56 = (f32[512]{0:T(512)S(1)}, f32[512]{0:T(512)}, u32[]{:S(2)}) copy-start(f32[512]{0:T(512)} %copy-done.55) | copy-start | bytes 6148
  445.3 18.5 %copy-start.59 = (f32[1,1,512]{2,1,0:T(1,128)S(1)}, f32[1,1,512]{2,1,0:T(1,128)}, u32[]{:S(2)}) copy-start(f32[1,1,512]{2,1,0:T(1,128)} %copy-done.58) | copy-start | bytes 6148
  445.3 18.5 %copy-start.72 = (f32[1,1,512]{2,1,0:T(1,128)S(1)}, f32[1,1,512]{2,1,0:T(1,128)}, u32[]{:S(2)}) copy-start(f32[1,1,512]{2,1,0:T(1,128)} %copy-done.71) | copy-start | bytes 6148
  491.9 17.8 %copy-start.9 = (f32[128,512]{1,0:T(8,128)S(1)}, f32[128,512]{1,0:T(8,128)}, u32[]{:S(2)}) copy-start(f32[128,512]{1,0:T(8,128)} %copy-done.7) | copy-start | bytes 786436
  492.0 17.8 %copy-start.54 = (f32[512]{0:T(512)S(1)}, f32[512]{0:T(512)}, u32[]{:S(2)}) copy-start(f32[512]{0:T(512)} %copy-done.52) | copy-start | bytes 6148
  492.0 17.8 %copy-start.57 = (f32[512]{0:T(512)S(1)}, f32[512]{0:T(512)}, u32[]{:S(2)}) copy-start(f32[512]{0:T(512)} %copy-done.55) | copy-start | bytes 6148
  492.0 18.8 %copy-start.34 = (bf16[8,16,512]{2,1,0:T(8,128)(2,1)S(1)}, bf16[8,16,512]{2,1,0:T(8,128)(2,1)}, u32[]{:S(2)}) copy-start(bf16[8,16,512]{2,1,0:T(8,128)(2,1)} %copy-done.33) | copy-start | bytes 393220
  529.3 22.7 %copy-start = (bf16[64,16,8,128]{3,2,1,0:T(8,128)(2,1)S(1)}, bf16[64,16,8,128]{3,2,1,0:T(8,128)(2,1)}, u32[]{:S(2)}) copy-start(bf16[64,16,8,128]{3,2,1,0:T(8,128)(2,1)} %fusion.10) | copy-start | bytes 6291460
  534.9 19.1 %copy-start.64 = (f32[512]{0:T(512)S(1)}, f32[512]{0:T(512)}, u32[]{:S(2)}) copy-start(f32[512]{0:T(512)} %get-tuple-element.148) | copy-start | bytes 6148
  534.9 19.2 %copy-start.14 = (bf16[8,16,2048]{2,1,0:T(8,128)(2,1)S(1)}, bf16[8,16,2048]{2,1,0:T(8,128)(2,1)}, u32[]{:S(2)}) copy-start(bf16[8,16,2048]{2,1,0:T(8,128)(2,1)} %param.12) | copy-start | bytes 1572868
  618.0 71.7 %copy-start.5 = (f32[128,2048]{1,0:T(8,128)S(1)}, f32[128,2048]{1,0:T(8,128)}, u32[]{:S(2)}) copy-start(f32[128,2048]{1,0:T(8,128)} %copy-done.4) | copy-start | bytes 3145732
  618.0 71.7 %copy-start.29 = (bf16[128,512]{1,0:T(8,128)(2,1)S(1)}, bf16[128,512]{1,0:T(8,128)(2,1)}, u32[]{:S(2)}) copy-start(bf16[128,512]{1,0:T(8,128)(2,1)} %copy-done.28) | copy-start | bytes 393220
  618.0 75.2 %copy-start.40 = (f32[10880]{0:T(1024)S(1)}, f32[10880]{0:T(1024)}, u32[]{:S(2)}) copy-start(f32[10880]{0:T(1024)} %param.21) | copy-start | bytes 130564
  618.0 76.6 %copy-start.37 = (f32[34944]{0:T(1024)S(1)}, f32[34944]{0:T(1024)}, u32[]{:S(2)}) copy-start(f32[34944]{0:T(1024)} %param.19) | copy-start | bytes 419332
  689.8 85.0 %copy-start.35 = (f32[512,216]{0,1:T(8,128)S(1)}, f32[512,216]{0,1:T(8,128)}, u32[]{:S(2)}) copy-start(f32[512,216]{0,1:T(8,128)} %param.23) | copy-start | bytes 1327108
  (51 other events, 445.3 us)
Sparse Core Ops, SparseCore 0:
  10.2 186.0 all-gather.1
  581.5 193.1 reduce-scatter.1

commit v2 on v0

v2 whole, which is shorter than its diff:
```python
import functools
import math

import jax
import jax.numpy as jnp
from jax import lax
from jax.experimental import pallas as pl
from jax.experimental.pallas import tpu as pltpu
from jax.sharding import PartitionSpec as P

MESH = pl.DeviceIdType.MESH
ANY = pl.BlockSpec(memory_space=pl.ANY)
VMEM = pl.BlockSpec(memory_space=pltpu.VMEM)
SMEM = pl.BlockSpec(memory_space=pltpu.SMEM)
BLOCK_ROWS = 273
HEAD_ROWS = 85
PAYLOAD = 384

CIN = 2048
MID = 512
ASPP = 256
SEG = 13
PART = 3
HEADS = 17


EPSILON = 1e-05
MOMENTUM_KEEP = 0.5
rate_list = (6, 12, 18)
block_dilation = 4
widest_margin = 18


def device_of(row, col):
    return {"rows": row, "cols": col}


def split_place():
    row, col = lax.axis_index("rows"), lax.axis_index("cols")
    return {
        "y": (row // 16) + 2 * (col // 2),
        "x": lax.rem(row // 4, 4),
        "z": lax.rem(row, 4),
        "core": lax.rem(col, 2),
    }


def device_at(place):
    row = lax.rem(place["y"], 2) * 16 + place["x"] * 4 + place["z"]
    return device_of(row, (place["y"] // 2) * 2 + place["core"])


def moved(place, axis, step, extent=4):
    other = dict(place)
    other[axis] = lax.rem(place[axis] + step + extent, extent)
    return other


def meet(sources, targets):
    barrier = pltpu.get_barrier_semaphore()
    for device in sources:
        pl.semaphore_signal(barrier, inc=1, device_id=device, device_id_type=MESH)
    pl.semaphore_wait(barrier, targets)


def remote(source, target, send_sem, recv_sem, device):
    return pltpu.make_async_remote_copy(
        src_ref=source,
        dst_ref=target,
        send_sem=send_sem,
        recv_sem=recv_sem,
        device_id=device,
        device_id_type=MESH,
    )


GATHER_ORDERS = (("z", "x", "y"), ("x", "y", "z"), ("y", "z", "x"))


def axis_view(place, fixed):
    index = [slice(None)] * 4
    if "y" in fixed:
        index[0], index[3] = lax.rem(place["y"], 2), place["y"] // 2
    if "x" in fixed:
        index[1] = place["x"]
    if "z" in fixed:
        index[2] = place["z"]
    return tuple(index)


def scatter_kernel(p_ref, o_ref, held, *rest):
    relays = rest[0:3]
    parts = [rest[3 + 3 * third : 6 + 3 * third] for third in range(3)]
    sums = [rest[12 + 2 * third : 14 + 2 * third] for third in range(3)]
    links = Links(rest[-2], rest[-1])
    first, own_first = links.take(45), links.take(3)
    me = split_place()
    everywhere = (slice(None),) * 4
    own_copies = []
    for third in range(3):
        rows = pl.ds(third * 128, 128)
        own_copies.append(
            pltpu.make_async_copy(
                p_ref.at[everywhere + (rows,)],
                held.at[everywhere + (rows,)],
                links.sends.at[own_first + third],
            )
        )
        own_copies[third].start()
    partners = [moved(me, axis, step) for axis in "xyz" for step in (1, 2, 3)]
    meet([device_at(place) for place in partners], 9)

    def view_of(third, phase, place, part=None):
        order = GATHER_ORDERS[third]
        axis = order[2 - phase]
        start, size = (0, 128) if part is None else (64 * part, 64)
        if phase == 0:
            return held.at[axis_view(place, [axis]) + (pl.ds(third * 128 + start, size),)]
        index = []
        for name, key in (("y", 0), ("x", 1), ("z", 2), ("y", 3)):
            if name not in order[: 3 - phase]:
                continue
            if name != axis:
                index.append(slice(None))
            elif name == "y":
                index.append(lax.rem(place["y"], 2) if key == 0 else place["y"] // 2)
            else:
                index.append(place[name])
        return sums[third][phase - 1].at[tuple(index) + (pl.ds(start, size),)]

    def link(third, phase, kind, step, outgoing, incoming):
        number = first + 15 * third + 5 * phase + (3 + step // 2 if kind else step - 1)
        return remote(
            outgoing,
            incoming,
            links.sends.at[number],
            links.recvs.at[number],
            device_at(moved(me, GATHER_ORDERS[third][2 - phase], step)),
        )

    def steps(phase):
        return (1, 2, 3) if phase else (1, 3)

    def relay(third, step):
        axis = GATHER_ORDERS[third][2]
        outgoing = view_of(third, 0, moved(me, axis, 2), step // 2)
        return link(third, 0, 1, step, outgoing, relays[third].at[step // 2])

    def copy(third, phase, step):
        axis = GATHER_ORDERS[third][2 - phase]
        outgoing = view_of(third, phase, moved(me, axis, step))
        slot = steps(phase).index(step)
        return link(third, phase, 0, step, outgoing, parts[third][phase].at[slot])

    for third in range(3):
        own_copies[third].wait()
        for step in (1, 3):
            relay(third, step).start()
    for third in range(3):
        axis = GATHER_ORDERS[third][2]
        for step in (1, 3):
            relay(third, step).wait_recv()
            view = view_of(third, 0, moved(me, axis, step), step // 2)
            view[...] = view[...] + relays[third][step // 2]
            copy(third, 0, step).start()
    for phase in range(1, 4):
        for third in range(3):
            total = view_of(third, phase - 1, me)[...].astype(jnp.float32)
            for slot, step in enumerate(steps(phase - 1)):
                copy(third, phase - 1, step).wait_recv()
                total = total + parts[third][phase - 1][slot].astype(jnp.float32)
            if phase == 3:
                o_ref[128 * third : 128 * third + 128] = total
            else:
                sums[third][phase - 1][...] = total.astype(jnp.bfloat16)
                for step in steps(phase):
                    copy(third, phase, step).start()
    for third in range(3):
        for step in (1, 3):
            relay(third, step).wait_send()
        for phase in range(3):
            for step in steps(phase):
                copy(third, phase, step).wait_send()


def scatter_params(packed, collective):
    def shape_left(left, rows):
        shape = ()
        for name, number in (("y", 2), ("x", 4), ("z", 4), ("y", 2)):
            if name in left:
                shape += (number,)
        return shape + (rows, 128)

    relays = []
    parts = []
    sums = []
    for order in GATHER_ORDERS:
        relays.append(pltpu.VMEM((2,) + shape_left(order[:2], 64), jnp.bfloat16))
        for phase in range(3):
            number = 3 if phase else 2
            parts.append(pltpu.VMEM((number,) + shape_left(order[: 2 - phase], 128), jnp.bfloat16))
        for phase in range(2):
            sums.append(pltpu.VMEM(shape_left(order[: 2 - phase], 128), jnp.bfloat16))
    half = (2, 4, 4, 2, PAYLOAD, 128)
    return pl.pallas_call(
        scatter_kernel,
        out_shape=jax.ShapeDtypeStruct((PAYLOAD, 128), jnp.float32),
        in_specs=[ANY],
        out_specs=VMEM,
        scratch_shapes=[pltpu.VMEM(half, jnp.bfloat16)]
        + relays
        + parts
        + sums
        + [pltpu.SemaphoreType.DMA((51,)), pltpu.SemaphoreType.DMA((51,))],
        compiler_params=pltpu.CompilerParams(
            collective_id=collective, has_side_effects=True, vmem_limit_bytes=56 * MEGABYTE
        ),
    )(packed)


def neighbour(row, col, offset):
    return lax.rem(row + offset[0] + 32, 32), lax.rem(col + offset[1] + 4, 4)


MEGABYTE = 1024 * 1024
OFFSETS = (-4, 4, -6, 6, -12, 12, -18, 18)
ID_ROW = 368
RATE_ROWS = 224


class Links:
    def __init__(self, sends, recvs):
        self.sends, self.recvs = sends, recvs
        self.cursor = 0

    def take(self, number):
        first = self.cursor
        self.cursor = first + number
        return first


class Total:
    def __init__(self, links, value, near, far):
        self.links, self.value, self.near, self.far = links, value, near, far
        self.first = links.take(24)
        self.row, self.col = lax.axis_index("rows"), lax.axis_index("cols")
        self.near_me = (self.row // 16) * 4 + self.col
        self.far_me = lax.rem(self.row, 16)

    def near_device(self, index):
        return device_of((index // 4) * 16 + self.far_me, lax.rem(index, 4))

    def far_device(self, index):
        return device_of((self.row // 16) * 16 + index, self.col)

    def copy(self, far, step, slot):
        buffer, me, size = (self.far, self.far_me, 16) if far else (self.near, self.near_me, 8)
        base = self.first + (8 if far else 0)
        target = lax.rem(me + step, size)
        return remote(
            self.value,
            buffer.at[slot],
            self.links.sends.at[base + step],
            self.links.recvs.at[base + slot],
            self.far_device(target) if far else self.near_device(target),
        )

    def send(self, far):
        buffer, me, size = (self.far, self.far_me, 16) if far else (self.near, self.near_me, 8)
        for step in range(1, size):
            self.copy(far, step, me).start()
        buffer[me] = self.value[...]

    def collect(self, far):
        buffer, me, size = (self.far, self.far_me, 16) if far else (self.near, self.near_me, 8)
        for step in range(1, size):
            self.copy(far, step, lax.rem(me + step, size)).wait_recv()
        for step in range(1, size):
            self.copy(far, step, me).wait_send()
        total = buffer[0]
        for index in range(1, size):
            total = total + buffer[index]
        self.value[...] = total

    def start(self, value):
        self.value[...] = value
        self.send(False)

    def middle(self):
        self.collect(False)
        self.send(True)

    def finish(self):
        self.collect(True)
        return self.value[...]


def total_scratch(rows, columns):
    return [
        pltpu.VMEM((rows, columns), jnp.float32),
        pltpu.VMEM((8, rows, columns), jnp.float32),
        pltpu.VMEM((16, rows, columns), jnp.float32),
    ]


def total_peers():
    row, col = lax.axis_index("rows"), lax.axis_index("cols")
    near_me, far_me = (row // 16) * 4 + col, lax.rem(row, 16)
    peers = []
    for step in range(1, 8):
        index = lax.rem(near_me + step, 8)
        peers.append(device_of((index // 4) * 16 + far_me, lax.rem(index, 4)))
    for step in range(1, 16):
        peers.append(device_of((row // 16) * 16 + lax.rem(far_me + step, 16), col))
    return peers


def halo_peers():
    row, col = lax.axis_index("rows"), lax.axis_index("cols")
    return [
        device_of(*neighbour(row, col, (row_step, col_step)))
        for row_step in (-1, 0, 1)
        for col_step in (-1, 0, 1)
        if (row_step, col_step) != (0, 0)
    ]


class Halo:
    def __init__(self, links, source, window):
        self.links, self.source, self.window = links, source, window
        self.first = links.take(9)

    def copies(self, own_side):
        row, col = lax.axis_index("rows"), lax.axis_index("cols")
        listed = []
        for row_step in (-1, 0, 1):
            for col_step in (-1, 0, 1):
                if (row_step, col_step) == (0, 0):
                    continue
                low, size, top = {-1: (0, 4, 12), 0: (0, 8, 4), 1: (4, 4, 0)}[row_step]
                left = {-1: 32, 0: 16, 1: 0}[col_step]
                number = self.first + 3 * (row_step + 1) + col_step + 1
                listed.append(
                    remote(
                        self.source.at[pl.ds(low, size)],
                        self.window.at[pl.ds(top, size), pl.ds(left, 16)],
                        self.links.sends.at[number],
                        self.links.recvs.at[number],
                        device_of(*neighbour(row, col, (row_step, col_step))),
                    )
                )
        return listed

    def start(self):
        for copy in self.copies(True):
            copy.start()
        self.window[4:12, 16:32] = self.source[...]

    def finish(self):
        for copy in self.copies(False):
            copy.wait_recv()
        for copy in self.copies(False):
            copy.wait_send()


def widen_window(window, wide):
    col = lax.axis_index("cols")
    left = jnp.where(col > 0, 1.0, 0.0)
    right = jnp.where(col < 3, 1.0, 0.0)
    wide[:, 0:16] = window[:, 0:16].astype(jnp.float32) * left
    wide[:, 16:32] = window[:, 16:32].astype(jnp.float32)
    wide[:, 32:48] = window[:, 32:48].astype(jnp.float32) * right


def pixel_mask(mask):
    return jnp.broadcast_to(mask[:, None, :], (8, 16, 128)).reshape(128, 128)


def across_lanes(mask, width):
    return jnp.concatenate([mask] * (width // 128), axis=1)


class Gather:
    def __init__(self, links, source, target):
        self.links, self.source, self.target = links, source, target
        self.first = links.take(45)
        self.core_first = links.take(12)
        self.me = split_place()
        self.twin = moved(self.me, "core", 1, 2)

    def block(self, place, third, free, part=None):
        fixed = [axis for axis in "xyz" if axis not in free]
        rows = pl.ds(third * 128, 128) if part is None else pl.ds(third * 128 + 64 * part, 64)
        return self.target.at[axis_view(place, fixed) + (place["core"], rows)]

    def link(self, third, phase, kind, step, outgoing, incoming):
        number = self.first + 15 * third + 5 * phase + (3 + step // 2 if kind else step - 1)
        return remote(
            outgoing,
            incoming,
            self.links.sends.at[number],
            self.links.recvs.at[number],
            device_at(moved(self.me, GATHER_ORDERS[third][phase], step)),
        )

    def copy(self, third, phase, step, sender):
        free = GATHER_ORDERS[third][:phase]
        if phase == 0:
            outgoing = self.source.at[pl.ds(third * 128, 128)]
        else:
            outgoing = self.block(self.me, third, free)
        return self.link(third, phase, 0, step, outgoing, self.block(sender, third, free))

    def relay(self, third, phase, step, sender):
        order = GATHER_ORDERS[third]
        view = self.block(moved(sender, order[phase], 4 - step), third, order[:phase], step // 2)
        return self.link(third, phase, 1, step, view, view)

    def core_copy(self, third, distance, sender):
        order = GATHER_ORDERS[third]
        view = self.block(moved(sender, order[2], distance), third, order[:2])
        number = self.core_first + 4 * third + distance
        return remote(
            view, view, self.links.sends.at[number], self.links.recvs.at[number], device_at(self.twin)
        )

    def behind(self, third, phase, step):
        return moved(self.me, GATHER_ORDERS[third][phase], 4 - step)

    def steps(self, phase):
        return (1, 3) if phase == 2 else (1, 2, 3)

    def run(self):
        me = self.me
        for phase in range(3):
            for third in range(3):
                if phase > 0:
                    for step in (1, 2, 3):
                        self.copy(third, phase - 1, step, self.behind(third, phase - 1, step)).wait_recv()
                for step in self.steps(phase):
                    self.copy(third, phase, step, me).start()
                if phase == 0:
                    self.block(me, third, ())[...] = self.source[pl.ds(third * 128, 128)]
                if phase == 2:
                    self.core_copy(third, 0, me).start()
        for third in range(3):
            for step in (1, 3):
                self.copy(third, 2, step, self.behind(third, 2, step)).wait_recv()
                self.relay(third, 2, step, me).start()
                self.core_copy(third, 4 - step, me).start()
        for third in range(3):
            for step in (1, 3):
                self.relay(third, 2, step, self.behind(third, 2, step)).wait_recv()
            self.core_copy(third, 2, me).start()
        for third in range(3):
            for distance in range(4):
                self.core_copy(third, distance, self.twin).wait_recv()

    def close(self):
        for third in range(3):
            for phase in range(3):
                for step in self.steps(phase):
                    self.copy(third, phase, step, self.me).wait_send()
            for step in (1, 3):
                self.relay(third, 2, step, self.me).wait_send()
            for distance in range(4):
                self.core_copy(third, distance, self.me).wait_send()


RATE_ORDERS = (("x", "z"), ("z", "x"))


class RateGather:
    def __init__(self, links, source, target):
        self.links, self.source, self.target = links, source, target
        self.first = links.take(82)
        self.me = split_place()
        self.low_y = lax.rem(self.me["y"], 2)
        self.other = dict(self.me)
        self.other["y"] = self.me["y"] + 1 - 2 * self.low_y
        self.half = RATE_ROWS // 2

    def own(self):
        return pltpu.make_async_copy(
            self.source,
            self.target.at[self.low_y, self.me["x"], self.me["z"]],
            self.links.recvs.at[self.first + 81],
        )

    def pair(self, sender):
        return remote(
            self.source,
            self.target.at[lax.rem(sender["y"], 2), self.me["x"], self.me["z"]],
            self.links.sends.at[self.first + 80],
            self.links.recvs.at[self.first + 80],
            device_at(self.other),
        )

    def axis(self, half, unit):
        return RATE_ORDERS[half][0 if unit < 2 else 1]

    def piece(self, half, unit, place, part=None):
        near = RATE_ORDERS[half][0]
        low_y = lax.rem(self.low_y + (unit if unit < 2 else (unit - 2) // 4), 2)
        places = {"x": place["x"], "z": place["z"]}
        if unit >= 2:
            places[near] = lax.rem(places[near] + (unit - 2) % 4, 4)
        start, size = {None: (0, 112), 0: (0, 64), 1: (64, 48)}[part]
        return self.target.at[low_y, places["x"], places["z"], pl.ds(half * self.half + start, size)]

    def link(self, half, unit, kind, step, view):
        number = self.first + 8 * unit + 4 * half + 2 * kind + step // 2
        return remote(
            view,
            view,
            self.links.sends.at[number],
            self.links.recvs.at[number],
            device_at(moved(self.me, self.axis(half, unit), step)),
        )

    def copy(self, half, unit, step, sender):
        return self.link(half, unit, 0, step, self.piece(half, unit, sender))

    def relay(self, half, unit, step, sender):
        first = moved(sender, self.axis(half, unit), 4 - step)
        return self.link(half, unit, 1, step, self.piece(half, unit, first, step // 2))

    def behind(self, half, unit, step):
        return moved(self.me, self.axis(half, unit), 4 - step)

    def each(self):
        return [(half, step) for half in range(2) for step in (1, 3)]

    def begin(self):
        self.own().start()
        self.pair(self.me).start()

    def send(self, *units):
        for unit in units:
            if unit == 0:
                self.own().wait()
            if unit == 1:
                self.pair(self.other).wait_recv()
            for half, step in self.each():
                self.copy(half, unit, step, self.me).start()

    def forward(self, *units):
        for unit in units:
            for half, step in self.each():
                self.copy(half, unit, step, self.behind(half, unit, step)).wait_recv()
                self.relay(half, unit, step, self.me).start()

    def receive(self, *units):
        for unit in units:
            for half, step in self.each():
                self.relay(half, unit, step, self.behind(half, unit, step)).wait_recv()

    def close(self):
        self.pair(self.me).wait_send()
        for unit in range(10):
            for half, step in self.each():
                self.copy(half, unit, step, self.me).wait_send()
                self.relay(half, unit, step, self.me).wait_send()


def assemble(gathered, first_row_group, staging, wide, stride):
    parts = len(wide)
    count, offset = (BLOCK_ROWS, 0) if parts == 4 else (HEAD_ROWS, BLOCK_ROWS)

    def step(group, carry):
        low_y, x, z = first_row_group // 16, group // 4, lax.rem(group, 4)
        for column in range(4):
            area = staging[column]
            if parts == 4:
                area[0:288] = gathered[low_y, x, z, column // 2, column % 2, 0:288].astype(jnp.float32)
            else:
                area[0:96] = gathered[low_y, x, z, column // 2, column % 2, 272:368].astype(jnp.float32)
            skip = offset - (0 if parts == 4 else 272)
            for part in range(parts):
                begin = (part - column * count) % parts
                number = (count - begin + parts - 1) // parts
                row = (column * count + begin - part) // parts
                group_rows = 4 * count // parts
                target = group_rows * (group + stride) + row
                wide[part][pl.ds(target, number), :] = area[
                    pl.ds(skip + begin, number, stride=parts), :
                ]
        return carry

    lax.fori_loop(0, 16, step, 0)


def wide_rows(wide, first, number):
    return jnp.concatenate([part[pl.ds(first, number), :] for part in wide], axis=1)


def block_forward_kernel(
    x_ref,
    block_ref,
    head_ref,
    image_ref,
    rate_params_ref,
    reduce_ref,
    spatial_ref,
    expand_ref,
    point_ref,
    pool_ref,
    project_ref,
    misc_ref,
    norms_ref,
    masks_ref,
    first_ref,
    second_ref,
    third_ref,
    act_ref,
    window_ref,
    out_ref,
    slab_ref,
    rates_ref,
    gathered,
    s0,
    s1,
    s2,
    s3,
    w0,
    w1,
    w2,
    w3,
    h0,
    h1,
    ids,
    wide,
    act_map,
    payload_wide,
    payload_ref,
    rate_ref,
    *rest,
):
    staging, matrix, head = (s0, s1, s2, s3), (w0, w1, w2, w3), (h0, h1)
    links = Links(rest[-2], rest[-1])
    totals = [Total(links, *rest[3 * number : 3 * number + 3]) for number in range(3)]
    payload_wide[0:BLOCK_ROWS, :] = block_ref[...]
    payload_wide[BLOCK_ROWS : BLOCK_ROWS + HEAD_ROWS, :] = head_ref[...]
    payload_wide[BLOCK_ROWS + HEAD_ROWS : PAYLOAD, :] = jnp.zeros(
        (PAYLOAD - BLOCK_ROWS - HEAD_ROWS, 128), jnp.float32
    )
    for step in range(8):
        payload_wide[ID_ROW + step : ID_ROW + step + 1, :] = jnp.full(
            (1, 128), image_ref[step].astype(jnp.float32)
        )
    payload_ref[...] = payload_wide[...].astype(jnp.bfloat16)
    rate_ref[...] = jnp.concatenate(
        [rate_params_ref[...], jnp.zeros((RATE_ROWS - 216, 512), jnp.float32)], axis=0
    ).astype(jnp.bfloat16)
    gather = Gather(links, payload_ref, gathered)
    rates = RateGather(links, rate_ref, rates_ref)
    halo = Halo(links, act_map, window_ref)
    slab_first = links.take(3)
    row, col = lax.axis_index("rows"), lax.axis_index("cols")
    peers = total_peers() + halo_peers()
    meet(peers, len(peers))
    rates.begin()
    gather.run()
    rates.send(0, 2, 1)

    for step in range(-3, 4):
        other = lax.rem(row + step + 32, 32)
        rows_there = gathered[
            other // 16, lax.rem(other // 4, 4), lax.rem(other, 4), 0, 0, ID_ROW : ID_ROW + 16
        ].astype(jnp.float32)[0:8]
        inside = jnp.logical_and(row + step >= 0, row + step < 32)
        ids[8 * (step + 3) : 8 * (step + 3) + 8, :] = jnp.where(inside, rows_there, -1.0)
    own_ids = ids[24:32, :]
    for number, offset in enumerate(OFFSETS):
        masks_ref[number] = jnp.where(ids[24 + offset : 32 + offset, :] == own_ids, 1.0, 0.0)
    masks_ref[len(OFFSETS)] = own_ids

    assemble(gathered, 0, staging, matrix, 0)
    for step in range(8):
        reduce_ref[256 * step : 256 * step + 256] = wide_rows(matrix, 256 * step, 256).astype(jnp.bfloat16)
    first = jnp.dot(x_ref[...], reduce_ref[...], preferred_element_type=jnp.float32)
    totals[0].start(
        jnp.concatenate(
            [jnp.sum(first, axis=0, keepdims=True), jnp.sum(first * first, axis=0, keepdims=True)], axis=0
        )
    )
    for step in range(5):
        spatial_ref[464 * step : 464 * step + 464] = wide_rows(matrix, 2048 + 464 * step, 464).astype(
            jnp.bfloat16
        )
    totals[0].middle()
    assemble(gathered, 16, staging, matrix, 0)
    for step in range(13):
        spatial_ref[2320 + 176 * step : 2320 + 176 * step + 176] = wide_rows(
            matrix, 176 * step, 176
        ).astype(jnp.bfloat16)
    for part in range(4):
        expand_ref[:, 512 * part : 512 * part + 512] = jnp.concatenate(
            [array[pl.ds(2288 + part, 512, stride=4), :] for array in matrix], axis=1
        ).astype(jnp.bfloat16)
    norms_ref[...] = wide_rows(matrix, 4336, 16)

    def normal(total, values, gain, shift, kept):
        average = total[0:1] / 16384.0
        variance = total[1:2] / 16384.0 - average * average
        scale = lax.rsqrt(variance + EPSILON)
        centered = (values - average) * scale
        kept[0:128] = centered
        kept[128:136] = jnp.broadcast_to(scale, (8, scale.shape[1]))
        return centered * gain + shift

    def silu(values):
        return values * jax.nn.sigmoid(values)

    def stats(values):
        return jnp.concatenate(
            [jnp.sum(values, axis=0, keepdims=True), jnp.sum(values * values, axis=0, keepdims=True)], axis=0
        )

    normed = normal(totals[0].finish(), first, norms_ref[0:1], norms_ref[1:2], first_ref)
    act_map[...] = silu(normed).astype(jnp.bfloat16).reshape(8, 16, MID)
    halo.start()
    rates.forward(0, 2, 1)
    rates.receive(0)
    rates.send(3)
    halo.finish()
    widen_window(window_ref, wide)
    second = None
    for row_tap in range(3):
        part = None
        for col_tap in range(3):
            tap = 3 * row_tap + col_tap
            region = wide[4 * row_tap : 4 * row_tap + 8, 12 + 4 * col_tap : 28 + 4 * col_tap]
            product = jnp.dot(
                region.reshape(128, MID).astype(jnp.bfloat16),
                spatial_ref[512 * tap : 512 * tap + 512],
                preferred_element_type=jnp.float32,
            )
            part = product if part is None else part + product
        if row_tap != 1:
            part = part * across_lanes(pixel_mask(masks_ref[row_tap // 2]), MID)
        second = part if second is None else second + part
    totals[1].start(stats(second))
    assemble(gathered, 0, staging, head, 0)
    assemble(gathered, 16, staging, head, 16)
    totals[1].middle()
    for step in range(8):
        point_ref[256 * step : 256 * step + 256] = wide_rows(head, 256 * step, 256).astype(jnp.bfloat16)
        pool_ref[256 * step : 256 * step + 256] = wide_rows(head, 2048 + 256 * step, 256).astype(jnp.bfloat16)
    for step in range(5):
        project_ref[256 * step : 256 * step + 256] = wide_rows(head, 4097 + 256 * step, 256).astype(
            jnp.bfloat16
        )
    misc_ref[0:8] = wide_rows(head, 4096, 8)
    misc_ref[8:72] = wide_rows(head, 5376, 64)
    normed = normal(totals[1].finish(), second, norms_ref[2:3], norms_ref[3:4], second_ref)
    rates.forward(3)
    rates.receive(1)
    rates.send(4, 5)
    act_ref[...] = silu(normed).astype(jnp.bfloat16)
    third = jnp.dot(act_ref[...], expand_ref[...], preferred_element_type=jnp.float32)
    totals[2].start(stats(third))
    totals[2].middle()
    out_gain = jnp.concatenate([norms_ref[4 + part : 5 + part] for part in range(4)], axis=1)
    out_shift = jnp.concatenate([norms_ref[8 + part : 9 + part] for part in range(4)], axis=1)
    normed = normal(totals[2].finish(), third, out_gain, out_shift, third_ref)
    block_out = silu(normed + x_ref[...].astype(jnp.float32)).astype(jnp.bfloat16)
    out_ref[...] = block_out.reshape(8, 16, CIN)

    def slab_copy(step, sender):
        return remote(
            out_ref.at[:, :, pl.ds(pl.multiple_of(lax.rem(col + step, 4) * 512, 512), 512)],
            slab_ref.at[:, pl.ds(pl.multiple_of(sender * 16, 16), 16)],
            links.sends.at[slab_first + step - 1],
            links.recvs.at[slab_first + step - 1],
            device_of(row, lax.rem(col + step, 4)),
        )

    for step in (1, 2, 3):
        slab_copy(step, col).start()
    rates.forward(4, 5)
    rates.send(6, 7, 8, 9)
    slab_ref[:, pl.ds(pl.multiple_of(col * 16, 16), 16)] = out_ref[
        :, :, pl.ds(pl.multiple_of(col * 512, 512), 512)
    ]
    for step in (1, 2, 3):
        copy = slab_copy(step, lax.rem(col + 4 - step, 4))
        copy.wait_recv()
        copy.wait_send()
    rates.forward(6, 7, 8, 9)
    rates.receive(2, 3, 4, 5, 6, 7, 8, 9)
    rates.close()
    gather.close()


def block_forward(arrays, collective):
    bf16, f32 = jnp.bfloat16, jnp.float32
    outs = [
        ((CIN, MID), bf16),
        ((9 * MID, MID), bf16),
        ((MID, CIN), bf16),
        ((CIN, ASPP), bf16),
        ((CIN, ASPP), bf16),
        ((5 * ASPP, ASPP), bf16),
        ((72, ASPP), f32),
        ((16, MID), f32),
        ((9, 8, 128), f32),
        ((136, MID), f32),
        ((136, MID), f32),
        ((136, CIN), f32),
        ((128, MID), bf16),
        ((16, 48, MID), bf16),
        ((8, 16, CIN), bf16),
        ((8, 64, CIN // 4), bf16),
        ((2, 4, 4, RATE_ROWS, CIN // 4), bf16),
    ]
    scratch = [pltpu.VMEM((2, 4, 4, 2, 2, PAYLOAD, 128), bf16)]
    scratch += [pltpu.VMEM((288, 128), f32)] * 4
    scratch += [pltpu.VMEM((4368, 128), f32)] * 4
    scratch += [pltpu.VMEM((5440, 128), f32)] * 2
    scratch += [
        pltpu.VMEM((56, 128), f32),
        pltpu.VMEM((16, 48, MID), f32),
        pltpu.VMEM((8, 16, MID), bf16),
        pltpu.VMEM((PAYLOAD, 128), f32),
        pltpu.VMEM((PAYLOAD, 128), bf16),
        pltpu.VMEM((RATE_ROWS, 512), bf16),
    ]
    for rows, columns in ((2, MID), (2, MID), (2, CIN)):
        scratch += total_scratch(rows, columns)
    scratch += [pltpu.SemaphoreType.DMA((240,)), pltpu.SemaphoreType.DMA((240,))]
    return pl.pallas_call(
        block_forward_kernel,
        out_shape=[jax.ShapeDtypeStruct(shape, dtype) for shape, dtype in outs],
        in_specs=[VMEM, VMEM, VMEM, SMEM, VMEM],
        out_specs=[VMEM] * 16 + [ANY],
        scratch_shapes=scratch,
        compiler_params=pltpu.CompilerParams(
            collective_id=collective, has_side_effects=True, vmem_limit_bytes=60 * MEGABYTE
        ),
    )(*arrays)


class RatePieces:
    def __init__(self, links, units):
        self.links = links
        self.first = links.take(6 * units + 4)
        self.extra = self.first + 6 * units
        self.me = split_place()
        self.low_y = lax.rem(self.me["y"], 2)
        self.other = dict(self.me)
        self.other["y"] = self.me["y"] + 1 - 2 * self.low_y

    def rows(self, half):
        return pl.ds(half * (RATE_ROWS // 2), RATE_ROWS // 2)

    def piece(self, array, half, low_y, first_axis, second_axis):
        places = {RATE_ORDERS[half][0]: first_axis, RATE_ORDERS[half][1]: second_axis}
        return array.at[low_y, places["x"], places["z"], self.rows(half)]

    def remote(self, unit, half, step, outgoing, incoming, axis):
        number = self.first + 6 * unit + 3 * half + step - 1
        return remote(
            outgoing,
            incoming,
            self.links.sends.at[number],
            self.links.recvs.at[number],
            device_at(moved(self.me, axis, step)),
        )

    def each(self):
        return [(half, step) for half in range(2) for step in (1, 2, 3)]


class RateFirst(RatePieces):
    def __init__(self, links, pieces, parts, sums, low_y):
        super().__init__(links, 4)
        self.pieces, self.parts, self.sums, self.from_y = pieces, parts, sums, low_y

    def copy(self, unit, half, step):
        far = RATE_ORDERS[half][1]
        target = moved(self.me, far, step)
        outgoing = self.piece(self.pieces, half, self.from_y, unit, target[far])
        return self.remote(unit, half, step, outgoing, self.parts.at[half, unit, step - 1], far)

    def send(self, unit):
        for half, step in self.each():
            self.copy(unit, half, step).start()

    def collect(self, unit, own=None):
        for half in range(2):
            total = None
            if own is None:
                mine = self.piece(self.pieces, half, self.from_y, unit, self.me[RATE_ORDERS[half][1]])[...]
            else:
                mine = own[half, unit]
            total = mine.astype(jnp.float32)
            for step in (1, 2, 3):
                self.copy(unit, half, step).wait_recv()
                total = total + self.parts[half, unit, step - 1].astype(jnp.float32)
            self.sums[half, unit] = total.astype(jnp.bfloat16)
        for half, step in self.each():
            self.copy(unit, half, step).wait_send()


class RateScatter(RatePieces):
    def __init__(self, links, sums, parts, pair_sums, pair_parts, target):
        super().__init__(links, 2)
        self.sums, self.parts, self.target = sums, parts, target
        self.pair_sums, self.pair_parts = pair_sums, pair_parts

    def copy(self, low_y, half, step):
        near = RATE_ORDERS[half][0]
        target = moved(self.me, near, step)
        outgoing = self.sums[low_y].at[half, target[near]]
        return self.remote(low_y, half, step, outgoing, self.parts.at[half, low_y, step - 1], near)

    def pair(self):
        return remote(
            self.pair_sums.at[1 - self.low_y],
            self.pair_parts,
            self.links.sends.at[self.extra],
            self.links.recvs.at[self.extra],
            device_at(self.other),
        )

    def send(self, low_y):
        for half, step in self.each():
            self.copy(low_y, half, step).start()

    def collect(self, low_y):
        for half in range(2):
            total = self.sums[low_y][half, self.me[RATE_ORDERS[half][0]]].astype(jnp.float32)
            for step in (1, 2, 3):
                self.copy(low_y, half, step).wait_recv()
                total = total + self.parts[half, low_y, step - 1].astype(jnp.float32)
            self.pair_sums[low_y, half] = total.astype(jnp.bfloat16)

    def finish(self):
        self.pair().wait_recv()
        for half in range(2):
            rows = slice(half * (RATE_ROWS // 2), (half + 1) * (RATE_ROWS // 2))
            self.target[rows] = self.pair_sums[self.low_y, half].astype(jnp.float32) + self.pair_parts[
                half
            ].astype(jnp.float32)
        for low_y in range(2):
            for half, step in self.each():
                self.copy(low_y, half, step).wait_send()
        self.pair().wait_send()


def disassemble(packed, first_row_group, staging, wide, stride):
    parts = len(wide)
    core = lax.rem(lax.axis_index("cols"), 2)
    count = BLOCK_ROWS if parts == 4 else HEAD_ROWS
    low_y = first_row_group // 16

    def step(group, carry):
        x, z = group // 4, lax.rem(group, 4)
        for column in range(4):
            area = staging[column]
            here = (lax.rem(column + core, 2), low_y, x, z, column // 2)
            if parts == 4:
                skip = 0
                area[272:288] = packed[here + (slice(272, 288),)].astype(jnp.float32)
            else:
                skip = 1
                area[80:112] = jnp.zeros((32, 128), jnp.float32)
            for part in range(parts):
                begin = (part - column * count) % parts
                number = (count - begin + parts - 1) // parts
                row = (column * count + begin - part) // parts
                origin = (4 * count // parts) * (group + stride) + row
                area[pl.ds(skip + begin, number, stride=parts), :] = wide[part][
                    pl.ds(origin, number), :
                ]
            if parts == 4:
                packed[here + (slice(0, 288),)] = area[0:288].astype(jnp.bfloat16)
            else:
                packed[here + (slice(272, 384),)] = area[0:112].astype(jnp.bfloat16)
        return carry

    lax.fori_loop(0, 16, step, 0)


def deal(wide, first, values):
    number = values.shape[0]
    for part, array in enumerate(wide):
        array[first : first + number, :] = values[:, 128 * part : 128 * part + 128]


def against_rows(left, right):
    return lax.dot_general(left, right, (((1,), (1,)), ((), ())), preferred_element_type=jnp.float32)


def over_pixels(left, right):
    return lax.dot_general(left, right, (((0,), (0,)), ((), ())), preferred_element_type=jnp.float32)


def block_backward_kernel(
    x_ref,
    grad_ref,
    norms_ref,
    masks_ref,
    first_ref,
    second_ref,
    third_ref,
    act_ref,
    window_ref,
    reduce_hbm,
    spatial_hbm,
    expand_hbm,
    point_ref,
    pool_ref,
    project_ref,
    misc_ref,
    pieces_ref,
    out_ref,
    held_ref,
    share_ref,
    s0,
    s1,
    s2,
    s3,
    w0,
    w1,
    w2,
    w3,
    wide,
    act_map,
    window,
    packed,
    twin_part,
    reduce_ref,
    spatial_ref,
    expand_ref,
    free_sem,
    *rest,
):
    staging, matrix, head = (s0, s1, s2, s3), (w0, w1, w2, w3), (w0, w1)
    links = Links(rest[-2], rest[-1])
    totals = [Total(links, *rest[3 * number : 3 * number + 3]) for number in range(3)]
    own, first_parts, first_sums_here, second_parts, pair_sums, pair_parts = rest[9:15]
    rates = [
        RateFirst(links, pieces_ref, first_parts.at[low_y], first_sums_here.at[low_y], low_y)
        for low_y in range(2)
    ]
    scatter = RateScatter(
        links,
        (first_sums_here.at[0], first_sums_here.at[1]),
        second_parts,
        pair_sums,
        pair_parts,
        share_ref,
    )
    me = scatter.me
    twin = device_at(moved(me, "core", 1, 2))
    halo = Halo(links, act_map, window)
    load_first, own_first, twin_first, out_first = (links.take(number) for number in (3, 4, 2, 2))
    loads = [
        pltpu.make_async_copy(source, target, links.recvs.at[load_first + number])
        for number, (source, target) in enumerate(
            ((expand_hbm, expand_ref), (spatial_hbm, spatial_ref), (reduce_hbm, reduce_ref))
        )
    ]
    own_copies = []
    for low_y in range(2):
        for half in range(2):
            places = {RATE_ORDERS[half][0]: slice(None), RATE_ORDERS[half][1]: me[RATE_ORDERS[half][1]]}
            own_copies.append(
                pltpu.make_async_copy(
                    pieces_ref.at[low_y, places["x"], places["z"], scatter.rows(half)],
                    own.at[low_y, half],
                    links.recvs.at[own_first + 2 * low_y + half],
                )
            )
    for copy in loads + own_copies:
        copy.start()

    def twin_copy(low_y):
        return remote(
            packed.at[1, low_y],
            twin_part,
            links.sends.at[twin_first + low_y],
            links.recvs.at[twin_first + low_y],
            twin,
        )

    def out_copy(low_y):
        return pltpu.make_async_copy(
            packed.at[0, low_y], held_ref.at[low_y], links.sends.at[out_first + low_y]
        )

    def join_twin(low_y):
        twin_copy(low_y).wait_recv()

        def add_block(index, carry):
            place = (index // 8, lax.rem(index // 2, 4), lax.rem(index, 2))
            packed[(0, low_y) + place] = packed[(0, low_y) + place] + twin_part[place]
            return carry

        lax.fori_loop(0, 32, add_block, 0)
        out_copy(low_y).start()

    peers = total_peers() + halo_peers()
    meet(peers, len(peers))

    def slope(values):
        part = jax.nn.sigmoid(values)
        return part * (1.0 + values * (1.0 - part))

    def local_sums(grad, kept):
        return jnp.concatenate(
            [
                jnp.sum(grad, axis=0, keepdims=True),
                jnp.sum(grad * kept[0:128], axis=0, keepdims=True),
            ],
            axis=0,
        )

    def through_norm(total, grad, kept, gain):
        return (
            gain
            * kept[128:129]
            * (grad - total[0:1] / 16384.0 - kept[0:128] * (total[1:2] / 16384.0))
        ).astype(jnp.bfloat16)

    rates[0].send(0)
    out_gain = jnp.concatenate([norms_ref[4 + part : 5 + part] for part in range(4)], axis=1)
    out_shift = jnp.concatenate([norms_ref[8 + part : 9 + part] for part in range(4)], axis=1)
    residual = third_ref[0:128] * out_gain + out_shift + x_ref[...].astype(jnp.float32)
    out_ref[...] = grad_ref[...] * slope(residual)
    third_sums = local_sums(out_ref[...], third_ref)
    totals[0].start(third_sums)
    for step in range(4):
        deal(head, 512 * step, point_ref[512 * step : 512 * step + 512].astype(jnp.float32))
    deal(head, 2048, pool_ref[0:672].astype(jnp.float32))
    disassemble(packed, 0, staging, head, 0)
    totals[0].middle()
    for step in range(4):
        deal(head, 344 * step, pool_ref[672 + 344 * step : 1016 + 344 * step].astype(jnp.float32))
    deal(head, 1376, misc_ref[0:1])
    for step in range(5):
        deal(head, 1377 + 256 * step, project_ref[256 * step : 256 * step + 256].astype(jnp.float32))
    deal(head, 2657, misc_ref[1:64])
    disassemble(packed, 16, staging, head, 0)
    third_grad = through_norm(totals[0].finish(), out_ref[...], third_ref, out_gain)
    rates[0].send(1)
    loads[0].wait()
    second_gain, second_shift = norms_ref[2:3], norms_ref[3:4]
    second_norm = second_ref[0:128] * second_gain + second_shift
    second_back = against_rows(third_grad, expand_ref[...]) * slope(second_norm)
    second_sums = local_sums(second_back, second_ref)
    totals[1].start(second_sums)
    for part in range(4):
        product = over_pixels(act_ref[...], third_grad[:, 512 * part : 512 * part + 512])
        for number, array in enumerate(matrix):
            array[pl.ds(2288 + part, 512, stride=4), :] = product[:, 128 * number : 128 * number + 128]
    totals[1].middle()
    widen_window(window_ref, wide)
    second_grad = through_norm(totals[1].finish(), second_back, second_ref, second_gain)
    act_map[...] = second_grad.reshape(8, 16, MID)
    halo.start()
    rates[0].send(2)
    rates[0].send(3)

    def spatial_grad(tap):
        row_tap, col_tap = tap // 3, tap % 3
        region = wide[4 * row_tap : 4 * row_tap + 8, 12 + 4 * col_tap : 28 + 4 * col_tap].reshape(128, MID)
        if row_tap != 1:
            region = region * across_lanes(pixel_mask(masks_ref[row_tap // 2]), MID)
        return over_pixels(region.astype(jnp.bfloat16), second_grad)

    middle_tap = spatial_grad(4)
    deal(matrix, 0, middle_tap[272:512])
    for tap in range(5, 9):
        deal(matrix, 240 + 512 * (tap - 5), spatial_grad(tap))
    halo.finish()
    widen_window(window, wide)
    loads[1].wait()
    first_back = None
    for row_tap in range(3):
        part = None
        for col_tap in range(3):
            tap = 3 * row_tap + col_tap
            region = wide[
                8 - 4 * row_tap : 16 - 4 * row_tap, 20 - 4 * col_tap : 36 - 4 * col_tap
            ]
            product = against_rows(
                region.reshape(128, MID).astype(jnp.bfloat16), spatial_ref[512 * tap : 512 * tap + 512]
            )
            part = product if part is None else part + product
        if row_tap != 1:
            part = part * across_lanes(pixel_mask(masks_ref[1 - row_tap // 2]), MID)
        first_back = part if first_back is None else first_back + part
    first_gain, first_shift = norms_ref[0:1], norms_ref[1:2]
    first_back = first_back * slope(first_ref[0:128] * first_gain + first_shift)
    first_sums = local_sums(first_back, first_ref)
    totals[2].start(first_sums)
    deal(matrix, 4336, first_sums[1:2])
    deal(matrix, 4337, first_sums[0:1])
    deal(matrix, 4338, second_sums[1:2])
    deal(matrix, 4339, second_sums[0:1])
    for part in range(4):
        deal(matrix, 4340 + part, third_sums[1:2, 512 * part : 512 * part + 512])
        deal(matrix, 4344 + part, third_sums[0:1, 512 * part : 512 * part + 512])
    deal(matrix, 4348, jnp.zeros((20, MID), jnp.float32))
    disassemble(packed, 16, staging, matrix, 0)
    twin_copy(1).start()
    totals[2].middle()
    widen_window(window_ref, wide)
    for copy in own_copies:
        copy.wait()
    for unit in range(3):
        rates[0].collect(unit, own.at[0])
    deal(matrix, 4096, middle_tap[0:272])
    for tap in range(4):
        deal(matrix, 2048 + 512 * tap, spatial_grad(tap))
    first_total = totals[2].finish()
    for unit in range(4):
        rates[1].send(unit)
    rates[0].collect(3, own.at[0])
    scatter.send(0)
    join_twin(1)
    pl.semaphore_signal(free_sem, inc=1, device_id=twin, device_id_type=MESH)
    loads[2].wait()
    first_grad = through_norm(first_total, first_back, first_ref, first_gain)
    for part in range(4):
        rows = slice(512 * part, 512 * part + 512)
        deal(matrix, 512 * part, over_pixels(x_ref[:, rows], first_grad))
        out_ref[:, rows] = out_ref[:, rows] + against_rows(first_grad, reduce_ref[rows])
    disassemble(packed, 0, staging, matrix, 0)
    pl.semaphore_wait(free_sem, 1)
    twin_copy(0).start()
    for unit in range(4):
        rates[1].collect(unit, own.at[1])
    scatter.send(1)
    scatter.collect(0)
    join_twin(0)
    scatter.collect(1)
    scatter.pair().start()
    scatter.finish()
    for low_y in range(2):
        twin_copy(low_y).wait_send()
        out_copy(low_y).wait()


def block_backward(arrays, collective):
    bf16, f32 = jnp.bfloat16, jnp.float32
    half = RATE_ROWS // 2
    scratch = [pltpu.VMEM((384, 128), f32)] * 4
    scratch += [pltpu.VMEM((4368, 128), f32)] * 4
    scratch += [
        pltpu.VMEM((16, 48, MID), f32),
        pltpu.VMEM((8, 16, MID), bf16),
        pltpu.VMEM((16, 48, MID), bf16),
        pltpu.VMEM((2, 2, 4, 4, 2, PAYLOAD, 128), bf16),
        pltpu.VMEM((4, 4, 2, PAYLOAD, 128), bf16),
        pltpu.VMEM((CIN, MID), bf16),
        pltpu.VMEM((9 * MID, MID), bf16),
        pltpu.VMEM((MID, CIN), bf16),
        pltpu.SemaphoreType.REGULAR,
    ]
    for rows, columns in ((2, CIN), (2, MID), (2, MID)):
        scratch += total_scratch(rows, columns)
    scratch += [
        pltpu.VMEM((2, 2, 4, half, 512), bf16),
        pltpu.VMEM((2, 2, 4, 3, half, 512), bf16),
        pltpu.VMEM((2, 2, 4, half, 512), bf16),
        pltpu.VMEM((2, 2, 3, half, 512), bf16),
        pltpu.VMEM((2, 2, half, 512), bf16),
        pltpu.VMEM((2, half, 512), bf16),
    ]
    scratch += [pltpu.SemaphoreType.DMA((176,)), pltpu.SemaphoreType.DMA((176,))]
    outs = [
        ((128, CIN), f32),
        ((2, 4, 4, 2, PAYLOAD, 128), bf16),
        ((RATE_ROWS, 512), f32),
    ]
    return pl.pallas_call(
        block_backward_kernel,
        out_shape=[jax.ShapeDtypeStruct(shape, dtype) for shape, dtype in outs],
        in_specs=[VMEM] * 9 + [ANY] * 3 + [VMEM] * (len(arrays) - 13) + [ANY],
        out_specs=[VMEM, ANY, VMEM],
        scratch_shapes=scratch,
        compiler_params=pltpu.CompilerParams(
            collective_id=collective, has_side_effects=True, vmem_limit_bytes=62 * MEGABYTE
        ),
    )(*arrays)


def row_peers():
    row, col = lax.axis_index("rows"), lax.axis_index("cols")
    return [device_of(lax.rem(row + step + 32, 32), col) for step in (-3, -2, -1, 1, 2, 3)]


def row_moves():
    listed = []
    for branch, rate in enumerate(rate_list):
        for direction in range(2):
            for hop in range(4):
                lead = 8 * hop - rate if direction == 0 else rate - 8 * hop
                first, last = max(0, lead), min(8, lead + 8)
                if first < last:
                    sign = 1 if direction == 0 else -1
                    listed.append((branch, direction, sign * hop, first, first - lead, last - first))
    return listed


class RowShift:
    def __init__(self, links, sources, target):
        self.links, self.sources, self.target = links, sources, target
        self.moves = row_moves()
        self.first = links.take(len(self.moves))

    def copies(self, branch):
        row, col = lax.axis_index("rows"), lax.axis_index("cols")
        for number, (owner, direction, hop, first, top, size) in enumerate(self.moves):
            if owner == branch and hop:
                yield remote(
                    self.sources[branch][direction].at[pl.ds(first, size)],
                    self.target.at[branch, direction, pl.ds(top, size)],
                    self.links.sends.at[self.first + number],
                    self.links.recvs.at[self.first + number],
                    device_of(lax.rem(row + hop + 32, 32), col),
                )

    def start(self, branch):
        for copy in self.copies(branch):
            copy.start()
        for owner, direction, hop, first, top, size in self.moves:
            if owner == branch and hop == 0:
                self.target[branch, direction, top : top + size] = self.sources[branch][direction][
                    first : first + size
                ]

    def finish(self, branch):
        for copy in self.copies(branch):
            copy.wait_recv()
            copy.wait_send()


MARGIN = 24


def silu_value(values):
    return values * jax.nn.sigmoid(values)


def silu_grad(values):
    part = jax.nn.sigmoid(values)
    return part * (1.0 + values * (1.0 - part))


def two_sums(first, second):
    return jnp.concatenate(
        [jnp.sum(first, axis=0, keepdims=True), jnp.sum(second, axis=0, keepdims=True)], axis=0
    )


def centered_values(total, values):
    average = total[0:1] / 16384.0
    variance = total[1:2] / 16384.0 - average * average
    scale = lax.rsqrt(variance + EPSILON)
    return (values - average) * scale, scale


def norm_grad(total, grad, centered, scale, gain):
    return (
        gain * scale * (grad - total[0:1] / 16384.0 - centered * (total[1:2] / 16384.0))
    ).astype(jnp.bfloat16)


def pyramid_kernel(
    grid_ref,
    slab_ref,
    pieces_ref,
    point_ref,
    pool_ref,
    project_ref,
    misc_ref,
    heads_ref,
    bias_ref,
    masks_ref,
    seg_ref,
    edge_ref,
    part_ref,
    weights_ref,
    loss_out,
    pooled_out,
    grad_out,
    point_out,
    pool_out,
    project_out,
    heads_out,
    norms_out,
    pieces_out,
    kernels,
    padded,
    moved_maps,
    taps,
    core_part,
    high_out,
    high_part,
    tap_own,
    rows_out,
    rows_in,
    grads_own,
    grads_in,
    stack,
    grad_taps,
    back_out,
    back_in,
    *rest,
):
    bf16, f32 = jnp.bfloat16, jnp.float32
    links = Links(rest[-2], rest[-1])
    totals = [Total(links, *rest[3 * number : 3 * number + 3]) for number in range(5)]
    row, col = lax.axis_index("rows"), lax.axis_index("cols")
    core, high = lax.rem(col, 2), col // 2
    twin = device_of(row, col + 1 - 2 * core)
    far_twin = device_of(row, col + 2 - 4 * high)
    pieces_sem = links.take(1)
    tap_core, tap_high = links.take(6), links.take(3)
    stack_high, stack_core = links.take(3), links.take(6)
    back = links.take(3)
    forward_shift = RowShift(
        links, [[rows_out.at[branch, direction] for direction in range(2)] for branch in range(3)], rows_in
    )
    backward_shift = RowShift(
        links, [[grads_own.at[branch] for _ in range(2)] for branch in range(3)], grads_in
    )
    load = pltpu.make_async_copy(pieces_ref, pieces_out, links.recvs.at[pieces_sem])
    load.start()
    peers = total_peers() + row_peers()
    meet(peers, len(peers))

    members_low = [jnp.where(masks_ref[8] == float(image), 1.0, 0.0) for image in range(4)]
    row_sums = jnp.sum(grid_ref[...].astype(f32), axis=1)
    pieces = []
    for image in range(4):
        chosen = members_low[image]
        pieces.append(
            jnp.concatenate(
                [
                    jnp.sum(row_sums * across_lanes(chosen, CIN), axis=0, keepdims=True),
                    jnp.sum(chosen, axis=0, keepdims=True),
                ],
                axis=1,
            )
        )
    totals[4].start(jnp.concatenate(pieces, axis=0))

    def columns_of(place):
        return pl.ds(pl.multiple_of(place * 16, 16), 16)

    padded[:, 0:MARGIN] = jnp.zeros((8, MARGIN, 512), f32)
    padded[:, MARGIN + 64 :] = jnp.zeros((8, MARGIN, 512), f32)
    padded[:, MARGIN : MARGIN + 64] = slab_ref[...].astype(f32)
    for branch, rate in enumerate(rate_list):
        for side in range(2):
            start = MARGIN + (2 * side - 1) * rate
            moved_maps[2 * branch + side] = (
                padded[:, start : start + 64].reshape(512, 512).astype(bf16)
            )
    slab = slab_ref[...].reshape(512, 512)
    load.wait()

    def join(pair, carry):
        both = jnp.concatenate(
            [pieces_out[2 * pair, 0:216].astype(f32), pieces_out[2 * pair + 1, 0:216].astype(f32)], axis=0
        )
        kernels[pl.ds(pl.multiple_of(432 * pair, 16), 432)] = both.astype(bf16)
        return carry

    lax.fori_loop(0, 16, join, 0)

    def tap_core_copy(branch, place):
        return remote(
            taps.at[pl.ds(3 * branch, 3), :, columns_of(2 * place + 1 - core)],
            core_part.at[branch, place],
            links.sends.at[tap_core + 2 * branch + place],
            links.recvs.at[tap_core + 2 * branch + place],
            twin,
        )

    def tap_high_copy(branch):
        return remote(
            high_out.at[branch],
            high_part.at[branch],
            links.sends.at[tap_high + branch],
            links.recvs.at[tap_high + branch],
            far_twin,
        )

    def tap_meet(branch):
        for place in range(2):
            tap_core_copy(branch, place).wait_recv()
        away = taps[pl.ds(3 * branch, 3), :, columns_of(2 * (1 - high) + core)].astype(f32)
        high_out[branch] = (away + core_part[branch, 1 - high].astype(f32)).astype(bf16)
        tap_high_copy(branch).start()
        here = taps[pl.ds(3 * branch, 3), :, columns_of(col)].astype(f32)
        tap_own[branch] = here + core_part[branch, high].astype(f32)

    def tap_finish(branch):
        tap_high_copy(branch).wait_recv()
        tap_own[branch] = tap_own[branch] + high_part[branch].astype(f32)
        for direction in range(2):
            rows_out[branch, direction] = tap_own[branch, 2 * direction].astype(bf16)
        forward_shift.start(branch)

    for branch in range(3):
        result = None
        for col_tap in range(3):
            left = slab if col_tap == 1 else moved_maps[2 * branch + col_tap // 2]
            right = jnp.concatenate(
                [
                    kernels[(9 * branch + 3 * tap + col_tap) * 256 : (9 * branch + 3 * tap + col_tap + 1) * 256]
                    for tap in range(3)
                ],
                axis=0,
            )
            product = against_rows(left, right)
            result = product if result is None else result + product
        for tap in range(3):
            taps[3 * branch + tap] = result[:, 256 * tap : 256 * tap + 256].astype(bf16).reshape(8, 64, 256)
        for place in range(2):
            tap_core_copy(branch, place).start()
        if branch == 0:
            totals[4].middle()
        else:
            tap_meet(branch - 1)
    tap_meet(2)
    grid = grid_ref[...].reshape(128, CIN)
    branches = [jnp.dot(grid, point_ref[...], preferred_element_type=f32)]
    pooled_sums = totals[4].finish()
    area = jnp.concatenate([pooled_sums[:, CIN : CIN + 128]] * 16, axis=1) * 16.0
    pooled = pooled_sums[:, 0:CIN] / area
    pooled_out[...] = pooled
    pooled_low = jnp.concatenate([pooled, jnp.zeros((4, CIN), f32)], axis=0).astype(bf16)
    pool_pre = jnp.dot(pooled_low, pool_ref[...], preferred_element_type=f32)[0:4] + misc_ref[0:1]
    pool_act = silu_value(pool_pre)
    members = [across_lanes(pixel_mask(members_low[image]), ASPP) for image in range(4)]
    pool_map = members[0] * pool_act[0:1]
    for image in range(1, 4):
        pool_map = pool_map + members[image] * pool_act[image : image + 1]
    for branch in range(3):
        tap_finish(branch)
    for branch in range(3):
        forward_shift.finish(branch)
        value = tap_own[branch, 1].reshape(128, 256)
        for direction in range(2):
            mask = across_lanes(pixel_mask(masks_ref[2 + 2 * branch + direction]), ASPP)
            value = value + rows_in[branch, direction].astype(f32).reshape(128, 256) * mask
        branches.append(value)
    before = jnp.concatenate(branches, axis=1)
    totals[0].start(two_sums(before, before * before))
    totals[0].middle()
    gains = jnp.concatenate([misc_ref[9 + 2 * branch : 10 + 2 * branch] for branch in range(4)], axis=1)
    shifts = jnp.concatenate([misc_ref[10 + 2 * branch : 11 + 2 * branch] for branch in range(4)], axis=1)
    centered, scale = centered_values(totals[0].finish(), before)
    normed = centered * gains + shifts
    joined = jnp.concatenate([silu_value(normed).astype(bf16), pool_map.astype(bf16)], axis=1)
    projected = jnp.dot(joined, project_ref[...], preferred_element_type=f32)
    totals[1].start(two_sums(projected, projected * projected))
    totals[1].middle()
    last_gain, last_shift = misc_ref[17:18], misc_ref[18:19]
    proj_centered, proj_scale = centered_values(totals[1].finish(), projected)
    proj_normed = proj_centered * last_gain + last_shift
    feature_map = silu_value(proj_normed).astype(bf16)
    logits = jnp.dot(feature_map, heads_ref[...], preferred_element_type=f32) + bias_ref[0:1]
    lane = lax.broadcasted_iota(jnp.int32, (128, 128), 1)

    def per_pixel(labels_ref):
        spread = jnp.broadcast_to(labels_ref[...].astype(f32)[:, None, :], (8, 16, 16))
        here = lax.broadcasted_iota(jnp.int32, (8, 16, 16), 1) == lax.broadcasted_iota(
            jnp.int32, (8, 16, 16), 2
        )
        return jnp.sum(jnp.where(here, spread, 0.0), axis=2, keepdims=True).reshape(128, 1)

    lane_value = lane.astype(f32)
    hot = (
        jnp.where(lane_value == per_pixel(seg_ref), 1.0, 0.0)
        + jnp.where(lane == SEG, per_pixel(edge_ref), 0.0)
        + jnp.where(lane_value == per_pixel(part_ref) + (SEG + 1.0), 1.0, 0.0)
    )

    def cross_entropy(inside):
        highest = jnp.max(jnp.where(inside, logits, -3.0e38), axis=1, keepdims=True)
        powers = jnp.where(inside, jnp.exp(jnp.where(inside, logits - highest, 0.0)), 0.0)
        total = jnp.sum(powers, axis=1, keepdims=True)
        picked = jnp.sum(jnp.where(inside, logits * hot, 0.0), axis=1, keepdims=True)
        return highest + jnp.log(total) - picked, powers / total

    seg_inside, part_inside = lane < SEG, jnp.logical_and(lane > SEG, lane < HEADS)
    seg_terms, seg_soft = cross_entropy(seg_inside)
    part_terms, part_soft = cross_entropy(part_inside)
    edge_inside = lane == SEG
    edge_all = (
        jnp.maximum(logits, 0.0) + jnp.log1p(jnp.exp(-jnp.abs(logits))) - hot * logits
    )
    edge_soft = jax.nn.sigmoid(logits)
    weights = [weights_ref[task].astype(f32) for task in range(3)]
    weight_total = weights[0] + weights[1] + weights[2]
    row_lane = lax.broadcasted_iota(jnp.int32, (1, 128), 1)
    shares = jnp.where(
        row_lane < SEG, weights[0], jnp.where(row_lane == SEG, weights[1], weights[2])
    ) / jnp.full((1, 128), weight_total)
    shares = jnp.where(row_lane < HEADS, shares, 0.0)
    terms = jnp.where(lane == 0, seg_terms, 0.0) + jnp.where(edge_inside, edge_all, 0.0)
    terms = (terms + jnp.where(lane == SEG + 1, part_terms, 0.0)) * shares
    loss_local = jnp.sum(jnp.sum(terms, axis=0, keepdims=True), axis=1, keepdims=True) / 16384.0
    soft = seg_soft + part_soft + jnp.where(edge_inside, edge_soft, 0.0)
    logit_grad = ((soft - hot) * shares / 16384.0).astype(bf16)
    feature_back = against_rows(logit_grad, heads_ref[...]) * silu_grad(proj_normed)
    proj_sums = two_sums(feature_back, feature_back * proj_centered)
    totals[2].start(
        jnp.concatenate([proj_sums, jnp.broadcast_to(loss_local, (1, ASPP))], axis=0)
    )
    heads_out[0:256] = over_pixels(feature_map, logit_grad)
    heads_out[256:264] = jnp.broadcast_to(
        jnp.sum(logit_grad.astype(f32), axis=0, keepdims=True), (8, 128)
    )
    totals[2].middle()
    total = totals[2].finish()
    loss_out[...] = jnp.broadcast_to(total[2:3, 0:128], (8, 128))
    projected_grad = norm_grad(total, feature_back, proj_centered, proj_scale, last_gain)
    joined_grad = against_rows(projected_grad, project_ref[...])
    pool_map_grad = joined_grad[:, 4 * ASPP :]
    pool_local = jnp.concatenate(
        [jnp.sum(pool_map_grad * members[image], axis=0, keepdims=True) for image in range(4)], axis=0
    )
    branch_back = joined_grad[:, : 4 * ASPP] * silu_grad(normed)
    branch_sums = two_sums(branch_back, branch_back * centered)
    pool_row = jnp.concatenate([pool_local[image : image + 1] for image in range(4)], axis=1)
    totals[3].start(jnp.concatenate([branch_sums, pool_row], axis=0))
    project_out[...] = over_pixels(joined, projected_grad).astype(bf16)
    totals[3].middle()
    pool_slope = silu_grad(pool_pre)
    pool_pre_local = pool_local * pool_slope
    norms_out[0:1] = jnp.sum(pool_pre_local, axis=0, keepdims=True)
    for branch in range(4):
        lanes = slice(256 * branch, 256 * branch + 256)
        norms_out[1 + 2 * branch : 2 + 2 * branch] = branch_sums[1:2, lanes]
        norms_out[2 + 2 * branch : 3 + 2 * branch] = branch_sums[0:1, lanes]
    norms_out[9:10] = proj_sums[1:2]
    norms_out[10:11] = proj_sums[0:1]
    norms_out[11:16] = jnp.zeros((5, ASPP), f32)
    padding = jnp.zeros((4, ASPP), f32)
    pool_out[...] = over_pixels(
        pooled_low, jnp.concatenate([pool_pre_local, padding], axis=0).astype(bf16)
    ).astype(bf16)
    total = totals[3].finish()
    branch_grad = norm_grad(total, branch_back, centered, scale, gains)
    for branch in range(3):
        grads_own[branch] = branch_grad[:, 256 * branch + 256 : 256 * branch + 512].reshape(8, 16, 256)
        backward_shift.start(branch)

    def stack_high_copy(branch, sender):
        view = stack.at[branch, :, :, columns_of(sender)]
        return remote(
            view, view, links.sends.at[stack_high + branch], links.recvs.at[stack_high + branch], far_twin
        )

    def stack_core_copy(branch, place, sender_core):
        view = stack.at[branch, :, :, columns_of(2 * place + sender_core)]
        number = stack_core + 2 * branch + place
        return remote(view, view, links.sends.at[number], links.recvs.at[number], twin)

    pool_grad = jnp.concatenate(
        [total[2:3, 256 * image : 256 * image + 256] for image in range(4)], axis=0
    )
    pooled_grad = against_rows(
        jnp.concatenate([pool_grad * pool_slope, padding], axis=0).astype(bf16), pool_ref[...]
    )[0:4] / area
    for branch in range(3):
        backward_shift.finish(branch)
        for tap, direction in ((0, 1), (2, 0)):
            mask = across_lanes(pixel_mask(masks_ref[2 + 2 * branch + direction]), ASPP)
            shifted = grads_in[branch, direction].astype(f32).reshape(128, 256) * mask
            stack[branch, tap, :, columns_of(col)] = shifted.astype(bf16).reshape(8, 16, 256)
        stack[branch, 1, :, columns_of(col)] = grads_own[branch]
        stack_high_copy(branch, col).start()
    point_grad = branch_grad[:, 0:256]
    point_out[...] = over_pixels(grid, point_grad).astype(bf16)
    grad_out[...] = against_rows(point_grad, point_ref[...])
    for image in range(4):
        grad_out[...] = grad_out[...] + across_lanes(
            pixel_mask(members_low[image]), CIN
        ) * pooled_grad[image : image + 1]
    for branch in range(3):
        stack_high_copy(branch, col + 2 - 4 * high).wait_recv()
        for place in range(2):
            stack_core_copy(branch, place, core).start()
    slab_grad = None
    for branch, rate in enumerate(rate_list):
        for place in range(2):
            stack_core_copy(branch, place, 1 - core).wait_recv()
        for tap in range(3):
            padded[:, MARGIN : MARGIN + 64, 0:256] = stack[branch, tap].astype(f32)
            for col_tap in range(3):
                start = MARGIN - (col_tap - 1) * rate
                lanes = slice(256 * (3 * tap + col_tap), 256 * (3 * tap + col_tap) + 256)
                grad_taps[:, lanes] = (
                    padded[:, start : start + 64, 0:256].reshape(512, 256).astype(bf16)
                )
        rows = slice(2304 * branch, 2304 * branch + 2304)
        product = jnp.dot(grad_taps[...], kernels[rows], preferred_element_type=f32)
        slab_grad = product if slab_grad is None else slab_grad + product
        kernels[rows] = over_pixels(grad_taps[...], slab).astype(bf16)
    back_out[...] = slab_grad.astype(bf16).reshape(8, 64, 512)

    def back_copy(step, sender):
        return remote(
            back_out.at[:, columns_of(lax.rem(col + step, 4))],
            back_in.at[:, :, pl.ds(pl.multiple_of(sender * 512, 512), 512)],
            links.sends.at[back + step - 1],
            links.recvs.at[back + step - 1],
            device_of(row, lax.rem(col + step, 4)),
        )

    for step in (1, 2, 3):
        back_copy(step, col).start()
    back_in[:, :, pl.ds(pl.multiple_of(col * 512, 512), 512)] = back_out[:, columns_of(col)]

    def split(pair, carry):
        both = kernels[pl.ds(pl.multiple_of(432 * pair, 16), 432)].astype(f32)
        zeros = jnp.zeros((8, 512), f32)
        pieces_out[2 * pair] = jnp.concatenate([both[0:216], zeros], axis=0).astype(bf16)
        pieces_out[2 * pair + 1] = jnp.concatenate([both[216:432], zeros], axis=0).astype(bf16)
        return carry

    lax.fori_loop(0, 16, split, 0)
    for step in (1, 2, 3):
        copy = back_copy(step, lax.rem(col + 4 - step, 4))
        copy.wait_recv()
        copy.wait_send()
    grad_out[...] = grad_out[...] + back_in[...].reshape(128, CIN).astype(f32)
    for branch in range(3):
        for place in range(2):
            tap_core_copy(branch, place).wait_send()
            stack_core_copy(branch, place, core).wait_send()
        tap_high_copy(branch).wait_send()
        stack_high_copy(branch, col).wait_send()


def pyramid(arrays, collective):
    bf16, f32 = jnp.bfloat16, jnp.float32
    outs = [
        ((8, 128), f32),
        ((4, CIN), f32),
        ((128, CIN), f32),
        ((CIN, ASPP), bf16),
        ((CIN, ASPP), bf16),
        ((5 * ASPP, ASPP), bf16),
        ((264, 128), f32),
        ((16, ASPP), f32),
        ((32, RATE_ROWS, 512), bf16),
    ]
    scratch = [
        pltpu.VMEM((27 * ASPP, 512), bf16),
        pltpu.VMEM((8, 64 + 2 * MARGIN, 512), f32),
        pltpu.VMEM((6, 512, 512), bf16),
        pltpu.VMEM((9, 8, 64, ASPP), bf16),
        pltpu.VMEM((3, 2, 3, 8, 16, ASPP), bf16),
        pltpu.VMEM((3, 3, 8, 16, ASPP), bf16),
        pltpu.VMEM((3, 3, 8, 16, ASPP), bf16),
        pltpu.VMEM((3, 3, 8, 16, ASPP), f32),
        pltpu.VMEM((3, 2, 8, 16, ASPP), bf16),
        pltpu.VMEM((3, 2, 8, 16, ASPP), bf16),
        pltpu.VMEM((3, 8, 16, ASPP), bf16),
        pltpu.VMEM((3, 2, 8, 16, ASPP), bf16),
        pltpu.VMEM((3, 3, 8, 64, ASPP), bf16),
        pltpu.VMEM((512, 9 * ASPP), bf16),
        pltpu.VMEM((8, 64, 512), bf16),
        pltpu.VMEM((8, 16, CIN), bf16),
    ]
    for rows, columns in ((2, 4 * ASPP), (2, ASPP), (3, ASPP), (3, 4 * ASPP), (4, CIN + 128)):
        scratch += total_scratch(rows, columns)
    scratch += [pltpu.SemaphoreType.DMA((184,)), pltpu.SemaphoreType.DMA((184,))]
    in_specs = [VMEM] * len(arrays)
    in_specs[2] = ANY
    in_specs[-1] = SMEM
    return pl.pallas_call(
        pyramid_kernel,
        out_shape=[jax.ShapeDtypeStruct(shape, dtype) for shape, dtype in outs],
        in_specs=in_specs,
        out_specs=[VMEM] * len(outs),
        scratch_shapes=scratch,
        compiler_params=pltpu.CompilerParams(
            collective_id=collective, has_side_effects=True, vmem_limit_bytes=62 * MEGABYTE
        ),
    )(*arrays)


def per_device(
    features,
    image_rows,
    seg_labels,
    edge_labels,
    part_labels,
    task_weights,
    block_params,
    block_moment,
    head_params,
    head_moment,
    rate_params,
    rate_moment,
):
    height, across, channels = features.shape
    pixels = height * across
    inputs = features.reshape(pixels, channels)
    (
        w_reduce,
        w_spatial,
        w_expand,
        w_point,
        w_pool,
        w_project,
        misc,
        norms,
        masks,
        first_kept,
        second_kept,
        third_kept,
        second_act,
        block_window,
        grid,
        slab_map,
        rates_all,
    ) = block_forward(
        (
            inputs,
            block_params.reshape(BLOCK_ROWS, 128),
            head_params.reshape(HEAD_ROWS, 128),
            image_rows,
            rate_params.T,
        ),
        1,
    )
    w_heads = jnp.pad(
        misc[19:36].reshape(ASPP, HEADS).astype(jnp.bfloat16), ((0, 0), (0, 128 - HEADS))
    )
    heads_bias = jnp.broadcast_to(misc[36:37, :128], (8, 128))
    heads_bias = heads_bias * (jnp.arange(128) < HEADS).astype(jnp.float32)
    (
        loss_rows,
        pooled,
        out_grad,
        grad_point,
        grad_pool,
        grad_project,
        grad_heads,
        norm_grads,
        rate_pieces,
    ) = pyramid(
        (
            grid,
            slab_map,
            rates_all.reshape(32, RATE_ROWS, channels // 4),
            w_point,
            w_pool,
            w_project,
            misc,
            w_heads,
            heads_bias,
            masks,
            seg_labels,
            edge_labels,
            part_labels,
            task_weights,
        ),
        2,
    )
    loss_total = loss_rows[0, 0]
    heads_flat = jnp.concatenate([grad_heads[:ASPP, :HEADS].reshape(-1), grad_heads[ASPP, :HEADS]])
    heads_flat = jnp.pad(heads_flat, (0, 53 * ASPP - heads_flat.shape[0])).reshape(53, ASPP)
    misc_grads = jnp.concatenate(
        [norm_grads[:11], heads_flat], axis=0
    )
    input_grad, packed, rate_sum = block_backward(
        (
            inputs,
            out_grad,
            norms,
            masks,
            first_kept,
            second_kept,
            third_kept,
            second_act,
            block_window,
            w_reduce,
            w_spatial,
            w_expand,
            grad_point,
            grad_pool,
            grad_project,
            misc_grads,
            rate_pieces.reshape(2, 4, 4, RATE_ROWS, channels // 4),
        ),
        16,
    )
    rate_share = rate_sum[: rate_params.shape[1]].T
    shares_all = scatter_params(packed, 20)
    block_share = shares_all[:BLOCK_ROWS].reshape(-1)
    head_share = shares_all[BLOCK_ROWS : BLOCK_ROWS + HEAD_ROWS].reshape(-1)
    block_moment_next = MOMENTUM_KEEP * block_moment + block_share
    head_moment_next = MOMENTUM_KEEP * head_moment + head_share
    rate_moment_next = MOMENTUM_KEEP * rate_moment + rate_share
    return (
        loss_total,
        pooled,
        input_grad.reshape(height, across, channels),
        block_moment_next,
        head_moment_next,
        rate_moment_next,
    )


def solution(mesh):
    return jax.shard_map(
        per_device,
        mesh=mesh,
        in_specs=(
            P("rows", "cols", None),
            P("rows"),
            P("rows", "cols"),
            P("rows", "cols"),
            P("rows", "cols"),
            P(),
            P(("rows", "cols")),
            P(("rows", "cols")),
            P(("rows", "cols")),
            P(("rows", "cols")),
            P("cols", "rows"),
            P("cols", "rows"),
        ),
        out_specs=(
            P(),
            P(),
            P("rows", "cols", None),
            P(("rows", "cols")),
            P(("rows", "cols")),
            P("cols", "rows"),
        ),
        check_vma=False,
    )
```

time: 2310 us -> 387 us (0.17)
  the two profiles are of different devices: /device:TPU:0 before, /device:TPU:6 now
where the time goes in v2:
time: 387 us; the launch traced here: 380 us
  Pallas kernels  366 us (95%)
  local copies, waits for them, and re-layouts  6.83 us (2%)
  other arithmetic  5.9 us (2%)
    pallas_call x1, Pallas kernels, block_forward(): pl.pallas_call(block_forward_kernel, out_shape=[jax.ShapeDtypeStruct(shap...  120 us
    pallas_call x1, Pallas kernels, pyramid(): pl.pallas_call(pyramid_kernel, out_shape=[jax.ShapeDtypeStruct(shape, dty...  113 us
    pallas_call x1, Pallas kernels, block_backward(): pl.pallas_call(block_backward_kernel, out_shape=[jax.ShapeDtypeStruct(sha...  92.3 us
    pallas_call x1, Pallas kernels, scatter_params(): pl.pallas_call(scatter_kernel, out_shape=jax.ShapeDtypeStruct((PAYLOAD, 1...  40.3 us

profile of v2, /device:TPU:6, one launch (start us, length us, event | category | flops | bytes accessed | tf_op | source)
XLA Modules:
  0.0 380.1 jit_solution(8512672915224547841)
XLA Ops:
  0.6 120.2 %shard_map.163 = (bf16[2048,512]{1,0:T(8,128)(2,1)}, bf16[4608,512]{1,0:T(8,128)(2,1)}, bf16[512,2048]{1,0:T(8,128)(2,1)}, bf16[2048,256]{1,0:T(8,128)(2,1)}, bf...) custom-call(bf16[128,2048]{1,0:T(8,128)(2,1)} %bitcast.21, ...), custom_call_target="tpu_custom_call" | custom-call | tf_op jit(solution)/shard_map/pallas_call | solution.py:832
  120.8 0.7 compare_select_fusion
  121.5 0.6 broadcast_in_dim.9.bias_ref
  122.1 0.8 slice.44
  122.9 0.2 convert_element_type.13
  123.1 0.6 pad.8.heads_ref
  123.7 113.4 %shard_map.164 = (f32[8,128]{1,0:T(8,128)}, f32[4,2048]{1,0:T(4,128)}, f32[128,2048]{1,0:T(8,128)}, bf16[2048,256]{1,0:T(8,128)(2,1)}, bf16[2048,256]{1,0:T(8,12...) custom-call(bf16[8,16,2048]{2,1,0:T(8,128)(2,1)} %get-tuple-element., ...), custom_call_target="tpu_custom_call" | custom-call | tf_op jit(solution)/shard_map/pallas_call | solution.py:1784
  237.1 1.2 slice.30
  238.3 0.7 slice_bitcast_fusion
  239.0 0.9 slice.32
  239.9 0.2 reshape.53
  240.2 1.4 pad_maximum_fusion.misc_ref
  241.5 92.3 %shard_map.165 = (f32[128,2048]{1,0:T(8,128)}, bf16[2,4,4,2,384,128]{5,4,3,2,1,0:T(8,128)(2,1)}, f32[224,512]{1,0:T(8,128)}) custom-call(bf16[128,2048]{1,0:T(8,128)(2,1)} %bitcast.22, f32[128,2048]{1,0:T(8,128)} %get-tuple-element.45.grad_ref, f32[16,512]{1,0:T(8,128)} %get-tuple-element.46.norms_ref, f32[9,8,128]{2,1,0:T(8,128)} %get-tuple-element.42.masks_ref, ...), custom_call_target="tpu_custom_call" | custom-call | tf_op jit(solution)/shard_map/pallas_call | solution.py:1280
  333.9 0.0 copy-start.4
  333.9 0.0 copy-start.3
  333.9 0.0 copy-start.1
  333.9 0.0 copy-start.2
  333.9 0.0 copy-start.5
  333.9 0.0 copy-start
  333.9 40.3 %shard_map.166 = f32[384,128]{1,0:T(8,128)} custom-call(bf16[2,4,4,2,384,128]{5,4,3,2,1,0:T(8,128)(2,1)} %get-tuple-element.62.p_ref), custom_call_target="tpu_custom_call" | custom-call | tf_op jit(solution)/shard_map/pallas_call | solution.py:205
  374.2 0.0 copy-done.4
  374.2 1.4 bitcast_add_fusion.2
  375.7 0.0 copy-done.3
  375.7 1.6 bitcast_add_fusion.1
  377.2 0.0 copy-done.1
  377.2 0.0 copy-done.2
  377.2 0.8 bitcast_add_fusion
  378.1 0.0 copy-done.5
  378.1 0.6 copy.20
  378.7 0.0 copy-done
  378.7 1.0 copy.21
  (2 shorter events, 0.0 us)
Async XLA Ops:
  333.9 40.4 %copy-start.4 = (f32[10880]{0:T(1024)S(1)}, f32[10880]{0:T(1024)}, u32[]{:S(2)}) copy-start(f32[10880]{0:T(1024)} %param.21) | copy-start | bytes 130564
  333.9 41.8 %copy-start.3 = (f32[34944]{0:T(1024)S(1)}, f32[34944]{0:T(1024)}, u32[]{:S(2)}) copy-start(f32[34944]{0:T(1024)} %param.19) | copy-start | bytes 419332
  333.9 43.4 %copy-start.1 = (f32[512,216]{0,1:T(8,128)S(1)}, f32[512,216]{0,1:T(8,128)}, u32[]{:S(2)}) copy-start(f32[512,216]{0,1:T(8,128)} %param.23) | copy-start | bytes 1327108
  333.9 43.3 %copy-start.2 = (f32[224,512]{1,0:T(8,128)S(1)}, f32[224,512]{1,0:T(8,128)}, u32[]{:S(2)}) copy-start(f32[224,512]{1,0:T(8,128)} %get-tuple-element.63) | copy-start | bytes 1376260
  333.9 44.2 %copy-start.5 = (f32[4,2048]{1,0:T(4,128)S(1)}, f32[4,2048]{1,0:T(4,128)}, u32[]{:S(2)}) copy-start(f32[4,2048]{1,0:T(4,128)} %get-tuple-element.71) | copy-start | bytes 98308
  333.9 44.8 %copy-start = (f32[128,2048]{1,0:T(8,128)S(1)}, f32[128,2048]{1,0:T(8,128)}, u32[]{:S(2)}) copy-start(f32[128,2048]{1,0:T(8,128)} %get-tuple-element.61) | copy-start | bytes 3145732

commit v3 on v2

--- a/solution.py
+++ b/solution.py
@@ -88,13 +88,14 @@
     return tuple(index)
 
 
-def scatter_kernel(p_ref, o_ref, held, *rest):
+def scatter_kernel(p_ref, late_ref, pair_ref, o_ref, share_ref, held, rate_parts, rate_sums, rate_pair, *rest):
     relays = rest[0:3]
     parts = [rest[3 + 3 * third : 6 + 3 * third] for third in range(3)]
     sums = [rest[12 + 2 * third : 14 + 2 * third] for third in range(3)]
     links = Links(rest[-2], rest[-1])
     first, own_first = links.take(45), links.take(3)
-    me = split_place()
+    rates = RateScatter(links, late_ref, rate_parts)
+    me = rates.me
     everywhere = (slice(None),) * 4
     own_copies = []
     for third in range(3):
@@ -109,6 +110,7 @@
         own_copies[third].start()
     partners = [moved(me, axis, step) for axis in "xyz" for step in (1, 2, 3)]
     meet([device_at(place) for place in partners], 9)
+    rates.send()
 
     def view_of(third, phase, place, part=None):
         order = GATHER_ORDERS[third]
@@ -163,6 +165,10 @@
             view = view_of(third, 0, moved(me, axis, step), step // 2)
             view[...] = view[...] + relays[third][step // 2]
             copy(third, 0, step).start()
+    rate_sums[0] = pair_ref[...]
+    rates.collect(rate_sums.at[1])
+    rate_exchange = rates.pair(rate_sums.at[1 - rates.low_y], rate_pair)
+    rate_exchange.start()
     for phase in range(1, 4):
         for third in range(3):
             total = view_of(third, phase - 1, me)[...].astype(jnp.float32)
@@ -175,6 +181,12 @@
                 sums[third][phase - 1][...] = total.astype(jnp.bfloat16)
                 for step in steps(phase):
                     copy(third, phase, step).start()
+    rate_exchange.wait()
+    for half in range(2):
+        rows = slice(half * (RATE_ROWS // 2), (half + 1) * (RATE_ROWS // 2))
+        share_ref[rows] = rate_sums[rates.low_y, half].astype(jnp.float32) + rate_pair[half].astype(
+            jnp.float32
+        )
     for third in range(3):
         for step in (1, 3):
             relay(third, step).wait_send()
@@ -183,7 +195,7 @@
                 copy(third, phase, step).wait_send()
 
 
-def scatter_params(packed, collective):
+def scatter_params(arrays, collective):
     def shape_left(left, rows):
         shape = ()
         for name, number in (("y", 2), ("x", 4), ("z", 4), ("y", 2)):
@@ -201,21 +213,27 @@
             parts.append(pltpu.VMEM((number,) + shape_left(order[: 2 - phase], 128), jnp.bfloat16))
         for phase in range(2):
             sums.append(pltpu.VMEM(shape_left(order[: 2 - phase], 128), jnp.bfloat16))
-    half = (2, 4, 4, 2, PAYLOAD, 128)
+    held = pltpu.VMEM((2, 4, 4, 2, PAYLOAD, 128), jnp.bfloat16)
+    half = (2, RATE_ROWS // 2, 512)
+    rates = [pltpu.VMEM(shape, jnp.bfloat16) for shape in ((2, 3) + half[1:], (2,) + half, half)]
     return pl.pallas_call(
         scatter_kernel,
-        out_shape=jax.ShapeDtypeStruct((PAYLOAD, 128), jnp.float32),
-        in_specs=[ANY],
-        out_specs=VMEM,
-        scratch_shapes=[pltpu.VMEM(half, jnp.bfloat16)]
+        out_shape=[
+            jax.ShapeDtypeStruct((PAYLOAD, 128), jnp.float32),
+            jax.ShapeDtypeStruct((RATE_ROWS, 512), jnp.float32),
+        ],
+        in_specs=[ANY, VMEM, VMEM],
+        out_specs=[VMEM, VMEM],
+        scratch_shapes=[held]
+        + rates
         + relays
         + parts
         + sums
-        + [pltpu.SemaphoreType.DMA((51,)), pltpu.SemaphoreType.DMA((51,))],
+        + [pltpu.SemaphoreType.DMA((64,)), pltpu.SemaphoreType.DMA((64,))],
         compiler_params=pltpu.CompilerParams(
             collective_id=collective, has_side_effects=True, vmem_limit_bytes=56 * MEGABYTE
         ),
-    )(packed)
+    )(*arrays)
 
 
 def neighbour(row, col, offset):
@@ -430,7 +448,7 @@
     def steps(self, phase):
         return (1, 3) if phase == 2 else (1, 2, 3)
 
-    def run(self):
+    def run(self, early, late):
         me = self.me
         for phase in range(3):
             for third in range(3):
@@ -443,6 +461,8 @@
                     self.block(me, third, ())[...] = self.source[pl.ds(third * 128, 128)]
                 if phase == 2:
                     self.core_copy(third, 0, me).start()
+            if phase == 0:
+                early()
         for third in range(3):
             for step in (1, 3):
                 self.copy(third, 2, step, self.behind(third, 2, step)).wait_recv()
@@ -452,6 +472,7 @@
             for step in (1, 3):
                 self.relay(third, 2, step, self.behind(third, 2, step)).wait_recv()
             self.core_copy(third, 2, me).start()
+        late()
         for third in range(3):
             for distance in range(4):
                 self.core_copy(third, distance, self.twin).wait_recv()
@@ -600,12 +621,12 @@
     head_ref,
     image_ref,
     rate_params_ref,
-    reduce_ref,
-    spatial_ref,
-    expand_ref,
-    point_ref,
-    pool_ref,
-    project_ref,
+    reduce_hbm,
+    spatial_hbm,
+    expand_hbm,
+    point_hbm,
+    pool_hbm,
+    project_hbm,
     misc_ref,
     norms_ref,
     masks_ref,
@@ -634,6 +655,12 @@
     payload_wide,
     payload_ref,
     rate_ref,
+    reduce_ref,
+    spatial_ref,
+    expand_ref,
+    point_ref,
+    pool_ref,
+    project_ref,
     *rest,
 ):
     staging, matrix, head = (s0, s1, s2, s3), (w0, w1, w2, w3), (h0, h1)
@@ -656,12 +683,33 @@
     rates = RateGather(links, rate_ref, rates_ref)
     halo = Halo(links, act_map, window_ref)
     slab_first = links.take(3)
+    out_first = links.take(6)
+    stores = [
+        pltpu.make_async_copy(source, target, links.sends.at[out_first + number])
+        for number, (source, target) in enumerate(
+            (
+                (reduce_ref, reduce_hbm),
+                (spatial_ref, spatial_hbm),
+                (expand_ref, expand_hbm),
+                (point_ref, point_hbm),
+                (pool_ref, pool_hbm),
+                (project_ref, project_hbm),
+            )
+        )
+    ]
     row, col = lax.axis_index("rows"), lax.axis_index("cols")
     peers = total_peers() + halo_peers()
     meet(peers, len(peers))
-    rates.begin()
-    gather.run()
-    rates.send(0, 2, 1)
+
+    def rates_early():
+        rates.begin()
+        rates.send(0)
+
+    def rates_late():
+        rates.forward(0)
+        rates.send(2, 1)
+
+    gather.run(rates_early, rates_late)
 
     for step in range(-3, 4):
         other = lax.rem(row + step + 32, 32)
@@ -699,6 +747,8 @@
             [array[pl.ds(2288 + part, 512, stride=4), :] for array in matrix], axis=1
         ).astype(jnp.bfloat16)
     norms_ref[...] = wide_rows(matrix, 4336, 16)
+    for store in stores[0:3]:
+        store.start()
 
     def normal(total, values, gain, shift, kept):
         average = total[0:1] / 16384.0
@@ -720,9 +770,9 @@
     normed = normal(totals[0].finish(), first, norms_ref[0:1], norms_ref[1:2], first_ref)
     act_map[...] = silu(normed).astype(jnp.bfloat16).reshape(8, 16, MID)
     halo.start()
-    rates.forward(0, 2, 1)
+    rates.forward(2, 1)
     rates.receive(0)
-    rates.send(3)
+    rates.send(3, 4)
     halo.finish()
     widen_window(window_ref, wide)
     second = None
@@ -751,12 +801,14 @@
         project_ref[256 * step : 256 * step + 256] = wide_rows(head, 4097 + 256 * step, 256).astype(
             jnp.bfloat16
         )
+    for store in stores[3:6]:
+        store.start()
     misc_ref[0:8] = wide_rows(head, 4096, 8)
     misc_ref[8:72] = wide_rows(head, 5376, 64)
     normed = normal(totals[1].finish(), second, norms_ref[2:3], norms_ref[3:4], second_ref)
-    rates.forward(3)
+    rates.forward(3, 4)
     rates.receive(1)
-    rates.send(4, 5)
+    rates.send(5, 6)
     act_ref[...] = silu(normed).astype(jnp.bfloat16)
     third = jnp.dot(act_ref[...], expand_ref[...], preferred_element_type=jnp.float32)
     totals[2].start(stats(third))
@@ -778,8 +830,8 @@
 
     for step in (1, 2, 3):
         slab_copy(step, col).start()
-    rates.forward(4, 5)
-    rates.send(6, 7, 8, 9)
+    rates.forward(5, 6)
+    rates.send(7, 8, 9)
     slab_ref[:, pl.ds(pl.multiple_of(col * 16, 16), 16)] = out_ref[
         :, :, pl.ds(pl.multiple_of(col * 512, 512), 512)
     ]
@@ -787,10 +839,12 @@
         copy = slab_copy(step, lax.rem(col + 4 - step, 4))
         copy.wait_recv()
         copy.wait_send()
-    rates.forward(6, 7, 8, 9)
+    rates.forward(7, 8, 9)
     rates.receive(2, 3, 4, 5, 6, 7, 8, 9)
     rates.close()
     gather.close()
+    for store in stores:
+        store.wait()
 
 
 def block_forward(arrays, collective):
@@ -826,14 +880,15 @@
         pltpu.VMEM((PAYLOAD, 128), bf16),
         pltpu.VMEM((RATE_ROWS, 512), bf16),
     ]
+    scratch += [pltpu.VMEM(shape, dtype) for shape, dtype in outs[:6]]
     for rows, columns in ((2, MID), (2, MID), (2, CIN)):
         scratch += total_scratch(rows, columns)
-    scratch += [pltpu.SemaphoreType.DMA((240,)), pltpu.SemaphoreType.DMA((240,))]
+    scratch += [pltpu.SemaphoreType.DMA((248,)), pltpu.SemaphoreType.DMA((248,))]
     return pl.pallas_call(
         block_forward_kernel,
         out_shape=[jax.ShapeDtypeStruct(shape, dtype) for shape, dtype in outs],
         in_specs=[VMEM, VMEM, VMEM, SMEM, VMEM],
-        out_specs=[VMEM] * 16 + [ANY],
+        out_specs=[ANY] * 6 + [VMEM] * 10 + [ANY],
         scratch_shapes=scratch,
         compiler_params=pltpu.CompilerParams(
             collective_id=collective, has_side_effects=True, vmem_limit_bytes=60 * MEGABYTE
@@ -844,8 +899,8 @@
 class RatePieces:
     def __init__(self, links, units):
         self.links = links
-        self.first = links.take(6 * units + 4)
-        self.extra = self.first + 6 * units
+        self.first = links.take(8 * units + 4)
+        self.extra = self.first + 8 * units
         self.me = split_place()
         self.low_y = lax.rem(self.me["y"], 2)
         self.other = dict(self.me)
@@ -858,8 +913,8 @@
         places = {RATE_ORDERS[half][0]: first_axis, RATE_ORDERS[half][1]: second_axis}
         return array.at[low_y, places["x"], places["z"], self.rows(half)]
 
-    def remote(self, unit, half, step, outgoing, incoming, axis):
-        number = self.first + 6 * unit + 3 * half + step - 1
+    def remote(self, unit, half, slot, outgoing, incoming, axis, step):
+        number = self.first + 8 * unit + 4 * half + slot
         return remote(
             outgoing,
             incoming,
@@ -873,80 +928,110 @@
 
 
 class RateFirst(RatePieces):
-    def __init__(self, links, pieces, parts, sums, low_y):
+    def __init__(self, links, pieces, own, relays, parts, low_y):
         super().__init__(links, 4)
-        self.pieces, self.parts, self.sums, self.from_y = pieces, parts, sums, low_y
+        self.pieces, self.own, self.relays, self.parts, self.from_y = pieces, own, relays, parts, low_y
+        loads = links.take(6)
+        self.loads = []
+        for half in range(2):
+            near, far = RATE_ORDERS[half]
+            for slot, step in enumerate((0, 1, 3)):
+                places = {near: slice(None), far: moved(self.me, far, step)[far]}
+                self.loads.append(
+                    pltpu.make_async_copy(
+                        pieces.at[low_y, places["x"], places["z"], self.rows(half)],
+                        own.at[half, slot],
+                        links.recvs.at[loads + 3 * half + slot],
+                    )
+                )
+
+    def part(self, step):
+        return pl.ds(0, 64) if step == 1 else pl.ds(64, 48)
+
+    def relay(self, unit, half, step):
+        far = RATE_ORDERS[half][1]
+        places = {RATE_ORDERS[half][0]: unit, far: moved(self.me, far, 2)[far]}
+        rows = self.part(step)
+        start = half * (RATE_ROWS // 2) + rows.start
+        return self.remote(
+            unit,
+            half,
+            step // 2 + 2,
+            self.pieces.at[self.from_y, places["x"], places["z"], pl.ds(start, rows.size)],
+            self.relays.at[half, unit, rows],
+            far,
+            step,
+        )
 
     def copy(self, unit, half, step):
         far = RATE_ORDERS[half][1]
-        target = moved(self.me, far, step)
-        outgoing = self.piece(self.pieces, half, self.from_y, unit, target[far])
-        return self.remote(unit, half, step, outgoing, self.parts.at[half, unit, step - 1], far)
-
-    def send(self, unit):
-        for half, step in self.each():
-            self.copy(unit, half, step).start()
-
-    def collect(self, unit, own=None):
-        for half in range(2):
-            total = None
-            if own is None:
-                mine = self.piece(self.pieces, half, self.from_y, unit, self.me[RATE_ORDERS[half][1]])[...]
-            else:
-                mine = own[half, unit]
-            total = mine.astype(jnp.float32)
-            for step in (1, 2, 3):
-                self.copy(unit, half, step).wait_recv()
-                total = total + self.parts[half, unit, step - 1].astype(jnp.float32)
-            self.sums[half, unit] = total.astype(jnp.bfloat16)
-        for half, step in self.each():
-            self.copy(unit, half, step).wait_send()
+        slot = step // 2
+        return self.remote(
+            unit, half, slot, self.own.at[half, 1 + slot, unit], self.parts.at[half, unit, slot], far, step
+        )
+
+    def each(self):
+        return [(half, step) for half in range(2) for step in (1, 3)]
+
+    def send(self, *units):
+        for unit in units:
+            for half, step in self.each():
+                self.relay(unit, half, step).start()
+
+    def forward(self, *units):
+        for unit in units:
+            for half, step in self.each():
+                self.relay(unit, half, step).wait_recv()
+                rows = self.part(step)
+                place = (half, 1 + step // 2, unit, rows)
+                self.own[place] = self.own[place] + self.relays[half, unit, rows]
+                self.copy(unit, half, step).start()
+
+    def collect(self, *units):
+        for unit in units:
+            for half in range(2):
+                total = self.own[half, 0, unit].astype(jnp.float32)
+                for step in (1, 3):
+                    self.copy(unit, half, step).wait_recv()
+                    total = total + self.parts[half, unit, step // 2].astype(jnp.float32)
+                self.own[half, 0, unit] = total.astype(jnp.bfloat16)
+            for half, step in self.each():
+                self.relay(unit, half, step).wait_send()
+                self.copy(unit, half, step).wait_send()
 
 
 class RateScatter(RatePieces):
-    def __init__(self, links, sums, parts, pair_sums, pair_parts, target):
-        super().__init__(links, 2)
-        self.sums, self.parts, self.target = sums, parts, target
-        self.pair_sums, self.pair_parts = pair_sums, pair_parts
-
-    def copy(self, low_y, half, step):
+    def __init__(self, links, sums, parts):
+        super().__init__(links, 1)
+        self.sums, self.parts = sums, parts
+
+    def copy(self, half, step):
         near = RATE_ORDERS[half][0]
-        target = moved(self.me, near, step)
-        outgoing = self.sums[low_y].at[half, target[near]]
-        return self.remote(low_y, half, step, outgoing, self.parts.at[half, low_y, step - 1], near)
-
-    def pair(self):
+        outgoing = self.sums.at[half, moved(self.me, near, step)[near]]
+        return self.remote(0, half, step - 1, outgoing, self.parts.at[half, step - 1], near, step)
+
+    def pair(self, outgoing, incoming):
         return remote(
-            self.pair_sums.at[1 - self.low_y],
-            self.pair_parts,
+            outgoing,
+            incoming,
             self.links.sends.at[self.extra],
             self.links.recvs.at[self.extra],
             device_at(self.other),
         )
 
-    def send(self, low_y):
+    def send(self):
         for half, step in self.each():
-            self.copy(low_y, half, step).start()
-
-    def collect(self, low_y):
+            self.copy(half, step).start()
+
+    def collect(self, target):
         for half in range(2):
-            total = self.sums[low_y][half, self.me[RATE_ORDERS[half][0]]].astype(jnp.float32)
+            total = self.sums[half, self.me[RATE_ORDERS[half][0]]].astype(jnp.float32)
             for step in (1, 2, 3):
-                self.copy(low_y, half, step).wait_recv()
-                total = total + self.parts[half, low_y, step - 1].astype(jnp.float32)
-            self.pair_sums[low_y, half] = total.astype(jnp.bfloat16)
-
-    def finish(self):
-        self.pair().wait_recv()
-        for half in range(2):
-            rows = slice(half * (RATE_ROWS // 2), (half + 1) * (RATE_ROWS // 2))
-            self.target[rows] = self.pair_sums[self.low_y, half].astype(jnp.float32) + self.pair_parts[
-                half
-            ].astype(jnp.float32)
-        for low_y in range(2):
-            for half, step in self.each():
-                self.copy(low_y, half, step).wait_send()
-        self.pair().wait_send()
+                self.copy(half, step).wait_recv()
+                total = total + self.parts[half, step - 1].astype(jnp.float32)
+            target[half] = total.astype(jnp.bfloat16)
+        for half, step in self.each():
+            self.copy(half, step).wait_send()
 
 
 def disassemble(packed, first_row_group, staging, wide, stride):
@@ -1017,7 +1102,8 @@
     pieces_ref,
     out_ref,
     held_ref,
-    share_ref,
+    late_ref,
+    pair_ref,
     s0,
     s1,
     s2,
@@ -1040,41 +1126,23 @@
     staging, matrix, head = (s0, s1, s2, s3), (w0, w1, w2, w3), (w0, w1)
     links = Links(rest[-2], rest[-1])
     totals = [Total(links, *rest[3 * number : 3 * number + 3]) for number in range(3)]
-    own, first_parts, first_sums_here, second_parts, pair_sums, pair_parts = rest[9:15]
+    own, relays, first_parts, second_parts = rest[9:13]
     rates = [
-        RateFirst(links, pieces_ref, first_parts.at[low_y], first_sums_here.at[low_y], low_y)
+        RateFirst(links, pieces_ref, own.at[low_y], relays.at[low_y], first_parts.at[low_y], low_y)
         for low_y in range(2)
     ]
-    scatter = RateScatter(
-        links,
-        (first_sums_here.at[0], first_sums_here.at[1]),
-        second_parts,
-        pair_sums,
-        pair_parts,
-        share_ref,
-    )
+    scatter = RateScatter(links, own.at[0, :, 0], second_parts)
     me = scatter.me
     twin = device_at(moved(me, "core", 1, 2))
     halo = Halo(links, act_map, window)
-    load_first, own_first, twin_first, out_first = (links.take(number) for number in (3, 4, 2, 2))
+    load_first, twin_first, out_first = (links.take(number) for number in (3, 2, 2))
     loads = [
         pltpu.make_async_copy(source, target, links.recvs.at[load_first + number])
         for number, (source, target) in enumerate(
             ((expand_hbm, expand_ref), (spatial_hbm, spatial_ref), (reduce_hbm, reduce_ref))
         )
     ]
-    own_copies = []
-    for low_y in range(2):
-        for half in range(2):
-            places = {RATE_ORDERS[half][0]: slice(None), RATE_ORDERS[half][1]: me[RATE_ORDERS[half][1]]}
-            own_copies.append(
-                pltpu.make_async_copy(
-                    pieces_ref.at[low_y, places["x"], places["z"], scatter.rows(half)],
-                    own.at[low_y, half],
-                    links.recvs.at[own_first + 2 * low_y + half],
-                )
-            )
-    for copy in loads + own_copies:
+    for copy in loads + rates[0].loads + rates[1].loads:
         copy.start()
 
     def twin_copy(low_y):
@@ -1125,7 +1193,7 @@
             * (grad - total[0:1] / 16384.0 - kept[0:128] * (total[1:2] / 16384.0))
         ).astype(jnp.bfloat16)
 
-    rates[0].send(0)
+    rates[0].send(0, 1, 2, 3)
     out_gain = jnp.concatenate([norms_ref[4 + part : 5 + part] for part in range(4)], axis=1)
     out_shift = jnp.concatenate([norms_ref[8 + part : 9 + part] for part in range(4)], axis=1)
     residual = third_ref[0:128] * out_gain + out_shift + x_ref[...].astype(jnp.float32)
@@ -1145,7 +1213,9 @@
     deal(head, 2657, misc_ref[1:64])
     disassemble(packed, 16, staging, head, 0)
     third_grad = through_norm(totals[0].finish(), out_ref[...], third_ref, out_gain)
-    rates[0].send(1)
+    for copy in rates[0].loads + rates[1].loads:
+        copy.wait()
+    rates[0].forward(0, 1)
     loads[0].wait()
     second_gain, second_shift = norms_ref[2:3], norms_ref[3:4]
     second_norm = second_ref[0:128] * second_gain + second_shift
@@ -1161,8 +1231,8 @@
     second_grad = through_norm(totals[1].finish(), second_back, second_ref, second_gain)
     act_map[...] = second_grad.reshape(8, 16, MID)
     halo.start()
-    rates[0].send(2)
-    rates[0].send(3)
+    rates[0].forward(2, 3)
+    rates[1].send(0, 1, 2, 3)
 
     def spatial_grad(tap):
         row_tap, col_tap = tap // 3, tap % 3
@@ -1176,6 +1246,8 @@
     for tap in range(5, 9):
         deal(matrix, 240 + 512 * (tap - 5), spatial_grad(tap))
     halo.finish()
+    rates[0].collect(0, 1, 2, 3)
+    scatter.send()
     widen_window(window, wide)
     loads[1].wait()
     first_back = None
@@ -1209,18 +1281,11 @@
     twin_copy(1).start()
     totals[2].middle()
     widen_window(window_ref, wide)
-    for copy in own_copies:
-        copy.wait()
-    for unit in range(3):
-        rates[0].collect(unit, own.at[0])
     deal(matrix, 4096, middle_tap[0:272])
     for tap in range(4):
         deal(matrix, 2048 + 512 * tap, spatial_grad(tap))
     first_total = totals[2].finish()
-    for unit in range(4):
-        rates[1].send(unit)
-    rates[0].collect(3, own.at[0])
-    scatter.send(0)
+    rates[1].forward(0, 1, 2, 3)
     join_twin(1)
     pl.semaphore_signal(free_sem, inc=1, device_id=twin, device_id_type=MESH)
     loads[2].wait()
@@ -1232,14 +1297,10 @@
     disassemble(packed, 0, staging, matrix, 0)
     pl.semaphore_wait(free_sem, 1)
     twin_copy(0).start()
-    for unit in range(4):
-        rates[1].collect(unit, own.at[1])
-    scatter.send(1)
-    scatter.collect(0)
+    rates[1].collect(0, 1, 2, 3)
+    late_ref[...] = own[1, :, 0]
+    scatter.collect(pair_ref)
     join_twin(0)
-    scatter.collect(1)
-    scatter.pair().start()
-    scatter.finish()
     for low_y in range(2):
         twin_copy(low_y).wait_send()
         out_copy(low_y).wait()
@@ -1264,24 +1325,23 @@
     for rows, columns in ((2, CIN), (2, MID), (2, MID)):
         scratch += total_scratch(rows, columns)
     scratch += [
+        pltpu.VMEM((2, 2, 3, 4, half, 512), bf16),
         pltpu.VMEM((2, 2, 4, half, 512), bf16),
-        pltpu.VMEM((2, 2, 4, 3, half, 512), bf16),
-        pltpu.VMEM((2, 2, 4, half, 512), bf16),
-        pltpu.VMEM((2, 2, 3, half, 512), bf16),
-        pltpu.VMEM((2, 2, half, 512), bf16),
-        pltpu.VMEM((2, half, 512), bf16),
+        pltpu.VMEM((2, 2, 4, 2, half, 512), bf16),
+        pltpu.VMEM((2, 3, half, 512), bf16),
     ]
-    scratch += [pltpu.SemaphoreType.DMA((176,)), pltpu.SemaphoreType.DMA((176,))]
+    scratch += [pltpu.SemaphoreType.DMA((232,)), pltpu.SemaphoreType.DMA((232,))]
     outs = [
         ((128, CIN), f32),
         ((2, 4, 4, 2, PAYLOAD, 128), bf16),
-        ((RATE_ROWS, 512), f32),
+        ((2, 4, half, 512), bf16),
+        ((2, half, 512), bf16),
     ]
     return pl.pallas_call(
         block_backward_kernel,
         out_shape=[jax.ShapeDtypeStruct(shape, dtype) for shape, dtype in outs],
         in_specs=[VMEM] * 9 + [ANY] * 3 + [VMEM] * (len(arrays) - 13) + [ANY],
-        out_specs=[VMEM, ANY, VMEM],
+        out_specs=[VMEM, ANY, VMEM, VMEM],
         scratch_shapes=scratch,
         compiler_params=pltpu.CompilerParams(
             collective_id=collective, has_side_effects=True, vmem_limit_bytes=62 * MEGABYTE
@@ -1375,12 +1435,10 @@
     grid_ref,
     slab_ref,
     pieces_ref,
-    point_ref,
-    pool_ref,
-    project_ref,
+    point_hbm,
+    pool_hbm,
+    project_hbm,
     misc_ref,
-    heads_ref,
-    bias_ref,
     masks_ref,
     seg_ref,
     edge_ref,
@@ -1392,9 +1450,8 @@
     point_out,
     pool_out,
     project_out,
-    heads_out,
     norms_out,
-    pieces_out,
+    pieces_hbm,
     kernels,
     padded,
     moved_maps,
@@ -1411,6 +1468,11 @@
     grad_taps,
     back_out,
     back_in,
+    pieces_out,
+    point_ref,
+    pool_ref,
+    project_ref,
+    heads_ref,
     *rest,
 ):
     bf16, f32 = jnp.bfloat16, jnp.float32
@@ -1420,7 +1482,7 @@
     core, high = lax.rem(col, 2), col // 2
     twin = device_of(row, col + 1 - 2 * core)
     far_twin = device_of(row, col + 2 - 4 * high)
-    pieces_sem = links.take(1)
+    pieces_sem = links.take(4)
     tap_core, tap_high = links.take(6), links.take(3)
     stack_high, stack_core = links.take(3), links.take(6)
     back = links.take(3)
@@ -1430,8 +1492,27 @@
     backward_shift = RowShift(
         links, [[grads_own.at[branch] for _ in range(2)] for branch in range(3)], grads_in
     )
-    load = pltpu.make_async_copy(pieces_ref, pieces_out, links.recvs.at[pieces_sem])
-    load.start()
+    loads = [
+        pltpu.make_async_copy(source, target, links.recvs.at[pieces_sem + number])
+        for number, (source, target) in enumerate(
+            (
+                (pieces_ref, pieces_out),
+                (point_hbm, point_ref),
+                (pool_hbm, pool_ref),
+                (project_hbm, project_ref),
+            )
+        )
+    ]
+    stores = [
+        pltpu.make_async_copy(
+            pieces_out.at[pl.ds(16 * part, 16)],
+            pieces_hbm.at[pl.ds(16 * part, 16)],
+            links.sends.at[pieces_sem + part],
+        )
+        for part in range(2)
+    ]
+    for load in loads:
+        load.start()
     peers = total_peers() + row_peers()
     meet(peers, len(peers))
 
@@ -1464,7 +1545,8 @@
                 padded[:, start : start + 64].reshape(512, 512).astype(bf16)
             )
     slab = slab_ref[...].reshape(512, 512)
-    load.wait()
+    for load in loads:
+        load.wait()
 
     def join(pair, carry):
         both = jnp.concatenate(
@@ -1533,6 +1615,28 @@
     tap_meet(2)
     grid = grid_ref[...].reshape(128, CIN)
     branches = [jnp.dot(grid, point_ref[...], preferred_element_type=f32)]
+    number = lax.broadcasted_iota(jnp.int32, (256, 256), 0) * HEADS
+    lane_256 = lax.broadcasted_iota(jnp.int32, (256, 256), 1)
+    number_32 = lax.broadcasted_iota(jnp.int32, (256, 32), 0) * HEADS
+    lane_32 = lax.broadcasted_iota(jnp.int32, (256, 32), 1)
+    lane_128 = lax.broadcasted_iota(jnp.int32, (256, 128), 1)
+
+    def rows_of_head(head):
+        return jnp.where(lane_32 == (number_32 + head) // 256, 1.0, 0.0).astype(bf16)
+
+    def lanes_of_head(head):
+        return lane_256 == lax.rem(number + head, 256)
+
+    flat_heads = misc_ref[19:51].astype(bf16)
+    heads = jnp.zeros((256, 128), f32)
+    for head in range(HEADS):
+        spread = jnp.dot(rows_of_head(head), flat_heads, preferred_element_type=f32)
+        column = jnp.sum(jnp.where(lanes_of_head(head), spread, 0.0), axis=1, keepdims=True)
+        heads = heads + jnp.where(lane_128 == head, column, 0.0)
+    heads_ref[...] = heads.astype(bf16)
+    bias = jnp.where(
+        lax.broadcasted_iota(jnp.int32, (1, 128), 1) < HEADS, misc_ref[36:37, 0:128], 0.0
+    )
     pooled_sums = totals[4].finish()
     area = jnp.concatenate([pooled_sums[:, CIN : CIN + 128]] * 16, axis=1) * 16.0
     pooled = pooled_sums[:, 0:CIN] / area
@@ -1568,7 +1672,7 @@
     proj_centered, proj_scale = centered_values(totals[1].finish(), projected)
     proj_normed = proj_centered * last_gain + last_shift
     feature_map = silu_value(proj_normed).astype(bf16)
-    logits = jnp.dot(feature_map, heads_ref[...], preferred_element_type=f32) + bias_ref[0:1]
+    logits = jnp.dot(feature_map, heads_ref[...], preferred_element_type=f32) + bias
     lane = lax.broadcasted_iota(jnp.int32, (128, 128), 1)
 
     def per_pixel(labels_ref):
@@ -1617,13 +1721,19 @@
     totals[2].start(
         jnp.concatenate([proj_sums, jnp.broadcast_to(loss_local, (1, ASPP))], axis=0)
     )
-    heads_out[0:256] = over_pixels(feature_map, logit_grad)
-    heads_out[256:264] = jnp.broadcast_to(
-        jnp.sum(logit_grad.astype(f32), axis=0, keepdims=True), (8, 128)
-    )
+    heads_grad = over_pixels(feature_map, logit_grad)
+    norms_out[11:64] = jnp.zeros((53, ASPP), f32)
+    flat_grad = None
+    for head in range(HEADS):
+        column = jnp.broadcast_to(heads_grad[:, head : head + 1], (256, 256))
+        spread = jnp.where(lanes_of_head(head), column, 0.0).astype(bf16)
+        part = over_pixels(rows_of_head(head), spread)
+        flat_grad = part if flat_grad is None else flat_grad + part
+    norms_out[11:28] = flat_grad[0:17]
+    norms_out[28:29, 0:128] = jnp.sum(logit_grad.astype(f32), axis=0, keepdims=True)
     totals[2].middle()
     total = totals[2].finish()
-    loss_out[...] = jnp.broadcast_to(total[2:3, 0:128], (8, 128))
+    loss_out[...] = total[2:3, 0:1]
     projected_grad = norm_grad(total, feature_back, proj_centered, proj_scale, last_gain)
     joined_grad = against_rows(projected_grad, project_ref[...])
     pool_map_grad = joined_grad[:, 4 * ASPP :]
@@ -1645,7 +1755,6 @@
         norms_out[2 + 2 * branch : 3 + 2 * branch] = branch_sums[0:1, lanes]
     norms_out[9:10] = proj_sums[1:2]
     norms_out[10:11] = proj_sums[0:1]
-    norms_out[11:16] = jnp.zeros((5, ASPP), f32)
     padding = jnp.zeros((4, ASPP), f32)
     pool_out[...] = over_pixels(
         pooled_low, jnp.concatenate([pool_pre_local, padding], axis=0).astype(bf16)
@@ -1692,6 +1801,13 @@
         stack_high_copy(branch, col + 2 - 4 * high).wait_recv()
         for place in range(2):
             stack_core_copy(branch, place, core).start()
+    def split(pair, carry):
+        both = kernels[pl.ds(pl.multiple_of(432 * pair, 16), 432)].astype(f32)
+        zeros = jnp.zeros((8, 512), f32)
+        pieces_out[2 * pair] = jnp.concatenate([both[0:216], zeros], axis=0).astype(bf16)
+        pieces_out[2 * pair + 1] = jnp.concatenate([both[216:432], zeros], axis=0).astype(bf16)
+        return carry
+
     slab_grad = None
     for branch, rate in enumerate(rate_list):
         for place in range(2):
@@ -1708,6 +1824,9 @@
         product = jnp.dot(grad_taps[...], kernels[rows], preferred_element_type=f32)
         slab_grad = product if slab_grad is None else slab_grad + product
         kernels[rows] = over_pixels(grad_taps[...], slab).astype(bf16)
+        if branch == 1:
+            lax.fori_loop(0, 8, split, 0)
+            stores[0].start()
     back_out[...] = slab_grad.astype(bf16).reshape(8, 64, 512)
 
     def back_copy(step, sender):
@@ -1723,14 +1842,8 @@
         back_copy(step, col).start()
     back_in[:, :, pl.ds(pl.multiple_of(col * 512, 512), 512)] = back_out[:, columns_of(col)]
 
-    def split(pair, carry):
-        both = kernels[pl.ds(pl.multiple_of(432 * pair, 16), 432)].astype(f32)
-        zeros = jnp.zeros((8, 512), f32)
-        pieces_out[2 * pair] = jnp.concatenate([both[0:216], zeros], axis=0).astype(bf16)
-        pieces_out[2 * pair + 1] = jnp.concatenate([both[216:432], zeros], axis=0).astype(bf16)
-        return carry
-
-    lax.fori_loop(0, 16, split, 0)
+    lax.fori_loop(8, 16, split, 0)
+    stores[1].start()
     for step in (1, 2, 3):
         copy = back_copy(step, lax.rem(col + 4 - step, 4))
         copy.wait_recv()
@@ -1742,19 +1855,20 @@
             stack_core_copy(branch, place, core).wait_send()
         tap_high_copy(branch).wait_send()
         stack_high_copy(branch, col).wait_send()
+    for store in stores:
+        store.wait()
 
 
 def pyramid(arrays, collective):
     bf16, f32 = jnp.bfloat16, jnp.float32
     outs = [
-        ((8, 128), f32),
+        ((1, 1), f32),
         ((4, CIN), f32),
         ((128, CIN), f32),
         ((CIN, ASPP), bf16),
         ((CIN, ASPP), bf16),
         ((5 * ASPP, ASPP), bf16),
-        ((264, 128), f32),
-        ((16, ASPP), f32),
+        ((64, ASPP), f32),
         ((32, RATE_ROWS, 512), bf16),
     ]
     scratch = [
@@ -1774,18 +1888,23 @@
         pltpu.VMEM((512, 9 * ASPP), bf16),
         pltpu.VMEM((8, 64, 512), bf16),
         pltpu.VMEM((8, 16, CIN), bf16),
+        pltpu.VMEM((32, RATE_ROWS, 512), bf16),
+        pltpu.VMEM((CIN, ASPP), bf16),
+        pltpu.VMEM((CIN, ASPP), bf16),
+        pltpu.VMEM((5 * ASPP, ASPP), bf16),
+        pltpu.VMEM((ASPP, 128), bf16),
     ]
     for rows, columns in ((2, 4 * ASPP), (2, ASPP), (3, ASPP), (3, 4 * ASPP), (4, CIN + 128)):
         scratch += total_scratch(rows, columns)
     scratch += [pltpu.SemaphoreType.DMA((184,)), pltpu.SemaphoreType.DMA((184,))]
     in_specs = [VMEM] * len(arrays)
-    in_specs[2] = ANY
+    in_specs[2:6] = [ANY] * 4
     in_specs[-1] = SMEM
     return pl.pallas_call(
         pyramid_kernel,
         out_shape=[jax.ShapeDtypeStruct(shape, dtype) for shape, dtype in outs],
         in_specs=in_specs,
-        out_specs=[VMEM] * len(outs),
+        out_specs=[VMEM] * (len(outs) - 1) + [ANY],
         scratch_shapes=scratch,
         compiler_params=pltpu.CompilerParams(
             collective_id=collective, has_side_effects=True, vmem_limit_bytes=62 * MEGABYTE
@@ -1838,11 +1957,6 @@
         ),
         1,
     )
-    w_heads = jnp.pad(
-        misc[19:36].reshape(ASPP, HEADS).astype(jnp.bfloat16), ((0, 0), (0, 128 - HEADS))
-    )
-    heads_bias = jnp.broadcast_to(misc[36:37, :128], (8, 128))
-    heads_bias = heads_bias * (jnp.arange(128) < HEADS).astype(jnp.float32)
     (
         loss_rows,
         pooled,
@@ -1850,8 +1964,7 @@
         grad_point,
         grad_pool,
         grad_project,
-        grad_heads,
-        norm_grads,
+        misc_grads,
         rate_pieces,
     ) = pyramid(
         (
@@ -1862,8 +1975,6 @@
             w_pool,
             w_project,
             misc,
-            w_heads,
-            heads_bias,
             masks,
             seg_labels,
             edge_labels,
@@ -1872,13 +1983,8 @@
         ),
         2,
     )
-    loss_total = loss_rows[0, 0]
-    heads_flat = jnp.concatenate([grad_heads[:ASPP, :HEADS].reshape(-1), grad_heads[ASPP, :HEADS]])
-    heads_flat = jnp.pad(heads_flat, (0, 53 * ASPP - heads_flat.shape[0])).reshape(53, ASPP)
-    misc_grads = jnp.concatenate(
-        [norm_grads[:11], heads_flat], axis=0
-    )
-    input_grad, packed, rate_sum = block_backward(
+    loss_total = loss_rows.reshape(())
+    input_grad, *flat_sums = block_backward(
         (
             inputs,
             out_grad,
@@ -1900,8 +2006,8 @@
         ),
         16,
     )
+    shares_all, rate_sum = scatter_params(flat_sums, 20)
     rate_share = rate_sum[: rate_params.shape[1]].T
-    shares_all = scatter_params(packed, 20)
     block_share = shares_all[:BLOCK_ROWS].reshape(-1)
     head_share = shares_all[BLOCK_ROWS : BLOCK_ROWS + HEAD_ROWS].reshape(-1)
     block_moment_next = MOMENTUM_KEEP * block_moment + block_share

time: 387 us -> 357 us (0.922)
  the two profiles are of different devices: /device:TPU:6 before, /device:TPU:0 now
where the time goes in v3:
time: 357 us; the launch traced here: 350 us
  Pallas kernels  341 us (96%)
  other arithmetic  4.85 us (1%)
    pallas_call x1, Pallas kernels, block_forward(): pl.pallas_call(block_forward_kernel, out_shape=[jax.ShapeDtypeStruct(shap...  114 us
    pallas_call x1, Pallas kernels, pyramid(): pl.pallas_call(pyramid_kernel, out_shape=[jax.ShapeDtypeStruct(shape, dty...  111 us
    pallas_call x1, Pallas kernels, block_backward(): pl.pallas_call(block_backward_kernel, out_shape=[jax.ShapeDtypeStruct(sha...  73.2 us
    pallas_call x1, Pallas kernels, scatter_params(): pl.pallas_call(scatter_kernel, out_shape=[jax.ShapeDtypeStruct((PAYLOAD,...  43.4 us

profile of v3, /device:TPU:0, one launch (start us, length us, event | category | flops | bytes accessed | tf_op | source)
XLA Modules:
  0.0 350.1 jit_solution(15838831181248270562)
XLA Ops:
  0.6 113.5 %shard_map.163 = (bf16[2048,512]{1,0:T(8,128)(2,1)}, bf16[4608,512]{1,0:T(8,128)(2,1)}, bf16[512,2048]{1,0:T(8,128)(2,1)}, bf16[2048,256]{1,0:T(8,128)(2,1)}, bf...) custom-call(bf16[128,2048]{1,0:T(8,128)(2,1)} %bitcast.16, ...), custom_call_target="tpu_custom_call" | custom-call | tf_op jit(solution)/shard_map/pallas_call | solution.py:887
  114.1 110.6 %shard_map.164 = (f32[1,1]{1,0:T(1,128)}, f32[4,2048]{1,0:T(4,128)}, f32[128,2048]{1,0:T(8,128)}, bf16[2048,256]{1,0:T(8,128)(2,1)}, bf16[2048,256]{1,0:T(8,128)...) custom-call(bf16[8,16,2048]{2,1,0:T(8,128)(2,1)} %get-tuple-element.37.grid_ref, ...), custom_call_target="tpu_custom_call" | custom-call | tf_op jit(solution)/shard_map/pallas_call | solution.py:1903
  224.8 73.2 %shard_map.165 = (f32[128,2048]{1,0:T(8,128)}, bf16[2,4,4,2,384,128]{5,4,3,2,1,0:T(8,128)(2,1)}, bf16[2,4,112,512]{3,2,1,0:T(8,128)(2,1)}, bf16[2,112,512]{2,1,0:T(8,128)(2,1)}) custom-call(bf16[128,2048]{1,0:T(8,128)(2,1)} %bitcast.17, f32[128,2048]{1,0:T(8,128)} %get-tuple-element.47.grad_ref, f32[16,512]{1,0:T(8,128)} %get-tuple-element.48.norms_ref, ...), custom_call_target="tpu_custom_call" | custom-call | tf_op jit(solution)/shard_map/pallas_call | solution.py:1340
  298.0 0.0 copy-start.1
  298.0 0.0 copy-start.3
  298.0 0.0 copy-start.2
  298.0 0.0 copy-start.4
  298.0 0.0 copy-start
  298.0 43.4 %shard_map.166 = (f32[384,128]{1,0:T(8,128)}, f32[224,512]{1,0:T(8,128)}) custom-call(bf16[2,4,4,2,384,128]{5,4,3,2,1,0:T(8,128)(2,1)} %get-tuple-element.63.p_ref, bf16[2,4,112,512]{3,2,1,0:T(8,128)(2,1)} %get-tuple-element.64.late_ref, bf16[2,112,512]{2,1,0:T(8,128)(2,1)} %get-tuple-element.65.pair_ref), custom_call_target="tpu_custom_call" | custom-call | tf_op jit(solution)/shard_map/pallas_call | solution.py:219
  341.4 0.0 copy-done.1
  341.4 1.8 bitcast_add_fusion
  343.3 0.0 copy-done.3
  343.3 1.4 bitcast_add_fusion.2
  344.7 0.0 copy-done.2
  344.7 1.6 bitcast_add_fusion.1
  346.9 0.0 copy-done.4
  346.9 0.6 copy.22
  347.5 0.0 copy-done
  347.5 1.0 copy.23
Async XLA Ops:
  298.0 43.5 %copy-start.1 = (f32[512,216]{0,1:T(8,128)S(1)}, f32[512,216]{0,1:T(8,128)}, u32[]{:S(2)}) copy-start(f32[512,216]{0,1:T(8,128)} %param.23) | copy-start | bytes 1327108
  298.0 45.3 %copy-start.3 = (f32[10880]{0:T(1024)S(1)}, f32[10880]{0:T(1024)}, u32[]{:S(2)}) copy-start(f32[10880]{0:T(1024)} %param.21) | copy-start | bytes 130564
  298.0 46.7 %copy-start.2 = (f32[34944]{0:T(1024)S(1)}, f32[34944]{0:T(1024)}, u32[]{:S(2)}) copy-start(f32[34944]{0:T(1024)} %param.19) | copy-start | bytes 419332
  298.0 48.9 %copy-start.4 = (f32[4,2048]{1,0:T(4,128)S(1)}, f32[4,2048]{1,0:T(4,128)}, u32[]{:S(2)}) copy-start(f32[4,2048]{1,0:T(4,128)} %get-tuple-element.75) | copy-start | bytes 98308
  298.0 49.5 %copy-start = (f32[128,2048]{1,0:T(8,128)S(1)}, f32[128,2048]{1,0:T(8,128)}, u32[]{:S(2)}) copy-start(f32[128,2048]{1,0:T(8,128)} %get-tuple-element.62) | copy-start | bytes 3145732
